TPU v7x, 128 devices: a whole 4x4x4 slice. The times are simulated.
128 devices in a mesh: row: 8 (over y, core), col: 16 (over z, x).
Axes of the slice: x: 4, y: 4, z: 4, core: 2. Of those that a mesh axis runs over, the one named last changes fastest.
Arguments:
- integrals: bfloat16 [8, 16, 32, 512, 512], P('row', 'col'), may hold values from -0.046875 to 0.046875
- tile_count: int32 [8, 16], P('row', 'col'), may hold values from 1 to 32, as said below
- tile_list: int32 [8, 16, 32], P('row', 'col'), may hold values from 0 to 31, as said below
- amplitudes: bfloat16 [64, 512, 1024], P('col', 'row'), may hold values from -6 to 6
- pair_energy: float32 [32768], P(('row', 'col')), may hold values from 1 to 4
- occ_energy: float32 [32], replicated, may hold values from -1.5 to -0.25
- partner: int32 [32768], P(('row', 'col')), may hold values from 0 to 32767, as said below
Outputs:
- amp_update: float32 [32768, 1024], P(('row', 'col'))
Inputs may be any that keep to these rules, and one draw needn't show every extreme that they name: `tile_count`: some grid cell holds exactly 32 live tiles. `tile_list`: each grid cell's list is a permutation of 0 to 31; only its first tile_count entries name live tiles. partner is an involution. Numbering the rows in consecutive blocks of 256, the rows of one block have their partners among the 16 blocks of the same aligned group of 4096 rows, exactly 16 of them in each of these blocks.
All inputs are finite; a program needn't handle non-finite values.
Results may differ from a plain program's by a relative error of at most 0.0003.
Values may be sent and summed in bfloat16 or wider, within the bound.
No kernel may reach another device: no remote copies, remote signals or barrier semaphores. Data moves between devices by JAX's collectives and lax.ppermute only.
A program may use at most 128 MiB of HBM per device.

v0:
```python
import jax
import jax.numpy as jnp
from jax import lax
from jax.sharding import PartitionSpec as P

slot_batch = 4


def add_tiles(partial_value, tile_data, blocks, last_slot, amp_blocks):
    nblock_col = amp_blocks.shape[0]
    slot_total = tile_data.shape[0]
    turn_count = (last_slot + slot_batch - 1) // slot_batch

    def one_turn(turn_no, running):
        slot_index = turn_no * slot_batch + jnp.arange(slot_batch, dtype=jnp.int32)
        is_live = slot_index < last_slot
        clipped = jnp.clip(slot_index, 0, slot_total - 1)
        chosen = jnp.take(tile_data, clipped, axis=0)
        position = jnp.take(blocks, clipped, axis=0)
        block_row = position // nblock_col
        block_col = position % nblock_col
        operand = jnp.take(amp_blocks, block_col, axis=0)
        product = jnp.einsum("uab,ubo->uao", chosen, operand, preferred_element_type=jnp.float32)
        product = product * is_live.astype(jnp.float32)[:, None, None]
        for member in range(slot_batch):
            current = lax.dynamic_index_in_dim(running, block_row[member], 0, keepdims=False)
            running = lax.dynamic_update_index_in_dim(
                running, current + product[member], block_row[member], 0
            )
        return running

    return lax.fori_loop(0, turn_count, one_turn, partial_value)


def swap_occupied(rows, occ_count):
    shaped = rows.reshape(rows.shape[0], occ_count, occ_count)
    return jnp.swapaxes(shaped, 1, 2).reshape(rows.shape)


def body(integrals, tile_count, tile_list, amplitudes, pair_energy, occ_energy, partner):
    tile_data = integrals[0, 0]
    blocks = tile_list[0, 0]
    own_count = tile_count[0, 0]
    slots = blocks.shape[0]
    gathered = lax.all_gather(amplitudes, "row", axis=1, tiled=True)
    nblock_col, tile_width, occ_pairs = gathered.shape
    nblock_row = slots // nblock_col
    partial_value = jnp.zeros((nblock_row, tile_width, occ_pairs), jnp.float32)
    partial_value = add_tiles(partial_value, tile_data, blocks, own_count, gathered)
    flat_rows = partial_value.reshape(nblock_row * tile_width, occ_pairs)
    occ_count = occ_energy.shape[0]
    col_count = lax.axis_size("col")
    rows_total = flat_rows.shape[0]
    own_rows = rows_total // col_count
    peer_rows = own_rows // col_count
    summed = lax.psum_scatter(flat_rows, "col", scatter_dimension=0, tiled=True)
    target = partner // own_rows % col_count
    key_local = partner % own_rows
    same_target = target[:, None] == target[None, :]
    send_rank = jnp.sum(same_target & (key_local[None, :] < key_local[:, None]), axis=1)
    row_ids = jnp.arange(own_rows, dtype=jnp.int32)
    recv_rank = jnp.sum(same_target & (row_ids[None, :] < row_ids[:, None]), axis=1)
    source = jnp.zeros((own_rows,), jnp.int32).at[target * peer_rows + send_rank].set(row_ids)
    outgoing = jnp.take(summed, source, axis=0)
    incoming = lax.all_to_all(outgoing, "col", split_axis=0, concat_axis=0, tiled=True)
    fetched = jnp.take(incoming, target * peer_rows + recv_rank, axis=0)
    symmetric = summed + swap_occupied(fetched, occ_count)
    denominator = pair_energy[:, None] - (occ_energy[:, None] + occ_energy[None, :]).reshape(
        1, occ_pairs
    )
    return symmetric / denominator


def solution(mesh):
    return jax.shard_map(
        body,
        mesh=mesh,
        in_specs=(
            P("row", "col", None, None, None),
            P("row", "col"),
            P("row", "col", None),
            P("col", "row", None),
            P(("row", "col")),
            P(),
            P(("row", "col")),
        ),
        out_specs=P(("row", "col"), None),
        check_vma=False,
    )
```

profile of v0, /device:TPU:0, one launch (start us, length us, event | category | flops | bytes accessed | tf_op | source)
XLA Modules:
  0.0 559.9 jit_solution(17950218124753343609)
XLA Ops:
  6.5 0.0 all-gather.2.cloned.1.call-start
  6.5 0.7 all-gather.2.cloned.1.call-update
  7.3 0.0 reduce-scatter.2.cloned.1.call-start
  8.0 35.7 %all-gather.2.cloned.1.call-done = bf16[4,512,1024]{2,1,0:T(8,128)(2,1)} async-done(((bf16[4,64,1024]{2,1,0:T(8,128)(2,1)}), bf16[4,512,1024]{2,1,0:T(8,128)(2,1)}) %all-gather.2.cloned.1.call-update) | async-done | bytes 4194320 | tf_op jit(solution)/shard_map/all_gather | solution.py:45
  43.7 7.9 %broadcast_in_dim.64 = f32[8,512,1024]{2,1,0:T(8,128)} broadcast(f32[]{:T(128)} %constant.192.clone.1), dimensions={} | broadcast | bytes 16777220 | tf_op jit(solution)/shard_map/broadcast_in_dim | solution.py:48
  51.6 0.0 copy-done
  51.6 90.0 %while.12 = (s32[]{:T(128)}, f32[8,512,1024]{2,1,0:T(8,128)}, s32[]{:T(128)}, s32[32]{0:T(128)S(1)}, bf16[32,512,512]{2,1,0:T(8,128)(2,1)}, /*index=5*/bf16[4,51...) while((s32[]{:T(128)}, f32[8,512,1024]{2,1,0:T(8,128)}, ...), condition=%wide.region_1.2_spmd, body=%wide.region_0.1_spmd.sunk | while | flops 2154825984 | bytes 52437604 | solution.py:32
  51.6 0.6 gather_fusion
  52.3 4.9 gather_fusion.1
  57.2 6.4 %gather_fusion.2 = bf16[4,512,512]{2,1,0:T(8,128)(2,1)S(1)} fusion(bf16[32,512,512]{2,1,0:T(8,128)(2,1)} %get-tuple-element.213, s32[1024]{0:T(1024)S(1)} %pad_clamp_fusion.6), kind=kCustom, calls=%fused_computation.1.clone.1 | custom fusion | bytes 4194320 | tf_op jit(solution)/shard_map/while/body/jit(_take)/gather | solution.py:18
  63.7 0.7 compare_convert_fusion.2
  64.3 7.9 %broadcast_multiply_fusion.2 = f32[4,512,1024]{2,1,0:T(8,128)} fusion(f32[4]{0:T(128)S(1)} %compare_convert_fusion.2, bf16[4,512,1024]{2,1,0:T(8,128)(2,1)} %gather_fusion.1, pred[4]{0:T(512)(128)(4,1)S(1)} %get-tuple-element.182, bf16[4,512,512]{2,1,0:T(8,128)(2,1)S(1)} %gather_fusion.2, pred[4]{0:T(512)(128)(4,1)S(1)} %get-tuple-element.183), kind=kOutput, calls=%fused_computation.6.clone.1 | convolution fusion | flops 2152726528 | bytes 14680088 | tf_op jit(solution)/shard_map/while/body/uab,ubo->uao/dot_general | solution.py:23
  72.2 0.6 fusion.33
  74.7 4.1 fusion.35
  80.8 4.1 fusion.36
  86.5 4.1 fusion.37
  92.5 4.1 fusion.38
  96.6 0.6 gather_fusion
  97.3 4.9 gather_fusion.1
  102.2 6.4 %gather_fusion.2 = bf16[4,512,512]{2,1,0:T(8,128)(2,1)S(1)} fusion(bf16[32,512,512]{2,1,0:T(8,128)(2,1)} %get-tuple-element.213, s32[1024]{0:T(1024)S(1)} %pad_clamp_fusion.6), kind=kCustom, calls=%fused_computation.1.clone.1 | custom fusion | bytes 4194320 | tf_op jit(solution)/shard_map/while/body/jit(_take)/gather | solution.py:18
  108.7 0.7 compare_convert_fusion.2
  109.4 7.9 %broadcast_multiply_fusion.2 = f32[4,512,1024]{2,1,0:T(8,128)} fusion(f32[4]{0:T(128)S(1)} %compare_convert_fusion.2, bf16[4,512,1024]{2,1,0:T(8,128)(2,1)} %gather_fusion.1, pred[4]{0:T(512)(128)(4,1)S(1)} %get-tuple-element.182, bf16[4,512,512]{2,1,0:T(8,128)(2,1)S(1)} %gather_fusion.2, pred[4]{0:T(512)(128)(4,1)S(1)} %get-tuple-element.183), kind=kOutput, calls=%fused_computation.6.clone.1 | convolution fusion | flops 2152726528 | bytes 14680088 | tf_op jit(solution)/shard_map/while/body/uab,ubo->uao/dot_general | solution.py:23
  117.2 0.6 fusion.33
  119.8 4.1 fusion.35
  125.8 4.1 fusion.36
  131.5 4.1 fusion.37
  137.5 4.1 fusion.38
  141.6 0.0 reduce-scatter.2.cloned.1.call-update
  141.6 0.7 copy-done.4
  142.3 0.3 convert_reduce_fusion
  142.6 1.4 scatter_custom_fusion
  144.0 378.6 %reduce-scatter.2.cloned.1.call-done = f32[256,1024]{1,0:T(8,128)} async-done(((f32[4096,1024]{1,0:T(8,128)}), f32[256,1024]{1,0:T(8,128)}) %reduce-scatter.2.cloned.1.call-update) | async-done | bytes 1048592 | tf_op jit(solution)/shard_map/reduce_scatter | solution.py:56
  522.6 2.8 gather_fusion.3
  525.4 0.0 copy-start.2
  525.4 1.1 broadcast_select_fusion.2
  526.5 5.0 all-to-all-start
  531.6 0.0 copy-done.2
  531.6 0.1 broadcast_add_fusion
  531.6 0.1 add.253
  531.7 17.5 %all-to-all-done = f32[16,16,1024]{2,1,0:T(8,128)S(1)} async-done(((f32[16,16,1024]{2,1,0:T(8,128)}), f32[16,16,1024]{2,1,0:T(8,128)S(1)}, u32[]{:S(2)}, u32[]{:S(2)}) %all-to-all-start) | async-done | bytes 1048608 | tf_op jit(solution)/shard_map/all_to_all | solution.py:65
  549.3 1.1 gather_fusion.4
  550.4 0.0 copy-start.1
  550.4 0.0 copy-start.3
  550.4 0.1 broadcast_select_fusion.1
  550.5 0.3 copy.12
  550.9 0.6 copy.13
  551.5 0.3 copy.14
  551.8 1.2 subtract_divide_fusion
  (24 shorter events, 0.2 us)
Async XLA Ops:
  6.5 37.1 %all-gather.2.cloned.1.call-start = ((), (), s32[]{:S(2)}) async-start(), calls=%async_computation.2 | async-start | bytes 4718592 | tf_op jit(solution)/shard_map/all_gather | solution.py:45
  7.3 515.3 %reduce-scatter.2.cloned.1.call-start = ((), (), s32[]{:S(2)}) async-start(), calls=%async_computation.3 | async-start | bytes 17825792 | tf_op jit(solution)/shard_map/reduce_scatter | solution.py:56
  43.7 7.9 %copy-start = (s32[1,1,32]{2,1,0:T(1,128)S(1)}, s32[1,1,32]{2,1,0:T(1,128)}, u32[]{:S(2)}) copy-start(s32[1,1,32]{2,1,0:T(1,128)} %param.13) | copy-start | bytes 388
  141.6 0.7 copy-start.4
  525.4 6.2 %copy-start.2 = (f32[32]{0:T(128)S(1)}, f32[32]{0:T(128)}, u32[]{:S(2)}) copy-start(f32[32]{0:T(128)} %param.16) | copy-start | bytes 388
  526.5 22.8 %all-to-all-start = ((f32[16,16,1024]{2,1,0:T(8,128)}), f32[16,16,1024]{2,1,0:T(8,128)S(1)}, u32[]{:S(2)}, u32[]{:S(2)}) async-start(f32[16,16,1024]{2,1,0:T(8,128)} %bitcast.11), calls=%async_computation.1 | async-start | bytes 2097152 | tf_op jit(solution)/shard_map/all_to_all | solution.py:65
  550.4 1.5 copy-start.1
  550.4 1.5 copy-start.3
Sparse Core Ops, SparseCore 0:
  9.0 34.5 all-gather.1
  141.8 380.7 reduce-scatter.1
where the time goes:
time: 562 us; the launch traced here: 560 us
  waiting for transfers between devices  433 us (77%)
  local copies, waits for them, and re-layouts  40.4 us (7%)
  other arithmetic  37.2 us (7%)
  matrix products  15.7 us (3%)
  loops' own time  14.7 us (3%)
  between operations  14.2 us (3%)
    reduce_scatter x1, waiting for transfers between devices, body(): summed = lax.psum_scatter(flat_rows, 'col', scatter_dimension=0, tiled=True)  379 us
    all_gather x1, waiting for transfers between devices, body(): gathered = lax.all_gather(amplitudes, 'row', axis=1, tiled=True)  35.7 us
    dynamic_update_slice x8, other arithmetic, one_turn(): lax.dynamic_update_index_in_dim(running, current + product[member], block...  32.9 us
    all_to_all x1, waiting for transfers between devices, body(): lax.all_to_all(outgoing, 'col', split_axis=0, concat_axis=0, tiled=True)  17.5 us
    dot_general x2, matrix products, one_turn(): jnp.einsum('uab,ubo->uao', chosen, operand, preferred_element_type=jnp.fl...  15.7 us
    another operation x1, loops' own time, add_tiles(): return lax.fori_loop(0, turn_count, one_turn, partial_value)  14.7 us
    gather x2, local copies, waits for them, and re-layouts, one_turn(): chosen = jnp.take(tile_data, clipped, axis=0)  12.9 us
  transfers between devices with their start and end apart: 3, of which 3 were waited for; matrix products, arithmetic and copies ran while one was open for 0% of the time, Pallas kernels for 0%

commit v1 on v0

v1 whole, which is shorter than its diff:
```python
import functools

import numpy as np
import jax
import jax.numpy as jnp
from jax import lax
from jax.experimental import pallas as pl
from jax.experimental.pallas import tpu as pltpu
from jax.sharding import PartitionSpec as P

F32, S32, S16, BF16 = jnp.float32, jnp.int32, jnp.int16, jnp.bfloat16
NO = 32
OCC = NO * NO
HALF = OCC // 2
CHUNKS = 2
CW = OCC // CHUNKS
LANES = 128
SIDE = 4
PAD = 16
LOG_GRID = 200.0
FULL = 32760.0
TINY = 1e-37
VMEM = 56 * 1024 * 1024


def pair_orders():
    first, mates = [], []
    for gap in range(1, NO // 2):
        for i in range(NO):
            j = (i + gap) % NO
            first.append(i * NO + j)
            mates.append(j * NO + i)
    first += [i * NO + i for i in range(NO)]
    mates += [i * NO + i + NO // 2 for i in range(NO // 2)]
    mates += [(i + NO // 2) * NO + i for i in range(NO // 2)]
    return np.array(first, np.int32), np.array(mates, np.int32)


def column_scale(level):
    return jnp.ceil(jnp.log(jnp.maximum(level, TINY)) * (LOG_GRID / float(np.log(2.0))))


def encode(values, scale):
    return jnp.round(values * (jnp.exp2(scale * (-1.0 / LOG_GRID)) * FULL)).astype(S32).astype(S16)


def decode(coded, scale):
    return coded.astype(S32).astype(F32) * (jnp.exp2(scale * (1.0 / LOG_GRID)) * (1.0 / FULL))


def pack(out_ref, values, far):
    rows = values.shape[0]
    scale = column_scale(jnp.max(jnp.abs(values), axis=0, keepdims=True))
    out_ref[pl.ds(0, rows), :] = encode(values, scale)
    heads = jnp.broadcast_to(scale, (PAD, LANES))
    if far is None:
        out_ref[pl.ds(rows, PAD), :] = heads.astype(S32).astype(S16)
        return
    far_scale = column_scale(jnp.max(jnp.abs(far), axis=0, keepdims=True))
    out_ref[pl.ds(rows, PAD), :] = encode(far, far_scale)
    which = lax.broadcasted_iota(S32, (PAD, LANES), 0)
    heads = jnp.where(which == 0, heads, jnp.broadcast_to(far_scale, (PAD, LANES)))
    out_ref[pl.ds(rows + PAD, PAD), :] = heads.astype(S32).astype(S16)


def unpack_sum(refs, rows, has_far):
    total, far = None, None
    for ref in refs:
        heads = ref[pl.ds(rows + (PAD if has_far else 0), PAD), :].astype(S32).astype(F32)
        part = decode(ref[pl.ds(0, rows), :], heads[0:1])
        total = part if total is None else total + part
        if has_far:
            part = decode(ref[pl.ds(rows, PAD), :], heads[1:2])
            far = part if far is None else far + part
    return total, far


def product_kernel(has_far, rows, order_ref, live_ref, mate_ref, place_ref, v0, v1, v2, v3, t_ref, *rest):
    outs, (prod, moved) = rest[:8], rest[8:]
    step = pl.program_id(0)
    tile = v0.shape[1]
    half = CW // 2
    for part in range(2):
        total = None
        for j, v_ref in enumerate((v0, v1, v2, v3)):
            live = live_ref[step * 4 + j] > 0
            v = jnp.where(live, v_ref[0], jnp.zeros((), BF16))
            t = t_ref[:, j, :, pl.ds(part * half, half)].reshape(tile, half)
            add = jnp.dot(v, t, preferred_element_type=F32)
            total = add if total is None else total + add
        prod[pl.ds(pl.multiple_of(step * tile, tile), tile), pl.ds(part * half, half)] = total

    @pl.when(step == pl.num_programs(0) - 1)
    def _():
        z, x = place_ref[0], place_ref[1]
        for kx in range(SIDE):
            for kz in range(SIDE):
                zt = lax.rem(z + kz, SIDE)
                xt = lax.rem(x + kx, SIDE)
                base = pl.multiple_of((zt * SIDE + xt) * rows, rows)

                def gather(turn, carry):
                    for member in range(16):
                        at = turn * 16 + member
                        mate = mate_ref[base + at]
                        moved[pl.ds(at, 1), :] = prod[pl.ds(mate, 1), pl.ds(half, half)]
                    return carry

                lax.fori_loop(0, rows // 16, gather, 0)
                for side in range(2):
                    mine = prod[pl.ds(base, rows), pl.ds(side * LANES, LANES)]
                    other = moved[:, pl.ds(side * LANES, LANES)]
                    if has_far and side == 1:
                        lane = lax.broadcasted_iota(S32, (rows, LANES), 1)
                        far = prod[pl.ds(base, rows), pl.ds(half + LANES, LANES)]
                        far = (far + pltpu.roll(other, LANES - 16, 1)).T[96:112]
                        other = jnp.where(lane < 96, other, 0.0)
                    if side == 0:
                        near = mine + other
                    else:
                        far_one = far[:, :LANES] if has_far else None
                        far_two = far[:, LANES:] if has_far else None
                        pack(outs[kx].at[zt], near, far_one)
                        pack(outs[4 + kz].at[xt], mine + other, far_two)


def packed_rows(rows, has_far):
    return rows + PAD * (2 if has_far else 1)


def product(integrals, gathered, order, live, mates, place, rows, has_far):
    tiles, tile, _ = integrals.shape
    height = packed_rows(rows, has_far)
    total = SIDE * SIDE * rows
    spec = lambda j: pl.BlockSpec((1, tile, tile), lambda i, order, live, mates, place: (order[i * 4 + j], 0, 0))
    whole = lambda shape: pl.BlockSpec(shape, lambda i, *_: (0,) * len(shape))
    out = (SIDE, height, LANES)
    return pl.pallas_call(
        functools.partial(product_kernel, has_far, rows),
        out_shape=[jax.ShapeDtypeStruct(out, S16)] * 8,
        grid_spec=pltpu.PrefetchScalarGridSpec(
            num_scalar_prefetch=4,
            grid=(tiles // 4,),
            in_specs=[spec(j) for j in range(4)] + [whole(gathered.shape)],
            out_specs=[whole(out)] * 8,
            scratch_shapes=[pltpu.VMEM((total, CW), F32), pltpu.VMEM((rows, CW // 2), F32)],
        ),
        compiler_params=pltpu.CompilerParams(vmem_limit_bytes=VMEM, dimension_semantics=("arbitrary",)),
        cost_estimate=pl.CostEstimate(
            flops=2 * tiles * tile * tile * CW, bytes_accessed=integrals.size * 2, transcendentals=0
        ),
        name="product",
    )(order, live, mates, place, integrals, integrals, integrals, integrals, gathered)


def relay_kernel(has_far, rows, place_ref, *refs):
    ins, outs = refs[:8], refs[8:]
    for side in range(2):
        for k in range(SIDE):
            at = lax.rem(place_ref[side] + k, SIDE)
            total, far = unpack_sum([r.at[at] for r in ins[side * 4 : side * 4 + 4]], rows, has_far)
            pack(outs[side * 4 + k], total, far)


def relay(pieces, place, rows, has_far):
    height = packed_rows(rows, has_far)
    vmem = pl.BlockSpec(memory_space=pltpu.VMEM)
    return pl.pallas_call(
        functools.partial(relay_kernel, has_far, rows),
        out_shape=[jax.ShapeDtypeStruct((height, LANES), S16)] * 8,
        in_specs=[pl.BlockSpec(memory_space=pltpu.SMEM)] + [vmem] * 8,
        out_specs=[vmem] * 8,
        compiler_params=pltpu.CompilerParams(vmem_limit_bytes=VMEM),
        name="relay",
    )(place, *pieces)


def owner_kernel(rows, far_flags, source_ref, *refs):
    count = 8 * len(far_flags)
    ins, own, send, moved = refs[:count], refs[count], refs[count + 1], refs[count + 2]
    for c, has_far in enumerate(far_flags):
        fars = []
        for side in range(2):
            at = c * 8 + side * 4
            total, far = unpack_sum(ins[at : at + 4], rows, has_far)
            own[:, pl.ds((c * 2 + side) * LANES, LANES)] = total
            fars.append(far)
        if has_far:
            far = jnp.concatenate(fars, axis=1)
            far = jnp.concatenate([jnp.zeros((96, rows), F32), far, jnp.zeros((16, rows), F32)], axis=0)
            own[:, pl.ds(HALF, LANES)] = far.T

    def gather(turn, carry):
        for member in range(16):
            at = turn * 16 + member
            moved[pl.ds(at, 1), :] = own[pl.ds(source_ref[at], 1), :]
        return carry

    lax.fori_loop(0, rows // 16, gather, 0)
    scale = column_scale(jnp.max(jnp.abs(moved[...]), axis=1, keepdims=True))
    send[:, pl.ds(0, HALF)] = encode(moved[:, pl.ds(0, HALF)], scale)
    lane = lax.broadcasted_iota(S32, (rows, LANES), 1)
    far = jnp.round(moved[:, pl.ds(HALF, LANES)] * (jnp.exp2(scale * (-1.0 / LOG_GRID)) * FULL))
    far = jnp.where(lane == 0, jnp.broadcast_to(scale, (rows, LANES)), far)
    send[:, pl.ds(HALF, LANES)] = far.astype(S32).astype(S16)


def owner(pieces, source, rows, far_flags):
    vmem = pl.BlockSpec(memory_space=pltpu.VMEM)
    width = HALF + LANES
    return pl.pallas_call(
        functools.partial(owner_kernel, rows, far_flags),
        out_shape=[jax.ShapeDtypeStruct((rows, width), F32), jax.ShapeDtypeStruct((rows, width), S16)],
        in_specs=[pl.BlockSpec(memory_space=pltpu.SMEM)] + [vmem] * len(pieces),
        out_specs=[vmem] * 2,
        scratch_shapes=[pltpu.VMEM((rows, width), F32)],
        compiler_params=pltpu.CompilerParams(vmem_limit_bytes=VMEM),
        name="owner",
    )(source, *pieces)


def close_kernel(rows, index_ref, own, came, energy, pair_sum, spread, out, plain, fetched, joined):
    width = HALF + LANES
    heads = came[:, pl.ds(HALF, LANES)].astype(S32).astype(F32)
    scale = jnp.exp2(heads[:, 0:1] * (1.0 / LOG_GRID)) * (1.0 / FULL)
    plain[...] = came[...].astype(S32).astype(F32) * scale

    def gather(turn, carry):
        for member in range(16):
            at = turn * 16 + member
            fetched[pl.ds(at, 1), :] = plain[pl.ds(index_ref[at], 1), :]
        return carry

    lax.fori_loop(0, rows // 16, gather, 0)
    lane = lax.broadcasted_iota(S32, (rows, LANES), 1)
    edge = HALF - LANES
    joined[:, pl.ds(0, edge)] = own[:, pl.ds(0, edge)]
    joined[:, pl.ds(HALF, edge)] = fetched[:, pl.ds(0, edge)]
    last_own, last_came = own[:, pl.ds(edge, LANES)], fetched[:, pl.ds(edge, LANES)]
    joined[:, pl.ds(edge, LANES)] = last_own + jnp.where(lane < 96, 0.0, last_came)
    far_own, far_came = own[:, pl.ds(HALF, LANES)], pltpu.roll(fetched[:, pl.ds(HALF, LANES)], 16, 1)
    far = jnp.where(lane < 112, far_own, far_came)
    joined[:, pl.ds(HALF + edge, LANES)] = jnp.where(lane < 96, last_came, far)
    rest = joined[...]
    total = None
    for _ in range(3):
        part = rest.astype(BF16)
        rest = rest - part.astype(F32)
        add = jnp.dot(part, spread[...], preferred_element_type=F32)
        total = add if total is None else total + add
    out[...] = total / (energy[...] - pair_sum[...])


def close(own, came, index, energy, pair_sum, spread, rows):
    vmem = pl.BlockSpec(memory_space=pltpu.VMEM)
    width = HALF + LANES
    return pl.pallas_call(
        functools.partial(close_kernel, rows),
        out_shape=jax.ShapeDtypeStruct((rows, OCC), F32),
        in_specs=[pl.BlockSpec(memory_space=pltpu.SMEM)] + [vmem] * 5,
        out_specs=vmem,
        scratch_shapes=[pltpu.VMEM((rows, width), F32)] * 2 + [pltpu.VMEM((rows, OCC), F32)],
        compiler_params=pltpu.CompilerParams(vmem_limit_bytes=VMEM),
        name="close",
    )(index, own, came, energy, pair_sum, spread)


def shifted(dz, dx):
    return [
        (z * SIDE + x, (z + dz) % SIDE * SIDE + (x + dx) % SIDE) for z in range(SIDE) for x in range(SIDE)
    ]


def spread_out(pieces, across_x_first):
    got = list(pieces)
    for k in (2, 1, 3):
        for side in range(2):
            along_x = (side == 0) == across_x_first
            perm = shifted(0, k) if along_x else shifted(k, 0)
            got[side * 4 + k] = lax.ppermute(pieces[side * 4 + k], "col", perm)
    return got


def body(integrals, tile_count, tile_list, amplitudes, pair_energy, occ_energy, partner):
    rows = partner.shape[0]
    col_count = SIDE * SIDE
    first, mates_of = pair_orders()
    pieces = CW // 2
    column_order = np.concatenate(
        [np.concatenate([first[c * pieces :][:pieces], mates_of[c * pieces :][:pieces]]) for c in range(CHUNKS)]
    )
    pair_ids = jnp.arange(OCC, dtype=S32)
    sort = (pair_ids[:, None] == jnp.asarray(column_order)[None, :]).astype(BF16)
    spread = (jnp.asarray(np.concatenate([first, mates_of]))[:, None] == pair_ids[None, :]).astype(BF16)

    blocks, depth, _ = amplitudes.shape
    sorted_amp = jnp.dot(amplitudes.reshape(blocks * depth, OCC), sort, preferred_element_type=F32).astype(BF16)
    gathered = []
    for c in range(CHUNKS):
        part = sorted_amp[:, c * CW : (c + 1) * CW].reshape(blocks, depth, CW)
        gathered.append(lax.all_gather(part, "row", axis=0))

    all_partners = lax.all_to_all(
        jnp.broadcast_to(partner[None, :], (col_count, rows)), "col", split_axis=0, concat_axis=0, tiled=True
    )
    mates = (all_partners % (col_count * rows)).reshape(-1)
    col = lax.axis_index("col")
    place = jnp.stack([col // SIDE, col % SIDE]).astype(S32)
    slots = tile_list[0, 0]
    slot_ids = jnp.arange(slots.shape[0], dtype=S32)
    order = jnp.sum(jnp.where(slots[None, :] == slot_ids[:, None], slot_ids[None, :], 0), axis=1)
    live = (order < tile_count[0, 0]).astype(S32)

    peer = rows // col_count
    target = partner // rows % col_count
    key_local = partner % rows
    row_ids = jnp.arange(rows, dtype=S32)
    same_target = target[:, None] == target[None, :]
    send_rank = jnp.sum(same_target & (key_local[None, :] < key_local[:, None]), axis=1)
    recv_rank = jnp.sum(same_target & (row_ids[None, :] < row_ids[:, None]), axis=1)
    send_slot = target * peer + send_rank
    source = jnp.sum(jnp.where(send_slot[None, :] == row_ids[:, None], row_ids[None, :], 0), axis=1)
    index = target * peer + recv_rank

    tiles = integrals[0, 0]
    far_flags = tuple(c == CHUNKS - 1 for c in range(CHUNKS))
    landed = []
    for c in range(CHUNKS):
        parts = product(tiles, gathered[c], order, live, mates, place, rows, far_flags[c])
        parts = spread_out(parts, True)
        parts = relay(parts, place, rows, far_flags[c])
        landed += spread_out(parts, False)
    own, send = owner(landed, source, rows, far_flags)
    came = lax.all_to_all(send, "col", split_axis=0, concat_axis=0, tiled=True)
    pair_sum = (occ_energy[:, None] + occ_energy[None, :]).reshape(1, OCC)
    return close(own, came, index, pair_energy[:, None], pair_sum, spread, rows)


def solution(mesh):
    return jax.shard_map(
        body,
        mesh=mesh,
        in_specs=(
            P("row", "col", None, None, None),
            P("row", "col"),
            P("row", "col", None),
            P("col", "row", None),
            P(("row", "col")),
            P(),
            P(("row", "col")),
        ),
        out_specs=P(("row", "col"), None),
        check_vma=False,
    )
```

time: 562 us -> 197 us (0.35)
  waiting for transfers between devices: 433 us -> 32.1 us
  Pallas kernels: 0 us -> 81.7 us
  starting transfers between devices: 5.09 us -> 55.9 us
  local copies, waits for them, and re-layouts: 40.4 us -> 5.34 us
  other arithmetic: 37.2 us -> 5.33 us
  loops' own time: 14.7 us -> 0 us
  matrix products: 15.7 us -> 1.58 us
    reduce_scatter x1 -> x0, waiting for transfers between devices: 379 us -> none  [body(): summed = lax.psum_scatter(flat_rows, 'col', scatter_dimension=0, tiled=True)]
    pallas_call x0 -> x6, Pallas kernels: none -> 81.7 us  [the longest x2 66.1 us: product(): pl.pallas_call(functools.partial(product_kernel, has_far, rows), out_shap...]
    ppermute x0 -> x24, starting transfers between devices: none -> 40.9 us  [spread_out(): got[side * 4 + k] = lax.ppermute(pieces[side * 4 + k], 'col', perm)]
    dynamic_update_slice x8 -> x0, other arithmetic: 32.9 us -> none  [one_turn(): lax.dynamic_update_index_in_dim(running, current + product[member], block...]
    gather x8 -> x0, local copies, waits for them, and re-layouts: 27.9 us -> none  [the longest x2 12.9 us: one_turn(): chosen = jnp.take(tile_data, clipped, axis=0)]
    all_gather x1 -> x2, waiting for transfers between devices: 35.7 us -> 10.3 us  [body(): gathered.append(lax.all_gather(part, 'row', axis=0))]
    another operation x1 -> x0, loops' own time: 14.7 us -> none  [add_tiles(): return lax.fori_loop(0, turn_count, one_turn, partial_value)]
    dot_general x2 -> x1, matrix products: 15.7 us -> 1.58 us  [body(): jnp.dot(amplitudes.reshape(blocks * depth, OCC), sort, preferred_element_...]
  transfers between devices with their start and end apart: 3 -> 28, of which waited for: 3 -> 9; matrix products, arithmetic and copies ran while one was open for 0% -> 4% of each run, Pallas kernels for 0% -> 37%
where the time goes in v1:
time: 197 us; the launch traced here: 196 us
  Pallas kernels  81.7 us (41%)
  starting transfers between devices  55.9 us (28%)
  waiting for transfers between devices  32.1 us (16%)
  between operations  14.4 us (7%)
  local copies, waits for them, and re-layouts  5.34 us (3%)
  other arithmetic  5.33 us (3%)
    pallas_call x2, Pallas kernels, product(): pl.pallas_call(functools.partial(product_kernel, has_far, rows), out_shap...  66.1 us
    ppermute x24, starting transfers between devices, spread_out(): got[side * 4 + k] = lax.ppermute(pieces[side * 4 + k], 'col', perm)  40.9 us
    all_gather x2, waiting for transfers between devices, body(): gathered.append(lax.all_gather(part, 'row', axis=0))  10.3 us
    ppermute x24, waiting for transfers between devices, spread_out(): got[side * 4 + k] = lax.ppermute(pieces[side * 4 + k], 'col', perm)  9.86 us
    all_to_all x1, starting transfers between devices, body(): lax.all_to_all(jnp.broadcast_to(partner[None, :], (col_count, rows)), 'co...  7.96 us
    all_to_all x1, starting transfers between devices, body(): came = lax.all_to_all(send, 'col', split_axis=0, concat_axis=0, tiled=True)  6.93 us
    pallas_call x2, Pallas kernels, relay(): pl.pallas_call(functools.partial(relay_kernel, has_far, rows), out_shape=...  6.07 us
    pallas_call x1, Pallas kernels, close(): pl.pallas_call(functools.partial(close_kernel, rows), out_shape=jax.Shape...  5.9 us
  transfers between devices with their start and end apart: 28, of which 9 were waited for; matrix products, arithmetic and copies ran while one was open for 4% of the time, Pallas kernels for 37%

profile of v1, /device:TPU:0, one launch (start us, length us, event | category | flops | bytes accessed | tf_op | source)
XLA Modules:
  0.0 196.4 jit_solution(16210797212070556937)
XLA Ops:
  6.5 1.0 copy-done
  7.6 1.6 fusion.4
  9.2 0.8 fusion.7
  10.1 0.7 all-gather.5.cloned.1.call-update
  11.4 8.0 %all-to-all-start = ((s32[16,1,256]{2,1,0:T(1,128)}), s32[16,1,256]{2,1,0:T(1,128)S(1)}, u32[]{:S(2)}, u32[]{:S(2)}) async-start(s32[16,1,256]{2,1,0:T(1,128)} %broadcast_in_dim.25), calls=%async_computation | async-start | bytes 32768 | tf_op jit(solution)/shard_map/all_to_all | solution.py:303
  20.7 0.6 pad_add_fusion.place_ref
  21.4 5.6 %all-to-all-done = s32[16,1,256]{2,1,0:T(1,128)S(1)} async-done(((s32[16,1,256]{2,1,0:T(1,128)}), s32[16,1,256]{2,1,0:T(1,128)S(1)}, u32[]{:S(2)}, u32[]{:S(2)}) %all-to-all-start) | async-done | bytes 16416 | tf_op jit(solution)/shard_map/all_to_all | solution.py:303
  27.0 0.6 add_select_fusion.mate_ref
  27.6 10.3 %all-gather.3.cloned.1.call-done.t_ref = bf16[8,4,64,512]{3,2,1,0:T(8,128)(2,1)} async-done(((bf16[1,4,64,512]{3,2,1,0:T(8,128)(2,1)}), bf16[8,4,64,512]{3,2,1,0:T(8,128)(2,1)}) %all-gather.3.cloned.1.call-update) | async-done | bytes 2097168 | tf_op jit(solution)/shard_map/all_gather | solution.py:301
  37.8 32.1 %product.2 = (s16[4,272,128]{2,1,0:T(8,128)(2,1)}, s16[4,272,128]{2,1,0:T(8,128)(2,1)}, s16[4,272,128]{2,1,0:T(8,128)(2,1)}, s16[4,272,128]{2,1,0:T(8,128)(2,1)}...) custom-call(s32[32]{0:T(128)} %copy-done.28, ...), custom_call_target="tpu_custom_call" | custom-call | flops 8589934592 | bytes 16777216 | tf_op jit(solution)/shard_map/product/pallas_call | solution.py:138
  69.9 1.5 collective-permute-start
  71.3 2.7 %collective-permute-start.1 = (s16[4,272,128]{2,1,0:T(8,128)(2,1)}, s16[4,272,128]{2,1,0:T(8,128)(2,1)S(1)}, u32[]{:S(2)}, u32[]{:S(2)}) collective-permute-start(s16[4,272,128]{2,1,0:T(8,128)(2,1)} %get-tuple-element.41), channel_id=1, source_target_pairs={{0,2},{1,3},{2,0},{3,1},{4,6},{5,7},{6,4},{7,5},{8,10},{9,11},{10,... | collective-permute-start | bytes 835592 | tf_op jit(solution)/shard_map/ppermute | solution.py:280
  74.1 1.4 collective-permute-start.2
  75.5 1.6 collective-permute-start.3
  77.0 34.1 %product.3 = (s16[4,288,128]{2,1,0:T(8,128)(2,1)}, s16[4,288,128]{2,1,0:T(8,128)(2,1)}, s16[4,288,128]{2,1,0:T(8,128)(2,1)}, s16[4,288,128]{2,1,0:T(8,128)(2,1)}...) custom-call(s32[32]{0:T(128)} %copy-done.28, ...), custom_call_target="tpu_custom_call" | custom-call | flops 8589934592 | bytes 16777216 | tf_op jit(solution)/shard_map/product/pallas_call | solution.py:138
  111.1 0.6 collective-permute-start.12
  111.8 3.0 %collective-permute-start.4 = (s16[4,272,128]{2,1,0:T(8,128)(2,1)S(1)}, s16[4,272,128]{2,1,0:T(8,128)(2,1)S(1)}, u32[]{:S(2)}, u32[]{:S(2)}) collective-permute-start(s16[4,272,128]{2,1,0:T(8,128)(2,1)S(1)} %copy-done.32), channel_id=1, source_target_pairs={{0,8},{1,9},{2,10},{3,11},{4,12},{5,13},{6,14},{7,15},{8,0},{9,1},... | collective-permute-start | bytes 835592 | tf_op jit(solution)/shard_map/ppermute | solution.py:280
  114.7 1.4 collective-permute-start.5
  116.2 0.9 collective-permute-start.13
  117.1 2.0 %collective-permute-start.14 = (s16[4,288,128]{2,1,0:T(8,128)(2,1)}, s16[4,288,128]{2,1,0:T(8,128)(2,1)S(1)}, u32[]{:S(2)}, u32[]{:S(2)}) collective-permute-start(s16[4,288,128]{2,1,0:T(8,128)(2,1)} %get-tuple-element.58), channel_id=1, source_target_pairs={{0,3},{1,0},{2,1},{3,2},{4,7},{5,4},{6,5},{7,6},{8,11},{9,8},{10,9... | collective-permute-start | bytes 884744 | tf_op jit(solution)/shard_map/ppermute | solution.py:280
  119.1 1.7 collective-permute-done.4.refs_6_
  120.8 3.7 %collective-permute-start.15 = (s16[4,288,128]{2,1,0:T(8,128)(2,1)}, s16[4,288,128]{2,1,0:T(8,128)(2,1)S(1)}, u32[]{:S(2)}, u32[]{:S(2)}) collective-permute-start(s16[4,288,128]{2,1,0:T(8,128)(2,1)} %get-tuple-element.60), channel_id=1, source_target_pairs={{0,4},{1,5},{2,6},{3,7},{4,8},{5,9},{6,10},{7,11},{8,12},{9,13},{1... | collective-permute-start | bytes 884744 | tf_op jit(solution)/shard_map/ppermute | solution.py:280
  124.5 1.5 collective-permute-done.5.refs_7_
  126.0 3.0 %collective-permute-start.16 = (s16[4,288,128]{2,1,0:T(8,128)(2,1)}, s16[4,288,128]{2,1,0:T(8,128)(2,1)S(1)}, u32[]{:S(2)}, u32[]{:S(2)}) collective-permute-start(s16[4,288,128]{2,1,0:T(8,128)(2,1)} %get-tuple-element.61), channel_id=1, source_target_pairs={{0,8},{1,9},{2,10},{3,11},{4,12},{5,13},{6,14},{7,15},{8,0},{9,1},... | collective-permute-start | bytes 884744 | tf_op jit(solution)/shard_map/ppermute | solution.py:280
  128.9 1.5 collective-permute-start.17
  130.5 3.0 %relay.2 = (s16[272,128]{1,0:T(8,128)(2,1)}, s16[272,128]{1,0:T(8,128)(2,1)}, s16[272,128]{1,0:T(8,128)(2,1)}, s16[272,128]{1,0:T(8,128)(2,1)}, s16[272,128]{1,0...) custom-call(s32[2]{0:T(128)} %pad_add_fusion.place_ref, ...), custom_call_target="tpu_custom_call" | custom-call | tf_op jit(solution)/shard_map/relay/pallas_call | solution.py:168
  133.5 1.3 collective-permute-start.10
  134.8 1.8 collective-permute-start.11
  137.5 1.8 collective-permute-start.7
  139.3 4.3 %collective-permute-done.17.refs_7_ = s16[4,288,128]{2,1,0:T(8,128)(2,1)S(1)} collective-permute-done((s16[4,288,128]{2,1,0:T(8,128)(2,1)}, s16[4,288,128]{2,1,0:T(8,128)(2,1)S(1)}, u32[]{:S(2)}, u32[]{:S(2)}) %collective-permute-start.17) | collective-permute-done | bytes 294944 | tf_op jit(solution)/shard_map/ppermute | solution.py:280
  143.6 2.6 %collective-permute-start.8 = (s16[272,128]{1,0:T(8,128)(2,1)}, s16[272,128]{1,0:T(8,128)(2,1)S(1)}, u32[]{:S(2)}, u32[]{:S(2)}) collective-permute-start(s16[272,128]{1,0:T(8,128)(2,1)} %get-tuple-element.50), channel_id=1, source_target_pairs={{0,12},{1,13},{2,14},{3,15},{4,0},{5,1},{6,2},{7,3},{8,4},{9,5},{1... | collective-permute-start | bytes 208904 | tf_op jit(solution)/shard_map/ppermute | solution.py:280
  146.3 3.1 %relay.3 = (s16[288,128]{1,0:T(8,128)(2,1)}, s16[288,128]{1,0:T(8,128)(2,1)}, s16[288,128]{1,0:T(8,128)(2,1)}, s16[288,128]{1,0:T(8,128)(2,1)}, s16[288,128]{1,0...) custom-call(s32[2]{0:T(128)} %pad_add_fusion.place_ref, ...), custom_call_target="tpu_custom_call" | custom-call | tf_op jit(solution)/shard_map/relay/pallas_call | solution.py:168
  149.9 0.6 multiply_add_fusion
  150.5 2.1 %collective-permute-start.19 = (s16[288,128]{1,0:T(8,128)(2,1)}, s16[288,128]{1,0:T(8,128)(2,1)S(1)}, u32[]{:S(2)}, u32[]{:S(2)}) collective-permute-start(s16[288,128]{1,0:T(8,128)(2,1)} %get-tuple-element.65), channel_id=1, source_target_pairs={{0,8},{1,9},{2,10},{3,11},{4,12},{5,13},{6,14},{7,15},{8,0},{9,1},... | collective-permute-start | bytes 221192 | tf_op jit(solution)/shard_map/ppermute | solution.py:280
  152.6 1.2 collective-permute-start.20
  153.8 0.8 collective-permute-start.21
  155.2 2.9 %collective-permute-start.22 = (s16[288,128]{1,0:T(8,128)(2,1)}, s16[288,128]{1,0:T(8,128)(2,1)S(1)}, u32[]{:S(2)}, u32[]{:S(2)}) collective-permute-start(s16[288,128]{1,0:T(8,128)(2,1)} %get-tuple-element.69), channel_id=1, source_target_pairs={{0,2},{1,3},{2,0},{3,1},{4,6},{5,7},{6,4},{7,5},{8,10},{9,11},{10,... | collective-permute-start | bytes 221192 | tf_op jit(solution)/shard_map/ppermute | solution.py:280
  158.1 2.1 %collective-permute-start.23 = (s16[288,128]{1,0:T(8,128)(2,1)}, s16[288,128]{1,0:T(8,128)(2,1)S(1)}, u32[]{:S(2)}, u32[]{:S(2)}) collective-permute-start(s16[288,128]{1,0:T(8,128)(2,1)} %get-tuple-element.70), channel_id=1, source_target_pairs={{0,3},{1,0},{2,1},{3,2},{4,7},{5,4},{6,5},{7,6},{8,11},{9,8},{10,9... | collective-permute-start | bytes 221192 | tf_op jit(solution)/shard_map/ppermute | solution.py:280
  160.1 0.7 select_reduce_fusion.source_ref
  161.4 1.2 collective-permute-done.23.refs_15_
  163.3 3.6 %owner.1 = (f32[256,640]{1,0:T(8,128)}, s16[256,640]{1,0:T(8,128)(2,1)}) custom-call(s32[256]{0:T(256)} %select_reduce_fusion.source_ref, s16[272,128]{1,0:T(8,128)(2,1)} %get-tuple-element.47.refs_0_, s16[272,128]{1,0:T(8,128)(2,1)} %copy-done.22, s16[272,128]{1,0:T(8,128)(2,1)} %copy-done.23, s16[272,128]{1,0:T(8,128)(2,1)} %copy-done.24, ...), custom_call_target="tpu_custom_call" | custom-call | tf_op jit(solution)/shard_map/owner/pallas_call | solution.py:211
  166.9 6.9 %all-to-all-start.1 = ((s16[16,16,640]{2,1,0:T(8,128)(2,1)}), s16[16,16,640]{2,1,0:T(8,128)(2,1)S(1)}, u32[]{:S(2)}, u32[]{:S(2)}) async-start(s16[16,16,640]{2,1,0:T(8,128)(2,1)} %bitcast.28), calls=%async_computation.1 | async-start | bytes 655360 | tf_op jit(solution)/shard_map/all_to_all | solution.py:334
  173.9 0.8 copy.12.energy
  174.7 0.7 add.61.pair_sum
  175.4 1.7 fusion.1.spread
  177.2 5.7 %all-to-all-done.1 = s16[16,16,640]{2,1,0:T(8,128)(2,1)S(1)} async-done(((s16[16,16,640]{2,1,0:T(8,128)(2,1)}), s16[16,16,640]{2,1,0:T(8,128)(2,1)S(1)}, u32[]{:S(2)}, u32[]{:S(2)}) %all-to-all-start.1) | async-done | bytes 327712 | tf_op jit(solution)/shard_map/all_to_all | solution.py:334
  182.9 0.7 copy-done.1
  183.6 5.9 %close.1 = f32[256,1024]{1,0:T(8,128)} custom-call(s32[256]{0:T(256)} %get-tuple-element.78.index_ref, f32[256,640]{1,0:T(8,128)} %get-tuple-element.71.own, s16[256,640]{1,0:T(8,128)(2,1)} %bitcast.25, f32[256,1]{1,0:T(8,128)} %copy.12.energy, f32[1,1024]{1,0:T(1,128)} %add.61.pair_sum, bf16[1024,1024]{1,0:T(8,128)(2,1)} %fusion.1.spread), custom_call_target="tpu_custom_call" | custom-call | tf_op jit(solution)/shard_map/close/pallas_call | solution.py:257
  (99 shorter events, 4.6 us)
Async XLA Ops:
  6.5 13.5 %copy-start.33 = (s32[1,1,32]{2,1,0:T(1,128)S(1)}, s32[1,1,32]{2,1,0:T(1,128)}, u32[]{:S(2)}) copy-start(s32[1,1,32]{2,1,0:T(1,128)} %param.11) | copy-start | bytes 388
  6.5 31.3 %all-gather.3.cloned.1.call-start = ((), (), s32[]{:S(2)}) async-start(), calls=%async_computation.2 | async-start | bytes 2359296 | tf_op jit(solution)/shard_map/all_gather | solution.py:301
  10.0 67.0 %all-gather.5.cloned.1.call-start = ((), (), s32[]{:S(2)}) async-start(), calls=%async_computation.3 | async-start | bytes 2359296 | tf_op jit(solution)/shard_map/all_gather | solution.py:301
  11.4 15.6 %all-to-all-start = ((s32[16,1,256]{2,1,0:T(1,128)}), s32[16,1,256]{2,1,0:T(1,128)S(1)}, u32[]{:S(2)}, u32[]{:S(2)}) async-start(s32[16,1,256]{2,1,0:T(1,128)} %broadcast_in_dim.25), calls=%async_computation | async-start | bytes 32768 | tf_op jit(solution)/shard_map/all_to_all | solution.py:303
  20.2 17.7 %copy-start.28 = (s32[32]{0:T(128)}, s32[32]{0:T(128)S(1)}, u32[]{:S(2)}) copy-start(s32[32]{0:T(128)S(1)} %select_reduce_fusion.1.order_ref) | copy-start | bytes 388
  69.9 41.9 %collective-permute-start = (s16[4,272,128]{2,1,0:T(8,128)(2,1)}, s16[4,272,128]{2,1,0:T(8,128)(2,1)S(1)}, u32[]{:S(2)}, u32[]{:S(2)}) collective-permute-start(s16[4,272,128]{2,1,0:T(8,128)(2,1)} %get-tuple-element.40), channel_id=1, source_target_pairs={{0,1},{1,2},{2,3},{3,0},{4,5},{5,6},{6,7},{7,4},{8,9},{9,10},{10,1... | collective-permute-start | bytes 835592 | tf_op jit(solution)/shard_map/ppermute | solution.py:280
  71.3 43.4 %collective-permute-start.1 = (s16[4,272,128]{2,1,0:T(8,128)(2,1)}, s16[4,272,128]{2,1,0:T(8,128)(2,1)S(1)}, u32[]{:S(2)}, u32[]{:S(2)}) collective-permute-start(s16[4,272,128]{2,1,0:T(8,128)(2,1)} %get-tuple-element.41), channel_id=1, source_target_pairs={{0,2},{1,3},{2,0},{3,1},{4,6},{5,7},{6,4},{7,5},{8,10},{9,11},{10,... | collective-permute-start | bytes 835592 | tf_op jit(solution)/shard_map/ppermute | solution.py:280
  74.1 42.1 %collective-permute-start.2 = (s16[4,272,128]{2,1,0:T(8,128)(2,1)}, s16[4,272,128]{2,1,0:T(8,128)(2,1)S(1)}, u32[]{:S(2)}, u32[]{:S(2)}) collective-permute-start(s16[4,272,128]{2,1,0:T(8,128)(2,1)} %get-tuple-element.42), channel_id=1, source_target_pairs={{0,3},{1,0},{2,1},{3,2},{4,7},{5,4},{6,5},{7,6},{8,11},{9,8},{10,9... | collective-permute-start | bytes 835592 | tf_op jit(solution)/shard_map/ppermute | solution.py:280
  75.5 36.3 %copy-start.32 = (s16[4,272,128]{2,1,0:T(8,128)(2,1)S(1)}, s16[4,272,128]{2,1,0:T(8,128)(2,1)}, u32[]{:S(2)}) copy-start(s16[4,272,128]{2,1,0:T(8,128)(2,1)} %get-tuple-element.45) | copy-start | bytes 835588
  75.5 39.2 %copy-start.31 = (s16[4,272,128]{2,1,0:T(8,128)(2,1)S(1)}, s16[4,272,128]{2,1,0:T(8,128)(2,1)}, u32[]{:S(2)}) copy-start(s16[4,272,128]{2,1,0:T(8,128)(2,1)} %get-tuple-element.46) | copy-start | bytes 835588
  75.5 41.6 %collective-permute-start.3 = (s16[4,272,128]{2,1,0:T(8,128)(2,1)}, s16[4,272,128]{2,1,0:T(8,128)(2,1)S(1)}, u32[]{:S(2)}, u32[]{:S(2)}) collective-permute-start(s16[4,272,128]{2,1,0:T(8,128)(2,1)} %get-tuple-element.44), channel_id=1, source_target_pairs={{0,4},{1,5},{2,6},{3,7},{4,8},{5,9},{6,10},{7,11},{8,12},{9,13},{1... | collective-permute-start | bytes 835592 | tf_op jit(solution)/shard_map/ppermute | solution.py:280
  111.1 62.8 %copy-start.29 = (f32[32]{0:T(128)S(1)}, f32[32]{0:T(128)}, u32[]{:S(2)}) copy-start(f32[32]{0:T(128)} %param.14) | copy-start | bytes 388
  111.1 62.8 %copy-start.30 = (f32[256]{0:T(256)S(1)}, f32[256]{0:T(256)}, u32[]{:S(2)}) copy-start(f32[256]{0:T(256)} %param.13) | copy-start | bytes 3076
  111.1 64.3 %copy-start.26 = (s32[1024]{0:T(1024)S(1)}, s32[1024]{0:T(1024)}, u32[]{:S(2)}) copy-start(s32[1024]{0:T(1024)} %constant.87.clone) | copy-start | bytes 12292
  111.1 17.8 %collective-permute-start.12 = (s16[4,288,128]{2,1,0:T(8,128)(2,1)}, s16[4,288,128]{2,1,0:T(8,128)(2,1)S(1)}, u32[]{:S(2)}, u32[]{:S(2)}) collective-permute-start(s16[4,288,128]{2,1,0:T(8,128)(2,1)} %get-tuple-element.56), channel_id=1, source_target_pairs={{0,1},{1,2},{2,3},{3,0},{4,5},{5,6},{6,7},{7,4},{8,9},{9,10},{10,1... | collective-permute-start | bytes 884744 | tf_op jit(solution)/shard_map/ppermute | solution.py:280
  111.8 18.7 %copy-start.8 = (s16[4,272,128]{2,1,0:T(8,128)(2,1)}, s16[4,272,128]{2,1,0:T(8,128)(2,1)S(1)}, u32[]{:S(2)}) copy-start(s16[4,272,128]{2,1,0:T(8,128)(2,1)S(1)} %collective-permute-done.refs_1_) | copy-start | bytes 835588
  111.8 9.0 %collective-permute-start.4 = (s16[4,272,128]{2,1,0:T(8,128)(2,1)S(1)}, s16[4,272,128]{2,1,0:T(8,128)(2,1)S(1)}, u32[]{:S(2)}, u32[]{:S(2)}) collective-permute-start(s16[4,272,128]{2,1,0:T(8,128)(2,1)S(1)} %copy-done.32), channel_id=1, source_target_pairs={{0,8},{1,9},{2,10},{3,11},{4,12},{5,13},{6,14},{7,15},{8,0},{9,1},... | collective-permute-start | bytes 835592 | tf_op jit(solution)/shard_map/ppermute | solution.py:280
  114.7 15.7 %copy-start.9 = (s16[4,272,128]{2,1,0:T(8,128)(2,1)}, s16[4,272,128]{2,1,0:T(8,128)(2,1)S(1)}, u32[]{:S(2)}) copy-start(s16[4,272,128]{2,1,0:T(8,128)(2,1)S(1)} %collective-permute-done.1.refs_2_) | copy-start | bytes 835588
  114.7 11.2 %collective-permute-start.5 = (s16[4,272,128]{2,1,0:T(8,128)(2,1)S(1)}, s16[4,272,128]{2,1,0:T(8,128)(2,1)S(1)}, u32[]{:S(2)}, u32[]{:S(2)}) collective-permute-start(s16[4,272,128]{2,1,0:T(8,128)(2,1)S(1)} %copy-done.31), channel_id=1, source_target_pairs={{0,12},{1,13},{2,14},{3,15},{4,0},{5,1},{6,2},{7,3},{8,4},{9,5},{1... | collective-permute-start | bytes 835592 | tf_op jit(solution)/shard_map/ppermute | solution.py:280
  116.2 14.3 %copy-start.10 = (s16[4,272,128]{2,1,0:T(8,128)(2,1)}, s16[4,272,128]{2,1,0:T(8,128)(2,1)S(1)}, u32[]{:S(2)}) copy-start(s16[4,272,128]{2,1,0:T(8,128)(2,1)S(1)} %collective-permute-done.2.refs_3_) | copy-start | bytes 835588
  116.2 17.4 %collective-permute-start.13 = (s16[4,288,128]{2,1,0:T(8,128)(2,1)}, s16[4,288,128]{2,1,0:T(8,128)(2,1)S(1)}, u32[]{:S(2)}, u32[]{:S(2)}) collective-permute-start(s16[4,288,128]{2,1,0:T(8,128)(2,1)} %get-tuple-element.57), channel_id=1, source_target_pairs={{0,2},{1,3},{2,0},{3,1},{4,6},{5,7},{6,4},{7,5},{8,10},{9,11},{10,... | collective-permute-start | bytes 884744 | tf_op jit(solution)/shard_map/ppermute | solution.py:280
  117.1 13.4 %copy-start.11 = (s16[4,272,128]{2,1,0:T(8,128)(2,1)}, s16[4,272,128]{2,1,0:T(8,128)(2,1)S(1)}, u32[]{:S(2)}) copy-start(s16[4,272,128]{2,1,0:T(8,128)(2,1)S(1)} %collective-permute-done.3.refs_5_) | copy-start | bytes 835588
  117.1 17.7 %collective-permute-start.14 = (s16[4,288,128]{2,1,0:T(8,128)(2,1)}, s16[4,288,128]{2,1,0:T(8,128)(2,1)S(1)}, u32[]{:S(2)}, u32[]{:S(2)}) collective-permute-start(s16[4,288,128]{2,1,0:T(8,128)(2,1)} %get-tuple-element.58), channel_id=1, source_target_pairs={{0,3},{1,0},{2,1},{3,2},{4,7},{5,4},{6,5},{7,6},{8,11},{9,8},{10,9... | collective-permute-start | bytes 884744 | tf_op jit(solution)/shard_map/ppermute | solution.py:280
  120.8 9.7 %copy-start.12 = (s16[4,272,128]{2,1,0:T(8,128)(2,1)}, s16[4,272,128]{2,1,0:T(8,128)(2,1)S(1)}, u32[]{:S(2)}) copy-start(s16[4,272,128]{2,1,0:T(8,128)(2,1)S(1)} %collective-permute-done.4.refs_6_) | copy-start | bytes 835588
  120.8 16.1 %collective-permute-start.15 = (s16[4,288,128]{2,1,0:T(8,128)(2,1)}, s16[4,288,128]{2,1,0:T(8,128)(2,1)S(1)}, u32[]{:S(2)}, u32[]{:S(2)}) collective-permute-start(s16[4,288,128]{2,1,0:T(8,128)(2,1)} %get-tuple-element.60), channel_id=1, source_target_pairs={{0,4},{1,5},{2,6},{3,7},{4,8},{5,9},{6,10},{7,11},{8,12},{9,13},{1... | collective-permute-start | bytes 884744 | tf_op jit(solution)/shard_map/ppermute | solution.py:280
  126.0 11.5 %collective-permute-start.16 = (s16[4,288,128]{2,1,0:T(8,128)(2,1)}, s16[4,288,128]{2,1,0:T(8,128)(2,1)S(1)}, u32[]{:S(2)}, u32[]{:S(2)}) collective-permute-start(s16[4,288,128]{2,1,0:T(8,128)(2,1)} %get-tuple-element.61), channel_id=1, source_target_pairs={{0,8},{1,9},{2,10},{3,11},{4,12},{5,13},{6,14},{7,15},{8,0},{9,1},... | collective-permute-start | bytes 884744 | tf_op jit(solution)/shard_map/ppermute | solution.py:280
  128.9 17.3 %copy-start.2 = (s16[4,288,128]{2,1,0:T(8,128)(2,1)}, s16[4,288,128]{2,1,0:T(8,128)(2,1)S(1)}, u32[]{:S(2)}) copy-start(s16[4,288,128]{2,1,0:T(8,128)(2,1)S(1)} %collective-permute-done.12.refs_1_) | copy-start | bytes 884740
  128.9 14.7 %collective-permute-start.17 = (s16[4,288,128]{2,1,0:T(8,128)(2,1)}, s16[4,288,128]{2,1,0:T(8,128)(2,1)S(1)}, u32[]{:S(2)}, u32[]{:S(2)}) collective-permute-start(s16[4,288,128]{2,1,0:T(8,128)(2,1)} %get-tuple-element.62), channel_id=1, source_target_pairs={{0,12},{1,13},{2,14},{3,15},{4,0},{5,1},{6,2},{7,3},{8,4},{9,5},{1... | collective-permute-start | bytes 884744 | tf_op jit(solution)/shard_map/ppermute | solution.py:280
  133.5 12.7 %copy-start.3 = (s16[4,288,128]{2,1,0:T(8,128)(2,1)}, s16[4,288,128]{2,1,0:T(8,128)(2,1)S(1)}, u32[]{:S(2)}) copy-start(s16[4,288,128]{2,1,0:T(8,128)(2,1)S(1)} %collective-permute-done.13.refs_2_) | copy-start | bytes 884740
  133.5 15.8 %collective-permute-start.10 = (s16[272,128]{1,0:T(8,128)(2,1)}, s16[272,128]{1,0:T(8,128)(2,1)S(1)}, u32[]{:S(2)}, u32[]{:S(2)}) collective-permute-start(s16[272,128]{1,0:T(8,128)(2,1)} %get-tuple-element.53), channel_id=1, source_target_pairs={{0,2},{1,3},{2,0},{3,1},{4,6},{5,7},{6,4},{7,5},{8,10},{9,11},{10,... | collective-permute-start | bytes 208904 | tf_op jit(solution)/shard_map/ppermute | solution.py:280
  134.8 11.5 %copy-start.4 = (s16[4,288,128]{2,1,0:T(8,128)(2,1)}, s16[4,288,128]{2,1,0:T(8,128)(2,1)S(1)}, u32[]{:S(2)}) copy-start(s16[4,288,128]{2,1,0:T(8,128)(2,1)S(1)} %collective-permute-done.14.refs_3_) | copy-start | bytes 884740
  134.8 15.1 %collective-permute-start.11 = (s16[272,128]{1,0:T(8,128)(2,1)}, s16[272,128]{1,0:T(8,128)(2,1)S(1)}, u32[]{:S(2)}, u32[]{:S(2)}) collective-permute-start(s16[272,128]{1,0:T(8,128)(2,1)} %get-tuple-element.54), channel_id=1, source_target_pairs={{0,3},{1,0},{2,1},{3,2},{4,7},{5,4},{6,5},{7,6},{8,11},{9,8},{10,9... | collective-permute-start | bytes 208904 | tf_op jit(solution)/shard_map/ppermute | solution.py:280
  136.9 9.4 %copy-start.5 = (s16[4,288,128]{2,1,0:T(8,128)(2,1)}, s16[4,288,128]{2,1,0:T(8,128)(2,1)S(1)}, u32[]{:S(2)}) copy-start(s16[4,288,128]{2,1,0:T(8,128)(2,1)S(1)} %collective-permute-done.15.refs_5_) | copy-start | bytes 884740
  136.9 13.6 %collective-permute-start.6 = (s16[272,128]{1,0:T(8,128)(2,1)}, s16[272,128]{1,0:T(8,128)(2,1)S(1)}, u32[]{:S(2)}, u32[]{:S(2)}) collective-permute-start(s16[272,128]{1,0:T(8,128)(2,1)} %get-tuple-element.48), channel_id=1, source_target_pairs={{0,4},{1,5},{2,6},{3,7},{4,8},{5,9},{6,10},{7,11},{8,12},{9,13},{1... | collective-permute-start | bytes 208904 | tf_op jit(solution)/shard_map/ppermute | solution.py:280
  137.5 15.1 %collective-permute-start.7 = (s16[272,128]{1,0:T(8,128)(2,1)}, s16[272,128]{1,0:T(8,128)(2,1)S(1)}, u32[]{:S(2)}, u32[]{:S(2)}) collective-permute-start(s16[272,128]{1,0:T(8,128)(2,1)} %get-tuple-element.49), channel_id=1, source_target_pairs={{0,8},{1,9},{2,10},{3,11},{4,12},{5,13},{6,14},{7,15},{8,0},{9,1},... | collective-permute-start | bytes 208904 | tf_op jit(solution)/shard_map/ppermute | solution.py:280
  143.6 10.2 %collective-permute-start.8 = (s16[272,128]{1,0:T(8,128)(2,1)}, s16[272,128]{1,0:T(8,128)(2,1)S(1)}, u32[]{:S(2)}, u32[]{:S(2)}) collective-permute-start(s16[272,128]{1,0:T(8,128)(2,1)} %get-tuple-element.50), channel_id=1, source_target_pairs={{0,12},{1,13},{2,14},{3,15},{4,0},{5,1},{6,2},{7,3},{8,4},{9,5},{1... | collective-permute-start | bytes 208904 | tf_op jit(solution)/shard_map/ppermute | solution.py:280
  149.4 13.3 %copy-start.20 = (s16[272,128]{1,0:T(8,128)(2,1)}, s16[272,128]{1,0:T(8,128)(2,1)S(1)}, u32[]{:S(2)}) copy-start(s16[272,128]{1,0:T(8,128)(2,1)S(1)} %collective-permute-done.10.refs_6_) | copy-start | bytes 208900
  149.4 5.8 %collective-permute-start.9 = (s16[272,128]{1,0:T(8,128)(2,1)}, s16[272,128]{1,0:T(8,128)(2,1)S(1)}, u32[]{:S(2)}, u32[]{:S(2)}) collective-permute-start(s16[272,128]{1,0:T(8,128)(2,1)} %get-tuple-element.52), channel_id=1, source_target_pairs={{0,1},{1,2},{2,3},{3,0},{4,5},{5,6},{6,7},{7,4},{8,9},{9,10},{10,1... | collective-permute-start | bytes 208904 | tf_op jit(solution)/shard_map/ppermute | solution.py:280
  149.8 12.8 %copy-start.21 = (s16[272,128]{1,0:T(8,128)(2,1)}, s16[272,128]{1,0:T(8,128)(2,1)S(1)}, u32[]{:S(2)}) copy-start(s16[272,128]{1,0:T(8,128)(2,1)S(1)} %collective-permute-done.11.refs_7_) | copy-start | bytes 208900
  149.8 8.2 %collective-permute-start.18 = (s16[288,128]{1,0:T(8,128)(2,1)}, s16[288,128]{1,0:T(8,128)(2,1)S(1)}, u32[]{:S(2)}, u32[]{:S(2)}) collective-permute-start(s16[288,128]{1,0:T(8,128)(2,1)} %get-tuple-element.64), channel_id=1, source_target_pairs={{0,4},{1,5},{2,6},{3,7},{4,8},{5,9},{6,10},{7,11},{8,12},{9,13},{1... | collective-permute-start | bytes 221192 | tf_op jit(solution)/shard_map/ppermute | solution.py:280
  150.5 12.2 %copy-start.22 = (s16[272,128]{1,0:T(8,128)(2,1)}, s16[272,128]{1,0:T(8,128)(2,1)S(1)}, u32[]{:S(2)}) copy-start(s16[272,128]{1,0:T(8,128)(2,1)S(1)} %collective-permute-done.6.refs_1_) | copy-start | bytes 208900
  150.5 10.4 %collective-permute-start.19 = (s16[288,128]{1,0:T(8,128)(2,1)}, s16[288,128]{1,0:T(8,128)(2,1)S(1)}, u32[]{:S(2)}, u32[]{:S(2)}) collective-permute-start(s16[288,128]{1,0:T(8,128)(2,1)} %get-tuple-element.65), channel_id=1, source_target_pairs={{0,8},{1,9},{2,10},{3,11},{4,12},{5,13},{6,14},{7,15},{8,0},{9,1},... | collective-permute-start | bytes 221192 | tf_op jit(solution)/shard_map/ppermute | solution.py:280
  152.6 10.1 %copy-start.23 = (s16[272,128]{1,0:T(8,128)(2,1)}, s16[272,128]{1,0:T(8,128)(2,1)S(1)}, u32[]{:S(2)}) copy-start(s16[272,128]{1,0:T(8,128)(2,1)S(1)} %collective-permute-done.7.refs_2_) | copy-start | bytes 208900
  152.6 8.3 %collective-permute-start.20 = (s16[288,128]{1,0:T(8,128)(2,1)}, s16[288,128]{1,0:T(8,128)(2,1)S(1)}, u32[]{:S(2)}, u32[]{:S(2)}) collective-permute-start(s16[288,128]{1,0:T(8,128)(2,1)} %get-tuple-element.66), channel_id=1, source_target_pairs={{0,12},{1,13},{2,14},{3,15},{4,0},{5,1},{6,2},{7,3},{8,4},{9,5},{1... | collective-permute-start | bytes 221192 | tf_op jit(solution)/shard_map/ppermute | solution.py:280
  153.8 7.1 %collective-permute-start.21 = (s16[288,128]{1,0:T(8,128)(2,1)}, s16[288,128]{1,0:T(8,128)(2,1)S(1)}, u32[]{:S(2)}, u32[]{:S(2)}) collective-permute-start(s16[288,128]{1,0:T(8,128)(2,1)} %get-tuple-element.68), channel_id=1, source_target_pairs={{0,1},{1,2},{2,3},{3,0},{4,5},{5,6},{6,7},{7,4},{8,9},{9,10},{10,1... | collective-permute-start | bytes 221192 | tf_op jit(solution)/shard_map/ppermute | solution.py:280
  155.2 6.2 %collective-permute-start.22 = (s16[288,128]{1,0:T(8,128)(2,1)}, s16[288,128]{1,0:T(8,128)(2,1)S(1)}, u32[]{:S(2)}, u32[]{:S(2)}) collective-permute-start(s16[288,128]{1,0:T(8,128)(2,1)} %get-tuple-element.69), channel_id=1, source_target_pairs={{0,2},{1,3},{2,0},{3,1},{4,6},{5,7},{6,4},{7,5},{8,10},{9,11},{10,... | collective-permute-start | bytes 221192 | tf_op jit(solution)/shard_map/ppermute | solution.py:280
  158.1 4.6 %collective-permute-start.23 = (s16[288,128]{1,0:T(8,128)(2,1)}, s16[288,128]{1,0:T(8,128)(2,1)S(1)}, u32[]{:S(2)}, u32[]{:S(2)}) collective-permute-start(s16[288,128]{1,0:T(8,128)(2,1)} %get-tuple-element.70), channel_id=1, source_target_pairs={{0,3},{1,0},{2,1},{3,2},{4,7},{5,4},{6,5},{7,6},{8,11},{9,8},{10,9... | collective-permute-start | bytes 221192 | tf_op jit(solution)/shard_map/ppermute | solution.py:280
  166.9 16.0 %all-to-all-start.1 = ((s16[16,16,640]{2,1,0:T(8,128)(2,1)}), s16[16,16,640]{2,1,0:T(8,128)(2,1)S(1)}, u32[]{:S(2)}, u32[]{:S(2)}) async-start(s16[16,16,640]{2,1,0:T(8,128)(2,1)} %bitcast.28), calls=%async_computation.1 | async-start | bytes 655360 | tf_op jit(solution)/shard_map/all_to_all | solution.py:334
  (14 other events, 50.5 us)
Sparse Core Ops, SparseCore 0:
  10.1 27.6 all-gather.2
  39.5 25.4 all-gather.4

commit v2 on v1

v2 whole, which is shorter than its diff:
```python
import functools

import numpy as np
import jax
import jax.numpy as jnp
from jax import lax
from jax.experimental import pallas as pl
from jax.experimental.pallas import tpu as pltpu
from jax.sharding import PartitionSpec as P

F32, S32, S16, BF16 = jnp.float32, jnp.int32, jnp.int16, jnp.bfloat16
NO = 32
OCC = NO * NO
HALF = OCC // 2
CHUNKS = 2
CW = OCC // CHUNKS
LANES = 128
SIDE = 4
PAD = 16
LOG_GRID = 200.0
FULL = 32760.0
TINY = 1e-37
VMEM = 28 * 1024 * 1024
SMALL = 16 * 1024 * 1024


def pair_orders():
    first, mates = [], []
    for gap in range(1, NO // 2 + 1):
        for i in range(NO if gap < NO // 2 else NO // 2):
            j = (i + gap) % NO
            first.append(i * NO + j)
            mates.append(j * NO + i)
    first += [i * NO + i for i in range(NO // 2)]
    mates += [i * NO + i for i in range(NO // 2, NO)]
    return np.array(first, np.int32), np.array(mates, np.int32)


def column_scale(level):
    return jnp.ceil(jnp.log(jnp.maximum(level, TINY)) * (LOG_GRID / float(np.log(2.0))))


def encode(values, scale):
    return jnp.round(values * (jnp.exp2(scale * (-1.0 / LOG_GRID)) * FULL)).astype(S32).astype(S16)


def decode(coded, scale):
    return coded.astype(S32).astype(F32) * (jnp.exp2(scale * (1.0 / LOG_GRID)) * (1.0 / FULL))


def pack(out_ref, values, far):
    rows = values.shape[0]
    scale = column_scale(jnp.max(jnp.abs(values), axis=0, keepdims=True))
    out_ref[pl.ds(0, rows), :] = encode(values, scale)
    heads = jnp.broadcast_to(scale, (PAD, LANES))
    if far is None:
        out_ref[pl.ds(rows, PAD), :] = heads.astype(S32).astype(S16)
        return
    far_scale = column_scale(jnp.max(jnp.abs(far), axis=0, keepdims=True))
    out_ref[pl.ds(rows, PAD), :] = encode(far, far_scale)
    which = lax.broadcasted_iota(S32, (PAD, LANES), 0)
    heads = jnp.where(which == 0, heads, jnp.broadcast_to(far_scale, (PAD, LANES)))
    out_ref[pl.ds(rows + PAD, PAD), :] = heads.astype(S32).astype(S16)


def unpack_sum(refs, rows, has_far):
    total, far = None, None
    for ref in refs:
        heads = ref[pl.ds(rows + (PAD if has_far else 0), PAD), :].astype(S32).astype(F32)
        part = decode(ref[pl.ds(0, rows), :], heads[0:1])
        total = part if total is None else total + part
        if has_far:
            part = decode(ref[pl.ds(rows, PAD), :], heads[1:2])
            far = part if far is None else far + part
    return total, far


def halves(values):
    high = values.astype(BF16)
    return high, (values - high.astype(F32)).astype(BF16)


def sort_rows(matrix, values):
    high, low = halves(values)
    return jnp.dot(matrix, high, preferred_element_type=F32) + jnp.dot(matrix, low, preferred_element_type=F32)


def stage_kernel(order_ref, live_ref, tiles_ref, out_ref, arrived):
    def copy(p):
        return pltpu.make_async_copy(tiles_ref.at[order_ref[p]], out_ref.at[p], arrived.at[p])

    for p in range(tiles_ref.shape[0]):

        @pl.when(live_ref[p] > 0)
        def _():
            copy(p).start()

    for p in range(tiles_ref.shape[0]):

        @pl.when(live_ref[p] <= 0)
        def _():
            out_ref[p] = jnp.zeros(out_ref.shape[1:], out_ref.dtype)

    for p in range(tiles_ref.shape[0]):

        @pl.when(live_ref[p] > 0)
        def _():
            copy(p).wait()


def stage(tiles, order, live):
    smem = pl.BlockSpec(memory_space=pltpu.SMEM)
    tiles = pltpu.with_memory_space_constraint(tiles, pltpu.HBM)
    return pl.pallas_call(
        stage_kernel,
        out_shape=pltpu.VMEM(tiles.shape, tiles.dtype),
        in_specs=[smem, smem, pl.BlockSpec(memory_space=pl.ANY)],
        out_specs=pl.BlockSpec(memory_space=pltpu.VMEM),
        scratch_shapes=[pltpu.SemaphoreType.DMA((tiles.shape[0],))],
        compiler_params=pltpu.CompilerParams(vmem_limit_bytes=4 * 1024 * 1024),
        cost_estimate=pl.CostEstimate(flops=0, bytes_accessed=tiles.size * 2, transcendentals=0),
        name="stage",
    )(order, live, tiles)


def product_kernel(has_far, rows, place_ref, v_ref, rank_ref, *rest):
    amps, outs, (first, mates, table, raw) = rest[:2], rest[2:10], rest[10:]
    tiles, tile, _ = v_ref.shape
    steps = tiles // 4
    half = CW // 2
    groups = SIDE * SIDE
    peer = rows // groups

    y, core = place_ref[2], place_ref[3]
    depth = amps[0].shape[2]
    for k in range(SIDE):
        chip = lax.rem(y + SIDE - k, SIDE) * 2
        for c in range(2):
            at = (chip + (core if c == 0 else 1 - core)) * depth
            for j in range(4):
                table[pl.ds(pl.multiple_of(j * tile + at, depth), depth), :] = amps[c][k, j]

    def multiply(step, part):
        total = None
        for j in range(4):
            v = v_ref[step * 4 + j]
            t = table[j * tile : (j + 1) * tile, part * half : (part + 1) * half]
            add = jnp.dot(v, t, preferred_element_type=F32)
            total = add if total is None else total + add
        return total

    def sort(step, part, values):
        for b in range(tile // rows):
            block = step * (tile // rows) + b
            rank = rank_ref[part, pl.ds(block, 1), :]
            matrix = (lax.broadcasted_iota(S32, (rows, rows), 0) == rank).astype(F32).astype(BF16)
            done = sort_rows(matrix, values[b * rows : (b + 1) * rows])
            if part == 0:
                first[pl.ds(pl.multiple_of(block * rows, rows), rows), :] = done
            else:
                mates[pl.ds(block, 1)] = done.reshape(1, groups, peer, half)

    def columns(part):
        return pl.ds(part * half, half)

    for part in range(2):
        raw[pl.ds(0, tile), columns(part)] = multiply(0, part)

    def turn(step, carry):
        before = pl.multiple_of(lax.rem(step + 1, 2) * tile, tile)
        now = pl.multiple_of(lax.rem(step, 2) * tile, tile)
        held = [raw[pl.ds(before, tile), columns(part)] for part in range(2)]
        for part in range(2):
            total = multiply(step, part)
            sort(step - 1, part, held[part])
            raw[pl.ds(now, tile), columns(part)] = total
        return carry

    lax.fori_loop(1, steps, turn, 0)
    for part in range(2):
        sort(steps - 1, part, raw[pl.ds((steps - 1) % 2 * tile, tile), columns(part)])

    z, x = place_ref[0], place_ref[1]
    for kx in range(SIDE):
        for kz in range(SIDE):
            zt = lax.rem(z + kz, SIDE)
            xt = lax.rem(x + kx, SIDE)
            owner_id = zt * SIDE + xt
            base = pl.multiple_of(owner_id * rows, rows)
            far_parts = [None, None]
            sums = []
            for side in range(2):
                mine = first[pl.ds(base, rows), pl.ds(side * LANES, LANES)]
                other = mates[:, pl.ds(owner_id, 1), :, pl.ds(side * LANES, LANES)].reshape(rows, LANES)
                if has_far and side == 1:
                    far = other.T[LANES - NO // 2 :]
                    far_parts = [far[:, :LANES], far[:, LANES:]]
                    lane = lax.broadcasted_iota(S32, (rows, LANES), 1)
                    other = jnp.where(lane < LANES - NO // 2, other, 0.0)
                sums.append(mine + other)
            pack(outs[kx].at[zt], sums[0], far_parts[0])
            pack(outs[4 + kz].at[xt], sums[1], far_parts[1])


def packed_rows(rows, has_far):
    return rows + PAD * (2 if has_far else 1)


def product(integrals, amps, ranks, place, rows, has_far):
    tiles, tile, _ = integrals.shape
    groups = SIDE * SIDE
    half = CW // 2
    vmem, smem = pl.BlockSpec(memory_space=pltpu.VMEM), pl.BlockSpec(memory_space=pltpu.SMEM)
    out = (SIDE, packed_rows(rows, has_far), LANES)
    return pl.pallas_call(
        functools.partial(product_kernel, has_far, rows),
        out_shape=[jax.ShapeDtypeStruct(out, S16)] * 8,
        in_specs=[smem] + [vmem] * (2 + len(amps)),
        out_specs=[vmem] * 8,
        scratch_shapes=[
            pltpu.VMEM((groups * rows, half), F32),
            pltpu.VMEM((groups, groups, rows // groups, half), F32),
            pltpu.VMEM((4 * tile, CW), BF16),
            pltpu.VMEM((2 * tile, CW), F32),
        ],
        compiler_params=pltpu.CompilerParams(vmem_limit_bytes=VMEM),
        cost_estimate=pl.CostEstimate(
            flops=2 * tiles * tile * tile * CW, bytes_accessed=4 * tile * CW * 4, transcendentals=0
        ),
        name="product",
    )(place, integrals, ranks, *amps)


def chunk_rows(rows, far_flags):
    heights = [packed_rows(rows, flag) for flag in far_flags]
    return [(sum(heights[:c]), heights[c]) for c in range(len(heights))]


def relay_kernel(rows, far_flags, place_ref, *refs):
    count = 8 * len(far_flags)
    ins, outs = refs[:count], refs[count:]
    for c, (top, height) in enumerate(chunk_rows(rows, far_flags)):
        for side in range(2):
            for k in range(SIDE):
                at = lax.rem(place_ref[side] + k, SIDE)
                blocks = [r.at[at] for r in ins[c * 8 + side * 4 :][:4]]
                total, far = unpack_sum(blocks, rows, far_flags[c])
                pack(outs[side * 4 + k].at[pl.ds(top, height)], total, far)


def relay(pieces, place, rows, far_flags):
    height = sum(h for _, h in chunk_rows(rows, far_flags))
    vmem = pl.BlockSpec(memory_space=pltpu.VMEM)
    return pl.pallas_call(
        functools.partial(relay_kernel, rows, far_flags),
        out_shape=[jax.ShapeDtypeStruct((height, LANES), S16)] * 8,
        in_specs=[pl.BlockSpec(memory_space=pltpu.SMEM)] + [vmem] * len(pieces),
        out_specs=[vmem] * 8,
        compiler_params=pltpu.CompilerParams(vmem_limit_bytes=SMALL),
        name="relay",
    )(place, *pieces)


def owner_kernel(rows, far_flags, *refs):
    ins, own, send = refs[:8], refs[8], refs[9]
    for c, (top, height) in enumerate(chunk_rows(rows, far_flags)):
        has_far = far_flags[c]
        fars = []
        for side in range(2):
            blocks = [r.at[pl.ds(top, height)] for r in ins[side * 4 :][:4]]
            total, far = unpack_sum(blocks, rows, has_far)
            own[:, pl.ds((c * 2 + side) * LANES, LANES)] = total
            fars.append(far)
        if has_far:
            far = jnp.concatenate([jnp.zeros((LANES - NO // 2, rows), F32), jnp.concatenate(fars, axis=1)], axis=0)
            own[:, pl.ds(HALF, LANES)] = far.T
    scale = column_scale(jnp.max(jnp.abs(own[...]), axis=1, keepdims=True))
    send[:, pl.ds(0, HALF)] = encode(own[:, pl.ds(0, HALF)], scale)
    lane = lax.broadcasted_iota(S32, (rows, LANES), 1)
    far = jnp.round(own[:, pl.ds(HALF, LANES)] * (jnp.exp2(scale * (-1.0 / LOG_GRID)) * FULL))
    far = jnp.where(lane == 0, jnp.broadcast_to(scale, (rows, LANES)), far)
    send[:, pl.ds(HALF, LANES)] = far.astype(S32).astype(S16)


def owner(pieces, rows, far_flags):
    vmem = pl.BlockSpec(memory_space=pltpu.VMEM)
    width = HALF + LANES
    return pl.pallas_call(
        functools.partial(owner_kernel, rows, far_flags),
        out_shape=[jax.ShapeDtypeStruct((rows, width), F32), jax.ShapeDtypeStruct((rows, width), S16)],
        in_specs=[vmem] * len(pieces),
        out_specs=[vmem] * 2,
        compiler_params=pltpu.CompilerParams(vmem_limit_bytes=SMALL),
        name="owner",
    )(*pieces)


def close_kernel(rows, own, came, ranks, energy, pair_sum, spread, out, joined):
    heads = came[:, pl.ds(HALF, LANES)].astype(S32).astype(F32)
    scale = jnp.exp2(heads[:, 0:1] * (1.0 / LOG_GRID)) * (1.0 / FULL)
    plain = came[...].astype(S32).astype(F32) * scale
    slot = lax.broadcasted_iota(S32, (rows, rows), 1)
    back = [(slot == ranks[:, k : k + 1]).astype(F32).astype(BF16) for k in range(2)]
    mine = sort_rows(back[0], own[...])
    other = sort_rows(back[1], plain)
    lane = lax.broadcasted_iota(S32, (rows, LANES), 1)
    off_diagonal = lane < LANES - NO // 2
    edge = HALF - LANES
    joined[:, pl.ds(0, edge)] = mine[:, :edge]
    joined[:, pl.ds(HALF, edge)] = other[:, :edge]
    last_mine, last_other = mine[:, edge:HALF], other[:, edge:HALF]
    joined[:, pl.ds(edge, LANES)] = last_mine + jnp.where(off_diagonal, 0.0, last_other)
    joined[:, pl.ds(HALF + edge, LANES)] = jnp.where(off_diagonal, last_other, mine[:, HALF:] + other[:, HALF:])
    total = None
    for part in halves(joined[...]):
        add = jnp.dot(part, spread[...], preferred_element_type=F32)
        total = add if total is None else total + add
    out[...] = total / (energy[...] - pair_sum[...])


def close(own, came, ranks, energy, pair_sum, spread, rows):
    vmem = pl.BlockSpec(memory_space=pltpu.VMEM)
    return pl.pallas_call(
        functools.partial(close_kernel, rows),
        out_shape=jax.ShapeDtypeStruct((rows, OCC), F32),
        in_specs=[vmem] * 6,
        out_specs=vmem,
        scratch_shapes=[pltpu.VMEM((rows, OCC), F32)],
        compiler_params=pltpu.CompilerParams(vmem_limit_bytes=SMALL),
        name="close",
    )(own, came, ranks, energy, pair_sum, spread)


def shifted(dz, dx):
    return [
        (z * SIDE + x, (z + dz) % SIDE * SIDE + (x + dx) % SIDE) for z in range(SIDE) for x in range(SIDE)
    ]


def spread_out(pieces, across_x_first):
    got = list(pieces)
    for k in (2, 1, 3):
        for side in range(2):
            along_x = (side == 0) == across_x_first
            perm = shifted(0, k) if along_x else shifted(k, 0)
            got[side * 4 + k] = lax.ppermute(pieces[side * 4 + k], "col", perm)
    return got


def shifted_rows(dy, dcore):
    return [(y * 2 + c, (y + dy) % SIDE * 2 + (c + dcore) % 2) for y in range(SIDE) for c in range(2)]


def fetch_along(part):
    return [part] + [lax.ppermute(part, "row", shifted_rows(k, 0)) for k in range(1, SIDE)]


def share(along):
    mine = jnp.stack(along)
    return [mine, lax.ppermute(mine, "row", shifted_rows(0, 1))]


def body(integrals, tile_count, tile_list, amplitudes, pair_energy, occ_energy, partner):
    rows = partner.shape[0]
    groups = SIDE * SIDE
    first, mates_of = pair_orders()
    half = CW // 2
    column_order = np.concatenate(
        [np.concatenate([first[c * half :][:half], mates_of[c * half :][:half]]) for c in range(CHUNKS)]
    )
    pair_ids = jnp.arange(OCC, dtype=S32)
    sort = (pair_ids[:, None] == jnp.asarray(column_order)[None, :]).astype(BF16)
    spread = (jnp.asarray(np.concatenate([first, mates_of]))[:, None] == pair_ids[None, :]).astype(BF16)

    blocks, depth, _ = amplitudes.shape
    sorted_amp = jnp.dot(amplitudes.reshape(blocks * depth, OCC), sort, preferred_element_type=F32).astype(BF16)
    parts = [sorted_amp[:, c * CW : (c + 1) * CW].reshape(blocks, depth, CW) for c in range(CHUNKS)]

    peer = rows // groups
    target = partner // rows % groups
    key_local = partner % rows
    row_ids = jnp.arange(rows, dtype=S32)
    same_target = target[:, None] == target[None, :]
    own_rank = target * peer + jnp.sum(same_target & (row_ids[None, :] < row_ids[:, None]), axis=1)
    mate_rank = target * peer + jnp.sum(same_target & (key_local[None, :] < key_local[:, None]), axis=1)
    both = jnp.concatenate([own_rank, mate_rank]).astype(S32)
    spoken = jnp.broadcast_to(both[None, :], (groups, 2 * rows))
    ranks = lax.all_to_all(spoken, "col", split_axis=0, concat_axis=0, tiled=True)
    along = [fetch_along(part) for part in parts]
    ranks, along[0] = lax.optimization_barrier((ranks, along[0]))
    ranks = jnp.stack([ranks[:, :rows], ranks[:, rows:]])

    col = lax.axis_index("col")
    row = lax.axis_index("row")
    place = jnp.stack([col // SIDE, col % SIDE, row // 2, row % 2]).astype(S32)
    slots = tile_list[0, 0]
    slot_ids = jnp.arange(slots.shape[0], dtype=S32)
    order = jnp.sum(jnp.where(slots[None, :] == slot_ids[:, None], slot_ids[None, :], 0), axis=1)
    live = (order < tile_count[0, 0]).astype(S32)

    tiles = stage(integrals[0, 0], order, live)
    far_flags = tuple(c == CHUNKS - 1 for c in range(CHUNKS))
    landed = []
    for c in range(CHUNKS):
        sent = product(tiles, share(along[c]), ranks, place, rows, far_flags[c])
        if c + 1 < CHUNKS:
            sent, along[c + 1] = lax.optimization_barrier((sent, along[c + 1]))
        landed += spread_out(sent, True)
    landed = spread_out(relay(landed, place, rows, far_flags), False)
    own, send = owner(landed, rows, far_flags)
    came = lax.all_to_all(send, "col", split_axis=0, concat_axis=0, tiled=True)
    pair_sum = (occ_energy[:, None] + occ_energy[None, :]).reshape(1, OCC)
    back = jnp.stack([own_rank, mate_rank], axis=1).astype(S32)
    return close(own, came, back, pair_energy[:, None], pair_sum, spread, rows)


def solution(mesh):
    return jax.shard_map(
        body,
        mesh=mesh,
        in_specs=(
            P("row", "col", None, None, None),
            P("row", "col"),
            P("row", "col", None),
            P("col", "row", None),
            P(("row", "col")),
            P(),
            P(("row", "col")),
        ),
        out_specs=P(("row", "col"), None),
        check_vma=False,
    )
```

time: 197 us -> 140 us (0.71)
  Pallas kernels: 81.7 us -> 38.3 us
  blocking collectives: 0 us -> 15.3 us
  starting transfers between devices: 55.9 us -> 40.6 us
  between operations: 14.4 us -> 0.91 us
  waiting for transfers between devices: 32.1 us -> 36.9 us
  other arithmetic: 5.33 us -> 2.2 us
    pallas_call x2, Pallas kernels: 66.1 us -> 29.3 us  [product(): pl.pallas_call(functools.partial(product_kernel, has_far, rows), out_shap...]
    ppermute x24 -> x18, waiting for transfers between devices: 9.86 us -> 28.6 us  [spread_out(): got[side * 4 + k] = lax.ppermute(pieces[side * 4 + k], 'col', perm)]
    ppermute x24 -> x18, starting transfers between devices: 40.9 us -> 25.3 us  [spread_out(): got[side * 4 + k] = lax.ppermute(pieces[side * 4 + k], 'col', perm)]
    all_to_all x0 -> x1, blocking collectives: none -> 15.3 us  [body(): lax.all_to_all(spoken, 'col', split_axis=0, concat_axis=0, tiled=True)]
    ppermute x0 -> x8, starting transfers between devices: none -> 10.4 us  [the longest x6 9.49 us: fetch_along(): lax.ppermute(part, 'row', shifted_rows(k, 0))]
    all_gather x2 -> x0, waiting for transfers between devices: 10.3 us -> none  [body(): gathered.append(lax.all_gather(part, 'row', axis=0))]
    all_to_all x1 -> x0, starting transfers between devices: 7.96 us -> none  [body(): lax.all_to_all(jnp.broadcast_to(partner[None, :], (col_count, rows)), 'co...]
    all_to_all x1 -> x0, waiting for transfers between devices: 5.59 us -> none  [body(): lax.all_to_all(jnp.broadcast_to(partner[None, :], (col_count, rows)), 'co...]
  transfers between devices with their start and end apart: 28 -> 27, of which waited for: 9 -> 11; matrix products, arithmetic and copies ran while one was open for 4% -> 1% of each run, Pallas kernels for 37% -> 23%
where the time goes in v2:
time: 140 us; the launch traced here: 139 us
  starting transfers between devices  40.6 us (29%)
  Pallas kernels  38.3 us (27%)
  waiting for transfers between devices  36.9 us (26%)
  blocking collectives  15.3 us (11%)
  local copies, waits for them, and re-layouts  3.39 us (2%)
  other arithmetic  2.2 us (2%)
  matrix products  1.58 us (1%)
    pallas_call x2, Pallas kernels, product(): pl.pallas_call(functools.partial(product_kernel, has_far, rows), out_shap...  29.3 us
    ppermute x18, waiting for transfers between devices, spread_out(): got[side * 4 + k] = lax.ppermute(pieces[side * 4 + k], 'col', perm)  28.6 us
    ppermute x18, starting transfers between devices, spread_out(): got[side * 4 + k] = lax.ppermute(pieces[side * 4 + k], 'col', perm)  25.3 us
    all_to_all x1, blocking collectives, body(): lax.all_to_all(spoken, 'col', split_axis=0, concat_axis=0, tiled=True)  15.3 us
    ppermute x6, starting transfers between devices, fetch_along(): lax.ppermute(part, 'row', shifted_rows(k, 0))  9.49 us
    all_to_all x1, waiting for transfers between devices, body(): came = lax.all_to_all(send, 'col', split_axis=0, concat_axis=0, tiled=True)  8.25 us
    all_to_all x1, starting transfers between devices, body(): came = lax.all_to_all(send, 'col', split_axis=0, concat_axis=0, tiled=True)  4.9 us
    pallas_call x1, Pallas kernels, stage(): pl.pallas_call(stage_kernel, out_shape=pltpu.VMEM(tiles.shape, tiles.dtyp...  3.16 us
  transfers between devices with their start and end apart: 27, of which 11 were waited for; matrix products, arithmetic and copies ran while one was open for 1% of the time, Pallas kernels for 23%

profile of v2, /device:TPU:0, one launch (start us, length us, event | category | flops | bytes accessed | tf_op | source)
XLA Modules:
  0.0 139.1 jit_solution(14454572840673002677)
XLA Ops:
  0.0 1.0 copy-done
  1.0 1.6 %fusion.4 = bf16[256,1024]{1,0:T(8,128)(2,1)S(1)} fusion(bf16[256,1024]{1,0:T(8,128)(2,1)S(1)} %bitcast.34, s32[1024]{0:T(1024)} %constant.93.clone), kind=kOutput, calls=%fused_computation.6 | convolution fusion | flops 538181632 | bytes 1052672 | tf_op jit(solution)/shard_map/dot_general | solution.py:376
  2.7 1.7 %collective-permute-start = (bf16[4,64,512]{2,1,0:T(8,128)(2,1)S(1)}, bf16[4,64,512]{2,1,0:T(8,128)(2,1)S(1)}, u32[]{:S(2)}, u32[]{:S(2)}) collective-permute-start(bf16[4,64,512]{2,1,0:T(8,128)(2,1)S(1)} %bitcast.41), channel_id=1, source_target_pairs={{0,32},{16,48},{32,64},{48,80},{64,96},{80,112},{96,0},{112,16},{1... | collective-permute-start | bytes 786440 | tf_op jit(solution)/shard_map/ppermute | solution.py:355
  4.4 2.9 %collective-permute-start.1 = (bf16[4,64,512]{2,1,0:T(8,128)(2,1)S(1)}, bf16[4,64,512]{2,1,0:T(8,128)(2,1)S(1)}, u32[]{:S(2)}, u32[]{:S(2)}) collective-permute-start(bf16[4,64,512]{2,1,0:T(8,128)(2,1)S(1)} %bitcast.42), channel_id=1, source_target_pairs={{0,64},{16,80},{32,96},{48,112},{64,0},{80,16},{96,32},{112,48},{1... | collective-permute-start | bytes 786440 | tf_op jit(solution)/shard_map/ppermute | solution.py:355
  7.3 1.3 collective-permute-start.2
  8.7 0.3 convert_reduce_fusion.1
  9.0 15.3 %all_to_all.20 = s32[16,1,512]{2,1,0:T(1,128)S(1)} all-to-all(s32[16,1,512]{2,1,0:T(1,128)S(1)} %broadcast_in_dim.14), channel_id=1, replica_groups=mesh['row'=8,'col'=16] {'col'}, dimensions={0} | all-to-all | bytes 65536 | tf_op jit(solution)/shard_map/all_to_all | solution.py:388
  24.3 0.1 pad_maximum_fusion.rest_0_
  24.5 0.7 collective-permute-start.4
  25.3 0.8 collective-permute-start.5
  26.1 2.0 %collective-permute-start.6 = (bf16[4,64,512]{2,1,0:T(8,128)(2,1)S(1)}, bf16[4,64,512]{2,1,0:T(8,128)(2,1)}, u32[]{:S(2)}, u32[]{:S(2)}) collective-permute-start(bf16[4,64,512]{2,1,0:T(8,128)(2,1)S(1)} %bitcast.39), channel_id=1, source_target_pairs={{0,96},{16,112},{32,0},{48,16},{64,32},{80,48},{96,64},{112,80},{1... | collective-permute-start | bytes 786440 | tf_op jit(solution)/shard_map/ppermute | solution.py:355
  28.8 3.2 %stage.1.v_ref = bf16[32,512,512]{2,1,0:T(8,128)(2,1)S(1)} custom-call(s32[32]{0:T(128)S(1)} %select_reduce_fusion.order_ref, s32[32]{0:T(128)S(1)} %compare_convert_fusion.live_ref, bf16[32,512,512]{2,1,0:T(8,128)(2,1)} %bitcast.36), custom_call_target="tpu_custom_call" | custom-call | bytes 16777216 | tf_op jit(solution)/shard_map/stage/pallas_call | solution.py:114
  32.1 14.5 %product.2 = (s16[4,272,128]{2,1,0:T(8,128)(2,1)S(1)}, s16[4,272,128]{2,1,0:T(8,128)(2,1)S(1)}, s16[4,272,128]{2,1,0:T(8,128)(2,1)S(1)}, s16[4,272,128]{2,1,0:T(...) custom-call(s32[4]{0:T(128)S(1)} %pad_add_fusion.3.place_ref, ...), custom_call_target="tpu_custom_call" | custom-call | flops 8589934592 | bytes 4194304 | tf_op jit(solution)/shard_map/product/pallas_call | solution.py:215
  46.7 1.1 pad_maximum_fusion.1.rest_0_
  47.8 0.8 collective-permute-start.13
  48.5 1.0 collective-permute-start.7
  49.6 3.4 %collective-permute-start.8 = (s16[4,272,128]{2,1,0:T(8,128)(2,1)S(1)}, s16[4,272,128]{2,1,0:T(8,128)(2,1)S(1)}, u32[]{:S(2)}, u32[]{:S(2)}) collective-permute-start(s16[4,272,128]{2,1,0:T(8,128)(2,1)S(1)} %get-tuple-element.63), channel_id=1, source_target_pairs={{0,2},{1,3},{2,0},{3,1},{4,6},{5,7},{6,4},{7,5},{8,10},{9,11},{10,... | collective-permute-start | bytes 835592 | tf_op jit(solution)/shard_map/ppermute | solution.py:346
  53.0 14.8 %product.3 = (s16[4,288,128]{2,1,0:T(8,128)(2,1)S(1)}, s16[4,288,128]{2,1,0:T(8,128)(2,1)S(1)}, s16[4,288,128]{2,1,0:T(8,128)(2,1)S(1)}, s16[4,288,128]{2,1,0:T(...) custom-call(s32[4]{0:T(128)S(1)} %pad_add_fusion.3.place_ref, ...), custom_call_target="tpu_custom_call" | custom-call | flops 8589934592 | bytes 4194304 | tf_op jit(solution)/shard_map/product/pallas_call | solution.py:215
  67.9 3.2 %collective-permute-start.9 = (s16[4,272,128]{2,1,0:T(8,128)(2,1)S(1)}, s16[4,272,128]{2,1,0:T(8,128)(2,1)S(1)}, u32[]{:S(2)}, u32[]{:S(2)}) collective-permute-start(s16[4,272,128]{2,1,0:T(8,128)(2,1)S(1)} %get-tuple-element.64), channel_id=1, source_target_pairs={{0,3},{1,0},{2,1},{3,2},{4,7},{5,4},{6,5},{7,6},{8,11},{9,8},{10,9... | collective-permute-start | bytes 835592 | tf_op jit(solution)/shard_map/ppermute | solution.py:346
  71.1 0.7 collective-permute-start.10
  71.8 2.8 %collective-permute-start.11 = (s16[4,272,128]{2,1,0:T(8,128)(2,1)S(1)}, s16[4,272,128]{2,1,0:T(8,128)(2,1)S(1)}, u32[]{:S(2)}, u32[]{:S(2)}) collective-permute-start(s16[4,272,128]{2,1,0:T(8,128)(2,1)S(1)} %get-tuple-element.67), channel_id=1, source_target_pairs={{0,8},{1,9},{2,10},{3,11},{4,12},{5,13},{6,14},{7,15},{8,0},{9,1},... | collective-permute-start | bytes 835592 | tf_op jit(solution)/shard_map/ppermute | solution.py:346
  74.6 0.1 collective-permute-start.12
  74.7 1.7 %collective-permute-done.9.refs_3_ = s16[4,272,128]{2,1,0:T(8,128)(2,1)S(1)} collective-permute-done((s16[4,272,128]{2,1,0:T(8,128)(2,1)S(1)}, s16[4,272,128]{2,1,0:T(8,128)(2,1)S(1)}, u32[]{:S(2)}, u32[]{:S(2)}) %collective-permute-start.9) | collective-permute-done | bytes 278560 | tf_op jit(solution)/shard_map/ppermute | solution.py:346
  76.4 2.4 %collective-permute-start.15 = (s16[4,288,128]{2,1,0:T(8,128)(2,1)S(1)}, s16[4,288,128]{2,1,0:T(8,128)(2,1)S(1)}, u32[]{:S(2)}, u32[]{:S(2)}) collective-permute-start(s16[4,288,128]{2,1,0:T(8,128)(2,1)S(1)} %get-tuple-element.75), channel_id=1, source_target_pairs={{0,2},{1,3},{2,0},{3,1},{4,6},{5,7},{6,4},{7,5},{8,10},{9,11},{10,... | collective-permute-start | bytes 884744 | tf_op jit(solution)/shard_map/ppermute | solution.py:346
  78.8 1.6 %collective-permute-done.10.refs_5_ = s16[4,272,128]{2,1,0:T(8,128)(2,1)S(1)} collective-permute-done((s16[4,272,128]{2,1,0:T(8,128)(2,1)S(1)}, s16[4,272,128]{2,1,0:T(8,128)(2,1)S(1)}, u32[]{:S(2)}, u32[]{:S(2)}) %collective-permute-start.10) | collective-permute-done | bytes 278560 | tf_op jit(solution)/shard_map/ppermute | solution.py:346
  80.4 0.3 collective-permute-start.16
  80.7 5.9 %collective-permute-done.11.refs_6_ = s16[4,272,128]{2,1,0:T(8,128)(2,1)S(1)} collective-permute-done((s16[4,272,128]{2,1,0:T(8,128)(2,1)S(1)}, s16[4,272,128]{2,1,0:T(8,128)(2,1)S(1)}, u32[]{:S(2)}, u32[]{:S(2)}) %collective-permute-start.11) | collective-permute-done | bytes 278560 | tf_op jit(solution)/shard_map/ppermute | solution.py:346
  86.7 1.6 %collective-permute-start.18 = (s16[4,288,128]{2,1,0:T(8,128)(2,1)S(1)}, s16[4,288,128]{2,1,0:T(8,128)(2,1)S(1)}, u32[]{:S(2)}, u32[]{:S(2)}) collective-permute-start(s16[4,288,128]{2,1,0:T(8,128)(2,1)S(1)} %get-tuple-element.79), channel_id=1, source_target_pairs={{0,8},{1,9},{2,10},{3,11},{4,12},{5,13},{6,14},{7,15},{8,0},{9,1},... | collective-permute-start | bytes 884744 | tf_op jit(solution)/shard_map/ppermute | solution.py:346
  88.3 2.0 %collective-permute-start.19 = (s16[4,288,128]{2,1,0:T(8,128)(2,1)S(1)}, s16[4,288,128]{2,1,0:T(8,128)(2,1)S(1)}, u32[]{:S(2)}, u32[]{:S(2)}) collective-permute-start(s16[4,288,128]{2,1,0:T(8,128)(2,1)S(1)} %get-tuple-element.80), channel_id=1, source_target_pairs={{0,12},{1,13},{2,14},{3,15},{4,0},{5,1},{6,2},{7,3},{8,4},{9,5},{1... | collective-permute-start | bytes 884744 | tf_op jit(solution)/shard_map/ppermute | solution.py:346
  90.3 2.2 %collective-permute-done.16.refs_11_ = s16[4,288,128]{2,1,0:T(8,128)(2,1)S(1)} collective-permute-done((s16[4,288,128]{2,1,0:T(8,128)(2,1)S(1)}, s16[4,288,128]{2,1,0:T(8,128)(2,1)S(1)}, u32[]{:S(2)}, u32[]{:S(2)}) %collective-permute-start.16) | collective-permute-done | bytes 294944 | tf_op jit(solution)/shard_map/ppermute | solution.py:346
  92.5 9.2 %collective-permute-done.17.refs_13_ = s16[4,288,128]{2,1,0:T(8,128)(2,1)S(1)} collective-permute-done((s16[4,288,128]{2,1,0:T(8,128)(2,1)S(1)}, s16[4,288,128]{2,1,0:T(8,128)(2,1)S(1)}, u32[]{:S(2)}, u32[]{:S(2)}) %collective-permute-start.17) | collective-permute-done | bytes 294944 | tf_op jit(solution)/shard_map/ppermute | solution.py:346
  101.8 1.4 %collective-permute-done.19.refs_15_ = s16[4,288,128]{2,1,0:T(8,128)(2,1)S(1)} collective-permute-done((s16[4,288,128]{2,1,0:T(8,128)(2,1)S(1)}, s16[4,288,128]{2,1,0:T(8,128)(2,1)S(1)}, u32[]{:S(2)}, u32[]{:S(2)}) %collective-permute-start.19) | collective-permute-done | bytes 294944 | tf_op jit(solution)/shard_map/ppermute | solution.py:346
  103.2 2.0 %relay.1 = (s16[560,128]{1,0:T(8,128)(2,1)S(1)}, s16[560,128]{1,0:T(8,128)(2,1)S(1)}, s16[560,128]{1,0:T(8,128)(2,1)S(1)}, s16[560,128]{1,0:T(8,128)(2,1)S(1)}, ...) custom-call(s32[4]{0:T(128)S(1)} %pad_add_fusion.3.place_ref, ...), custom_call_target="tpu_custom_call" | custom-call | tf_op jit(solution)/shard_map/relay/pallas_call | solution.py:254
  105.2 1.2 collective-permute-start.20
  106.4 2.9 %collective-permute-start.21 = (s16[560,128]{1,0:T(8,128)(2,1)S(1)}, s16[560,128]{1,0:T(8,128)(2,1)S(1)}, u32[]{:S(2)}, u32[]{:S(2)}) collective-permute-start(s16[560,128]{1,0:T(8,128)(2,1)S(1)} %get-tuple-element.83), channel_id=1, source_target_pairs={{0,8},{1,9},{2,10},{3,11},{4,12},{5,13},{6,14},{7,15},{8,0},{9,1},... | collective-permute-start | bytes 430088 | tf_op jit(solution)/shard_map/ppermute | solution.py:346
  109.3 0.4 collective-permute-start.22
  109.8 1.9 %collective-permute-start.24 = (s16[560,128]{1,0:T(8,128)(2,1)S(1)}, s16[560,128]{1,0:T(8,128)(2,1)S(1)}, u32[]{:S(2)}, u32[]{:S(2)}) collective-permute-start(s16[560,128]{1,0:T(8,128)(2,1)S(1)} %get-tuple-element.87), channel_id=1, source_target_pairs={{0,2},{1,3},{2,0},{3,1},{4,6},{5,7},{6,4},{7,5},{8,10},{9,11},{10,... | collective-permute-start | bytes 430088 | tf_op jit(solution)/shard_map/ppermute | solution.py:346
  111.8 1.1 collective-permute-start.25
  113.0 3.0 %collective-permute-done.21.refs_2_ = s16[560,128]{1,0:T(8,128)(2,1)S(1)} collective-permute-done((s16[560,128]{1,0:T(8,128)(2,1)S(1)}, s16[560,128]{1,0:T(8,128)(2,1)S(1)}, u32[]{:S(2)}, u32[]{:S(2)}) %collective-permute-start.21) | collective-permute-done | bytes 143392 | tf_op jit(solution)/shard_map/ppermute | solution.py:346
  116.1 2.7 %collective-permute-done.23.refs_5_ = s16[560,128]{1,0:T(8,128)(2,1)S(1)} collective-permute-done((s16[560,128]{1,0:T(8,128)(2,1)S(1)}, s16[560,128]{1,0:T(8,128)(2,1)S(1)}, u32[]{:S(2)}, u32[]{:S(2)}) %collective-permute-start.23) | collective-permute-done | bytes 143392 | tf_op jit(solution)/shard_map/ppermute | solution.py:346
  118.7 0.6 collective-permute-done.25.refs_7_
  119.4 1.1 owner.1
  120.5 0.8 copy-done.1
  121.3 4.9 %all-to-all-start.1 = ((s16[16,16,640]{2,1,0:T(8,128)(2,1)}), s16[16,16,640]{2,1,0:T(8,128)(2,1)S(1)}, u32[]{:S(2)}, u32[]{:S(2)}) async-start(s16[16,16,640]{2,1,0:T(8,128)(2,1)} %bitcast.21), calls=%async_computation.1 | async-start | bytes 655360 | tf_op jit(solution)/shard_map/all_to_all | solution.py:411
  126.6 0.4 fusion.1.spread
  127.1 8.3 %all-to-all-done.1 = s16[16,16,640]{2,1,0:T(8,128)(2,1)S(1)} async-done(((s16[16,16,640]{2,1,0:T(8,128)(2,1)}), s16[16,16,640]{2,1,0:T(8,128)(2,1)S(1)}, u32[]{:S(2)}, u32[]{:S(2)}) %all-to-all-start.1) | async-done | bytes 327712 | tf_op jit(solution)/shard_map/all_to_all | solution.py:411
  135.3 1.1 copy-done.2
  136.4 2.7 %close.1 = f32[256,1024]{1,0:T(8,128)} custom-call(f32[256,640]{1,0:T(8,128)S(1)} %copy-done.2, s16[256,640]{1,0:T(8,128)(2,1)S(1)} %bitcast.35, s32[256,2]{1,0:T(8,128)S(1)} %copy.15.ranks, f32[256,1]{1,0:T(8,128)S(1)} %copy.16.energy, f32[1,1024]{1,0:T(1,128)S(1)} %add.58.pair_sum, bf16[1024,1024]{1,0:T(8,128)(2,1)S(1)} %fusion.1.spread), custom_call_target="tpu_custom_call" | custom-call | tf_op jit(solution)/shard_map/close/pallas_call | solution.py:323
  (50 shorter events, 1.2 us)
Async XLA Ops:
  0.0 1.0 copy-start
  0.0 8.7 %copy-start.6 = (s32[256]{0:T(256)S(1)}, s32[256]{0:T(256)}, u32[]{:S(2)}) copy-start(s32[256]{0:T(256)} %param.15) | copy-start | bytes 3076
  0.0 28.7 %copy-start.7 = (s32[1,1,32]{2,1,0:T(1,128)S(1)}, s32[1,1,32]{2,1,0:T(1,128)}, u32[]{:S(2)}) copy-start(s32[1,1,32]{2,1,0:T(1,128)} %param.11) | copy-start | bytes 388
  2.7 21.6 %collective-permute-start = (bf16[4,64,512]{2,1,0:T(8,128)(2,1)S(1)}, bf16[4,64,512]{2,1,0:T(8,128)(2,1)S(1)}, u32[]{:S(2)}, u32[]{:S(2)}) collective-permute-start(bf16[4,64,512]{2,1,0:T(8,128)(2,1)S(1)} %bitcast.41), channel_id=1, source_target_pairs={{0,32},{16,48},{32,64},{48,80},{64,96},{80,112},{96,0},{112,16},{1... | collective-permute-start | bytes 786440 | tf_op jit(solution)/shard_map/ppermute | solution.py:355
  4.4 19.9 %collective-permute-start.1 = (bf16[4,64,512]{2,1,0:T(8,128)(2,1)S(1)}, bf16[4,64,512]{2,1,0:T(8,128)(2,1)S(1)}, u32[]{:S(2)}, u32[]{:S(2)}) collective-permute-start(bf16[4,64,512]{2,1,0:T(8,128)(2,1)S(1)} %bitcast.42), channel_id=1, source_target_pairs={{0,64},{16,80},{32,96},{48,112},{64,0},{80,16},{96,32},{112,48},{1... | collective-permute-start | bytes 786440 | tf_op jit(solution)/shard_map/ppermute | solution.py:355
  7.3 17.0 %collective-permute-start.2 = (bf16[4,64,512]{2,1,0:T(8,128)(2,1)S(1)}, bf16[4,64,512]{2,1,0:T(8,128)(2,1)S(1)}, u32[]{:S(2)}, u32[]{:S(2)}) collective-permute-start(bf16[4,64,512]{2,1,0:T(8,128)(2,1)S(1)} %bitcast.43), channel_id=1, source_target_pairs={{0,96},{16,112},{32,0},{48,16},{64,32},{80,48},{96,64},{112,80},{1... | collective-permute-start | bytes 786440 | tf_op jit(solution)/shard_map/ppermute | solution.py:355
  24.4 7.7 %collective-permute-start.3 = (bf16[4,4,64,512]{3,2,1,0:T(8,128)(2,1)S(1)}, bf16[4,4,64,512]{3,2,1,0:T(8,128)(2,1)S(1)}, u32[]{:S(2)}, u32[]{:S(2)}) collective-permute-start(bf16[4,4,64,512]{3,2,1,0:T(8,128)(2,1)S(1)} %pad_maximum_fusion.rest_0_), channel_id=1, source_target_pairs={{0,16},{16,0},{32,48},{48,32},{64,80},{80,64},{96,112},{112,96},{1... | collective-permute-start | bytes 3145736 | tf_op jit(solution)/shard_map/ppermute | solution.py:360
  24.5 22.1 %collective-permute-start.4 = (bf16[4,64,512]{2,1,0:T(8,128)(2,1)S(1)}, bf16[4,64,512]{2,1,0:T(8,128)(2,1)S(1)}, u32[]{:S(2)}, u32[]{:S(2)}) collective-permute-start(bf16[4,64,512]{2,1,0:T(8,128)(2,1)S(1)} %bitcast.37), channel_id=1, source_target_pairs={{0,32},{16,48},{32,64},{48,80},{64,96},{80,112},{96,0},{112,16},{1... | collective-permute-start | bytes 786440 | tf_op jit(solution)/shard_map/ppermute | solution.py:355
  25.3 21.4 %collective-permute-start.5 = (bf16[4,64,512]{2,1,0:T(8,128)(2,1)S(1)}, bf16[4,64,512]{2,1,0:T(8,128)(2,1)S(1)}, u32[]{:S(2)}, u32[]{:S(2)}) collective-permute-start(bf16[4,64,512]{2,1,0:T(8,128)(2,1)S(1)} %bitcast.38), channel_id=1, source_target_pairs={{0,64},{16,80},{32,96},{48,112},{64,0},{80,16},{96,32},{112,48},{1... | collective-permute-start | bytes 786440 | tf_op jit(solution)/shard_map/ppermute | solution.py:355
  26.1 20.6 %collective-permute-start.6 = (bf16[4,64,512]{2,1,0:T(8,128)(2,1)S(1)}, bf16[4,64,512]{2,1,0:T(8,128)(2,1)}, u32[]{:S(2)}, u32[]{:S(2)}) collective-permute-start(bf16[4,64,512]{2,1,0:T(8,128)(2,1)S(1)} %bitcast.39), channel_id=1, source_target_pairs={{0,96},{16,112},{32,0},{48,16},{64,32},{80,48},{96,64},{112,80},{1... | collective-permute-start | bytes 786440 | tf_op jit(solution)/shard_map/ppermute | solution.py:355
  47.8 5.2 %collective-permute-start.13 = (bf16[4,4,64,512]{3,2,1,0:T(8,128)(2,1)S(1)}, bf16[4,4,64,512]{3,2,1,0:T(8,128)(2,1)S(1)}, u32[]{:S(2)}, u32[]{:S(2)}) collective-permute-start(bf16[4,4,64,512]{3,2,1,0:T(8,128)(2,1)S(1)} %pad_maximum_fusion.1.rest_0_), channel_id=1, source_target_pairs={{0,16},{16,0},{32,48},{48,32},{64,80},{80,64},{96,112},{112,96},{1... | collective-permute-start | bytes 3145736 | tf_op jit(solution)/shard_map/ppermute | solution.py:360
  48.5 23.2 %collective-permute-start.7 = (s16[4,272,128]{2,1,0:T(8,128)(2,1)S(1)}, s16[4,272,128]{2,1,0:T(8,128)(2,1)S(1)}, u32[]{:S(2)}, u32[]{:S(2)}) collective-permute-start(s16[4,272,128]{2,1,0:T(8,128)(2,1)S(1)} %get-tuple-element.62), channel_id=1, source_target_pairs={{0,1},{1,2},{2,3},{3,0},{4,5},{5,6},{6,7},{7,4},{8,9},{9,10},{10,1... | collective-permute-start | bytes 835592 | tf_op jit(solution)/shard_map/ppermute | solution.py:346
  49.6 25.0 %collective-permute-start.8 = (s16[4,272,128]{2,1,0:T(8,128)(2,1)S(1)}, s16[4,272,128]{2,1,0:T(8,128)(2,1)S(1)}, u32[]{:S(2)}, u32[]{:S(2)}) collective-permute-start(s16[4,272,128]{2,1,0:T(8,128)(2,1)S(1)} %get-tuple-element.63), channel_id=1, source_target_pairs={{0,2},{1,3},{2,0},{3,1},{4,6},{5,7},{6,4},{7,5},{8,10},{9,11},{10,... | collective-permute-start | bytes 835592 | tf_op jit(solution)/shard_map/ppermute | solution.py:346
  67.8 45.2 %copy-start.4 = (f32[32]{0:T(128)S(1)}, f32[32]{0:T(128)}, u32[]{:S(2)}) copy-start(f32[32]{0:T(128)} %param.14) | copy-start | bytes 388
  67.8 58.6 %copy-start.5 = (f32[256]{0:T(256)S(1)}, f32[256]{0:T(256)}, u32[]{:S(2)}) copy-start(f32[256]{0:T(256)} %param.13) | copy-start | bytes 3076
  67.8 58.8 %copy-start.3 = (s32[1024]{0:T(1024)S(1)}, s32[1024]{0:T(1024)}, u32[]{:S(2)}) copy-start(s32[1024]{0:T(1024)} %constant.94.clone) | copy-start | bytes 12292
  67.8 20.5 %collective-permute-start.14 = (s16[4,288,128]{2,1,0:T(8,128)(2,1)S(1)}, s16[4,288,128]{2,1,0:T(8,128)(2,1)S(1)}, u32[]{:S(2)}, u32[]{:S(2)}) collective-permute-start(s16[4,288,128]{2,1,0:T(8,128)(2,1)S(1)} %get-tuple-element.74), channel_id=1, source_target_pairs={{0,1},{1,2},{2,3},{3,0},{4,5},{5,6},{6,7},{7,4},{8,9},{9,10},{10,1... | collective-permute-start | bytes 884744 | tf_op jit(solution)/shard_map/ppermute | solution.py:346
  67.9 8.5 %collective-permute-start.9 = (s16[4,272,128]{2,1,0:T(8,128)(2,1)S(1)}, s16[4,272,128]{2,1,0:T(8,128)(2,1)S(1)}, u32[]{:S(2)}, u32[]{:S(2)}) collective-permute-start(s16[4,272,128]{2,1,0:T(8,128)(2,1)S(1)} %get-tuple-element.64), channel_id=1, source_target_pairs={{0,3},{1,0},{2,1},{3,2},{4,7},{5,4},{6,5},{7,6},{8,11},{9,8},{10,9... | collective-permute-start | bytes 835592 | tf_op jit(solution)/shard_map/ppermute | solution.py:346
  71.1 9.3 %collective-permute-start.10 = (s16[4,272,128]{2,1,0:T(8,128)(2,1)S(1)}, s16[4,272,128]{2,1,0:T(8,128)(2,1)S(1)}, u32[]{:S(2)}, u32[]{:S(2)}) collective-permute-start(s16[4,272,128]{2,1,0:T(8,128)(2,1)S(1)} %get-tuple-element.66), channel_id=1, source_target_pairs={{0,4},{1,5},{2,6},{3,7},{4,8},{5,9},{6,10},{7,11},{8,12},{9,13},{1... | collective-permute-start | bytes 835592 | tf_op jit(solution)/shard_map/ppermute | solution.py:346
  71.8 14.9 %collective-permute-start.11 = (s16[4,272,128]{2,1,0:T(8,128)(2,1)S(1)}, s16[4,272,128]{2,1,0:T(8,128)(2,1)S(1)}, u32[]{:S(2)}, u32[]{:S(2)}) collective-permute-start(s16[4,272,128]{2,1,0:T(8,128)(2,1)S(1)} %get-tuple-element.67), channel_id=1, source_target_pairs={{0,8},{1,9},{2,10},{3,11},{4,12},{5,13},{6,14},{7,15},{8,0},{9,1},... | collective-permute-start | bytes 835592 | tf_op jit(solution)/shard_map/ppermute | solution.py:346
  74.6 12.1 %collective-permute-start.12 = (s16[4,272,128]{2,1,0:T(8,128)(2,1)S(1)}, s16[4,272,128]{2,1,0:T(8,128)(2,1)S(1)}, u32[]{:S(2)}, u32[]{:S(2)}) collective-permute-start(s16[4,272,128]{2,1,0:T(8,128)(2,1)S(1)} %get-tuple-element.68), channel_id=1, source_target_pairs={{0,12},{1,13},{2,14},{3,15},{4,0},{5,1},{6,2},{7,3},{8,4},{9,5},{1... | collective-permute-start | bytes 835592 | tf_op jit(solution)/shard_map/ppermute | solution.py:346
  76.4 13.9 %collective-permute-start.15 = (s16[4,288,128]{2,1,0:T(8,128)(2,1)S(1)}, s16[4,288,128]{2,1,0:T(8,128)(2,1)S(1)}, u32[]{:S(2)}, u32[]{:S(2)}) collective-permute-start(s16[4,288,128]{2,1,0:T(8,128)(2,1)S(1)} %get-tuple-element.75), channel_id=1, source_target_pairs={{0,2},{1,3},{2,0},{3,1},{4,6},{5,7},{6,4},{7,5},{8,10},{9,11},{10,... | collective-permute-start | bytes 884744 | tf_op jit(solution)/shard_map/ppermute | solution.py:346
  80.4 12.1 %collective-permute-start.16 = (s16[4,288,128]{2,1,0:T(8,128)(2,1)S(1)}, s16[4,288,128]{2,1,0:T(8,128)(2,1)S(1)}, u32[]{:S(2)}, u32[]{:S(2)}) collective-permute-start(s16[4,288,128]{2,1,0:T(8,128)(2,1)S(1)} %get-tuple-element.76), channel_id=1, source_target_pairs={{0,3},{1,0},{2,1},{3,2},{4,7},{5,4},{6,5},{7,6},{8,11},{9,8},{10,9... | collective-permute-start | bytes 884744 | tf_op jit(solution)/shard_map/ppermute | solution.py:346
  86.6 15.1 %collective-permute-start.17 = (s16[4,288,128]{2,1,0:T(8,128)(2,1)S(1)}, s16[4,288,128]{2,1,0:T(8,128)(2,1)S(1)}, u32[]{:S(2)}, u32[]{:S(2)}) collective-permute-start(s16[4,288,128]{2,1,0:T(8,128)(2,1)S(1)} %get-tuple-element.78), channel_id=1, source_target_pairs={{0,4},{1,5},{2,6},{3,7},{4,8},{5,9},{6,10},{7,11},{8,12},{9,13},{1... | collective-permute-start | bytes 884744 | tf_op jit(solution)/shard_map/ppermute | solution.py:346
  86.7 15.1 %collective-permute-start.18 = (s16[4,288,128]{2,1,0:T(8,128)(2,1)S(1)}, s16[4,288,128]{2,1,0:T(8,128)(2,1)S(1)}, u32[]{:S(2)}, u32[]{:S(2)}) collective-permute-start(s16[4,288,128]{2,1,0:T(8,128)(2,1)S(1)} %get-tuple-element.79), channel_id=1, source_target_pairs={{0,8},{1,9},{2,10},{3,11},{4,12},{5,13},{6,14},{7,15},{8,0},{9,1},... | collective-permute-start | bytes 884744 | tf_op jit(solution)/shard_map/ppermute | solution.py:346
  88.3 14.9 %collective-permute-start.19 = (s16[4,288,128]{2,1,0:T(8,128)(2,1)S(1)}, s16[4,288,128]{2,1,0:T(8,128)(2,1)S(1)}, u32[]{:S(2)}, u32[]{:S(2)}) collective-permute-start(s16[4,288,128]{2,1,0:T(8,128)(2,1)S(1)} %get-tuple-element.80), channel_id=1, source_target_pairs={{0,12},{1,13},{2,14},{3,15},{4,0},{5,1},{6,2},{7,3},{8,4},{9,5},{1... | collective-permute-start | bytes 884744 | tf_op jit(solution)/shard_map/ppermute | solution.py:346
  105.2 6.6 %collective-permute-start.20 = (s16[560,128]{1,0:T(8,128)(2,1)S(1)}, s16[560,128]{1,0:T(8,128)(2,1)S(1)}, u32[]{:S(2)}, u32[]{:S(2)}) collective-permute-start(s16[560,128]{1,0:T(8,128)(2,1)S(1)} %get-tuple-element.82), channel_id=1, source_target_pairs={{0,4},{1,5},{2,6},{3,7},{4,8},{5,9},{6,10},{7,11},{8,12},{9,13},{1... | collective-permute-start | bytes 430088 | tf_op jit(solution)/shard_map/ppermute | solution.py:346
  106.4 9.6 %collective-permute-start.21 = (s16[560,128]{1,0:T(8,128)(2,1)S(1)}, s16[560,128]{1,0:T(8,128)(2,1)S(1)}, u32[]{:S(2)}, u32[]{:S(2)}) collective-permute-start(s16[560,128]{1,0:T(8,128)(2,1)S(1)} %get-tuple-element.83), channel_id=1, source_target_pairs={{0,8},{1,9},{2,10},{3,11},{4,12},{5,13},{6,14},{7,15},{8,0},{9,1},... | collective-permute-start | bytes 430088 | tf_op jit(solution)/shard_map/ppermute | solution.py:346
  109.3 6.7 %collective-permute-start.22 = (s16[560,128]{1,0:T(8,128)(2,1)S(1)}, s16[560,128]{1,0:T(8,128)(2,1)S(1)}, u32[]{:S(2)}, u32[]{:S(2)}) collective-permute-start(s16[560,128]{1,0:T(8,128)(2,1)S(1)} %get-tuple-element.84), channel_id=1, source_target_pairs={{0,12},{1,13},{2,14},{3,15},{4,0},{5,1},{6,2},{7,3},{8,4},{9,5},{1... | collective-permute-start | bytes 430088 | tf_op jit(solution)/shard_map/ppermute | solution.py:346
  109.7 9.0 %collective-permute-start.23 = (s16[560,128]{1,0:T(8,128)(2,1)S(1)}, s16[560,128]{1,0:T(8,128)(2,1)S(1)}, u32[]{:S(2)}, u32[]{:S(2)}) collective-permute-start(s16[560,128]{1,0:T(8,128)(2,1)S(1)} %get-tuple-element.86), channel_id=1, source_target_pairs={{0,1},{1,2},{2,3},{3,0},{4,5},{5,6},{6,7},{7,4},{8,9},{9,10},{10,1... | collective-permute-start | bytes 430088 | tf_op jit(solution)/shard_map/ppermute | solution.py:346
  109.8 8.9 %collective-permute-start.24 = (s16[560,128]{1,0:T(8,128)(2,1)S(1)}, s16[560,128]{1,0:T(8,128)(2,1)S(1)}, u32[]{:S(2)}, u32[]{:S(2)}) collective-permute-start(s16[560,128]{1,0:T(8,128)(2,1)S(1)} %get-tuple-element.87), channel_id=1, source_target_pairs={{0,2},{1,3},{2,0},{3,1},{4,6},{5,7},{6,4},{7,5},{8,10},{9,11},{10,... | collective-permute-start | bytes 430088 | tf_op jit(solution)/shard_map/ppermute | solution.py:346
  111.8 7.6 %collective-permute-start.25 = (s16[560,128]{1,0:T(8,128)(2,1)S(1)}, s16[560,128]{1,0:T(8,128)(2,1)S(1)}, u32[]{:S(2)}, u32[]{:S(2)}) collective-permute-start(s16[560,128]{1,0:T(8,128)(2,1)S(1)} %get-tuple-element.88), channel_id=1, source_target_pairs={{0,3},{1,0},{2,1},{3,2},{4,7},{5,4},{6,5},{7,6},{8,11},{9,8},{10,9... | collective-permute-start | bytes 430088 | tf_op jit(solution)/shard_map/ppermute | solution.py:346
  120.5 0.8 copy-start.1
  121.3 14.0 %all-to-all-start.1 = ((s16[16,16,640]{2,1,0:T(8,128)(2,1)}), s16[16,16,640]{2,1,0:T(8,128)(2,1)S(1)}, u32[]{:S(2)}, u32[]{:S(2)}) async-start(s16[16,16,640]{2,1,0:T(8,128)(2,1)} %bitcast.21), calls=%async_computation.1 | async-start | bytes 655360 | tf_op jit(solution)/shard_map/all_to_all | solution.py:411
  135.3 1.1 copy-start.2

commit v3 on v2

--- a/solution.py
+++ b/solution.py
@@ -20,7 +20,7 @@
 LOG_GRID = 200.0
 FULL = 32760.0
 TINY = 1e-37
-VMEM = 28 * 1024 * 1024
+VMEM = 20 * 1024 * 1024
 SMALL = 16 * 1024 * 1024
 
 
@@ -131,7 +131,7 @@
     groups = SIDE * SIDE
     peer = rows // groups
 
-    y, core = place_ref[2], place_ref[3]
+    z, x, y, core = place_ref[0], place_ref[1], place_ref[2], place_ref[3]
     depth = amps[0].shape[2]
     for k in range(SIDE):
         chip = lax.rem(y + SIDE - k, SIDE) * 2
@@ -139,6 +139,9 @@
             at = (chip + (core if c == 0 else 1 - core)) * depth
             for j in range(4):
                 table[pl.ds(pl.multiple_of(j * tile + at, depth), depth), :] = amps[c][k, j]
+
+    def relative(block):
+        return lax.rem(z + SIDE - block // SIDE, SIDE) * SIDE + lax.rem(x + SIDE - lax.rem(block, SIDE), SIDE)
 
     def multiply(step, part):
         total = None
@@ -152,7 +155,7 @@
     def sort(step, part, values):
         for b in range(tile // rows):
             block = step * (tile // rows) + b
-            rank = rank_ref[part, pl.ds(block, 1), :]
+            rank = rank_ref[part, pl.ds(relative(block), 1), :]
             matrix = (lax.broadcasted_iota(S32, (rows, rows), 0) == rank).astype(F32).astype(BF16)
             done = sort_rows(matrix, values[b * rows : (b + 1) * rows])
             if part == 0:
@@ -180,7 +183,6 @@
     for part in range(2):
         sort(steps - 1, part, raw[pl.ds((steps - 1) % 2 * tile, tile), columns(part)])
 
-    z, x = place_ref[0], place_ref[1]
     for kx in range(SIDE):
         for kz in range(SIDE):
             zt = lax.rem(z + kz, SIDE)
@@ -384,11 +386,13 @@
     own_rank = target * peer + jnp.sum(same_target & (row_ids[None, :] < row_ids[:, None]), axis=1)
     mate_rank = target * peer + jnp.sum(same_target & (key_local[None, :] < key_local[:, None]), axis=1)
     both = jnp.concatenate([own_rank, mate_rank]).astype(S32)
-    spoken = jnp.broadcast_to(both[None, :], (groups, 2 * rows))
-    ranks = lax.all_to_all(spoken, "col", split_axis=0, concat_axis=0, tiled=True)
+    def fetch_across(part, step):
+        return jnp.concatenate([part] + [lax.ppermute(part, "col", step(k)) for k in range(1, SIDE)])
+
     along = [fetch_along(part) for part in parts]
+    ranks = fetch_across(both.reshape(1, 2, rows), lambda k: shifted(0, k))
     ranks, along[0] = lax.optimization_barrier((ranks, along[0]))
-    ranks = jnp.stack([ranks[:, :rows], ranks[:, rows:]])
+    ranks = jnp.swapaxes(fetch_across(ranks, lambda k: shifted(k, 0)), 0, 1)
 
     col = lax.axis_index("col")
     row = lax.axis_index("row")
@@ -403,6 +407,8 @@
     landed = []
     for c in range(CHUNKS):
         sent = product(tiles, share(along[c]), ranks, place, rows, far_flags[c])
+        if c > 0:
+            sent, landed = lax.optimization_barrier((sent, landed))
         if c + 1 < CHUNKS:
             sent, along[c + 1] = lax.optimization_barrier((sent, along[c + 1]))
         landed += spread_out(sent, True)

time: 140 us -> 145 us (1.036)
  blocking collectives: 15.3 us -> 0 us
  starting transfers between devices: 40.6 us -> 52 us
  waiting for transfers between devices: 36.9 us -> 44.6 us
  Pallas kernels: 38.3 us -> 40 us
    all_to_all x1 -> x0, blocking collectives: 15.3 us -> none  [body(): lax.all_to_all(spoken, 'col', split_axis=0, concat_axis=0, tiled=True)]
    ppermute x0 -> x6, starting transfers between devices: none -> 12.4 us  [fetch_across(): lax.ppermute(part, 'col', step(k))]
    ppermute x18, waiting for transfers between devices: 28.6 us -> 32.2 us  [spread_out(): got[side * 4 + k] = lax.ppermute(pieces[side * 4 + k], 'col', perm)]
    ppermute x18, starting transfers between devices: 25.3 us -> 22.5 us  [spread_out(): got[side * 4 + k] = lax.ppermute(pieces[side * 4 + k], 'col', perm)]
    ppermute x0 -> x6, waiting for transfers between devices: none -> 2.62 us  [fetch_across(): lax.ppermute(part, 'col', step(k))]
    ppermute x6, starting transfers between devices: 9.49 us -> 11.3 us  [fetch_along(): lax.ppermute(part, 'row', shifted_rows(k, 0))]
    ppermute x6, waiting for transfers between devices: 0.02 us -> 1.53 us  [fetch_along(): lax.ppermute(part, 'row', shifted_rows(k, 0))]
    pallas_call x1, Pallas kernels: 3.16 us -> 4.66 us  [stage(): pl.pallas_call(stage_kernel, out_shape=pltpu.VMEM(tiles.shape, tiles.dtyp...]
  transfers between devices with their start and end apart: 27 -> 33, of which waited for: 11 -> 14; matrix products, arithmetic and copies ran while one was open for 1% -> 1% of each run, Pallas kernels for 23% -> 24%
where the time goes in v3:
time: 145 us; the launch traced here: 144 us
  starting transfers between devices  52 us (36%)
  waiting for transfers between devices  44.6 us (31%)
  Pallas kernels  40 us (28%)
  local copies, waits for them, and re-layouts  3.37 us (2%)
  matrix products  1.58 us (1%)
    ppermute x18, waiting for transfers between devices, spread_out(): got[side * 4 + k] = lax.ppermute(pieces[side * 4 + k], 'col', perm)  32.2 us
    pallas_call x2, Pallas kernels, product(): pl.pallas_call(functools.partial(product_kernel, has_far, rows), out_shap...  29.6 us
    ppermute x18, starting transfers between devices, spread_out(): got[side * 4 + k] = lax.ppermute(pieces[side * 4 + k], 'col', perm)  22.5 us
    ppermute x6, starting transfers between devices, fetch_across(): lax.ppermute(part, 'col', step(k))  12.4 us
    ppermute x6, starting transfers between devices, fetch_along(): lax.ppermute(part, 'row', shifted_rows(k, 0))  11.3 us
    all_to_all x1, waiting for transfers between devices, body(): came = lax.all_to_all(send, 'col', split_axis=0, concat_axis=0, tiled=True)  8.23 us
    all_to_all x1, starting transfers between devices, body(): came = lax.all_to_all(send, 'col', split_axis=0, concat_axis=0, tiled=True)  5.64 us
    pallas_call x1, Pallas kernels, stage(): pl.pallas_call(stage_kernel, out_shape=pltpu.VMEM(tiles.shape, tiles.dtyp...  4.66 us
  transfers between devices with their start and end apart: 33, of which 14 were waited for; matrix products, arithmetic and copies ran while one was open for 1% of the time, Pallas kernels for 24%

profile of v3, /device:TPU:0, one launch (start us, length us, event | category | flops | bytes accessed | tf_op | source)
XLA Modules:
  0.0 143.8 jit_solution(2316778041707518929)
XLA Ops:
  0.0 1.0 copy-done
  1.0 1.6 %fusion.4 = bf16[256,1024]{1,0:T(8,128)(2,1)S(1)} fusion(bf16[256,1024]{1,0:T(8,128)(2,1)S(1)} %bitcast.30, s32[1024]{0:T(1024)} %constant.93.clone), kind=kOutput, calls=%fused_computation.6 | convolution fusion | flops 538181632 | bytes 1052672 | tf_op jit(solution)/shard_map/dot_general | solution.py:378
  2.7 1.7 %collective-permute-start.3 = (bf16[4,64,512]{2,1,0:T(8,128)(2,1)S(1)}, bf16[4,64,512]{2,1,0:T(8,128)(2,1)S(1)}, u32[]{:S(2)}, u32[]{:S(2)}) collective-permute-start(bf16[4,64,512]{2,1,0:T(8,128)(2,1)S(1)} %bitcast.37), channel_id=1, source_target_pairs={{0,32},{16,48},{32,64},{48,80},{64,96},{80,112},{96,0},{112,16},{1... | collective-permute-start | bytes 786440 | tf_op jit(solution)/shard_map/ppermute | solution.py:357
  4.4 2.9 %collective-permute-start.4 = (bf16[4,64,512]{2,1,0:T(8,128)(2,1)S(1)}, bf16[4,64,512]{2,1,0:T(8,128)(2,1)S(1)}, u32[]{:S(2)}, u32[]{:S(2)}) collective-permute-start(bf16[4,64,512]{2,1,0:T(8,128)(2,1)S(1)} %bitcast.38), channel_id=1, source_target_pairs={{0,64},{16,80},{32,96},{48,112},{64,0},{80,16},{96,32},{112,48},{1... | collective-permute-start | bytes 786440 | tf_op jit(solution)/shard_map/ppermute | solution.py:357
  7.3 1.3 collective-permute-start.5
  9.0 1.6 %collective-permute-start = (s32[1,2,256]{2,0,1:T(1,128)S(1)}, s32[1,2,256]{2,0,1:T(1,128)S(1)}, u32[]{:S(2)}, u32[]{:S(2)}) collective-permute-start(s32[1,2,256]{2,0,1:T(1,128)S(1)} %bitcast.49), channel_id=1, source_target_pairs={{0,1},{1,2},{2,3},{3,0},{4,5},{5,6},{6,7},{7,4},{8,9},{9,10},{10,1... | collective-permute-start | bytes 6152 | tf_op jit(solution)/shard_map/ppermute | solution.py:390
  10.5 2.7 %collective-permute-start.1 = (s32[1,2,256]{2,0,1:T(1,128)S(1)}, s32[1,2,256]{2,0,1:T(1,128)S(1)}, u32[]{:S(2)}, u32[]{:S(2)}) collective-permute-start(s32[1,2,256]{2,0,1:T(1,128)S(1)} %bitcast.50), channel_id=1, source_target_pairs={{0,2},{1,3},{2,0},{3,1},{4,6},{5,7},{6,4},{7,5},{8,10},{9,11},{10,... | collective-permute-start | bytes 6152 | tf_op jit(solution)/shard_map/ppermute | solution.py:390
  13.2 0.6 collective-permute-done
  13.8 1.5 %collective-permute-start.2 = (s32[1,2,256]{2,0,1:T(1,128)S(1)}, s32[1,2,256]{2,0,1:T(1,128)S(1)}, u32[]{:S(2)}, u32[]{:S(2)}) collective-permute-start(s32[1,2,256]{2,0,1:T(1,128)S(1)} %bitcast.51), channel_id=1, source_target_pairs={{0,3},{1,0},{2,1},{3,2},{4,7},{5,4},{6,5},{7,6},{8,11},{9,8},{10,9... | collective-permute-start | bytes 6152 | tf_op jit(solution)/shard_map/ppermute | solution.py:390
  15.6 1.8 %collective-permute-done.2 = s32[1,2,256]{2,0,1:T(1,128)S(1)} collective-permute-done((s32[1,2,256]{2,0,1:T(1,128)S(1)}, s32[1,2,256]{2,0,1:T(1,128)S(1)}, u32[]{:S(2)}, u32[]{:S(2)}) %collective-permute-start.2) | collective-permute-done | bytes 2080 | tf_op jit(solution)/shard_map/ppermute | solution.py:390
  17.4 1.5 %collective-permute-done.4 = bf16[4,64,512]{2,1,0:T(8,128)(2,1)S(1)} collective-permute-done((bf16[4,64,512]{2,1,0:T(8,128)(2,1)S(1)}, bf16[4,64,512]{2,1,0:T(8,128)(2,1)S(1)}, u32[]{:S(2)}, u32[]{:S(2)}) %collective-permute-start.4) | collective-permute-done | bytes 262176 | tf_op jit(solution)/shard_map/ppermute | solution.py:357
  19.2 1.3 collective-permute-start.10
  21.3 2.0 %collective-permute-start.6 = (s32[4,2,256]{2,0,1:T(4,128)S(1)}, s32[4,2,256]{2,0,1:T(4,128)S(1)}, u32[]{:S(2)}, u32[]{:S(2)}) collective-permute-start(s32[4,2,256]{2,0,1:T(4,128)S(1)} %pad_add_fusion), channel_id=1, source_target_pairs={{0,4},{1,5},{2,6},{3,7},{4,8},{5,9},{6,10},{7,11},{8,12},{9,13},{1... | collective-permute-start | bytes 24584 | tf_op jit(solution)/shard_map/ppermute | solution.py:390
  23.3 3.6 %collective-permute-start.7 = (s32[4,2,256]{2,0,1:T(4,128)S(1)}, s32[4,2,256]{2,0,1:T(4,128)S(1)}, u32[]{:S(2)}, u32[]{:S(2)}) collective-permute-start(s32[4,2,256]{2,0,1:T(4,128)S(1)} %pad_add_fusion), channel_id=1, source_target_pairs={{0,8},{1,9},{2,10},{3,11},{4,12},{5,13},{6,14},{7,15},{8,0},{9,1},... | collective-permute-start | bytes 24584 | tf_op jit(solution)/shard_map/ppermute | solution.py:390
  26.8 1.0 collective-permute-start.8
  27.9 4.7 %stage.1.v_ref = bf16[32,512,512]{2,1,0:T(8,128)(2,1)S(1)} custom-call(s32[32]{0:T(128)S(1)} %select_reduce_fusion.order_ref, s32[32]{0:T(128)S(1)} %compare_convert_fusion.live_ref, bf16[32,512,512]{2,1,0:T(8,128)(2,1)} %bitcast.32), custom_call_target="tpu_custom_call" | custom-call | bytes 16777216 | tf_op jit(solution)/shard_map/stage/pallas_call | solution.py:114
  32.6 0.6 collective-permute-start.11
  33.3 3.4 %collective-permute-start.12 = (bf16[4,64,512]{2,1,0:T(8,128)(2,1)S(1)}, bf16[4,64,512]{2,1,0:T(8,128)(2,1)S(1)}, u32[]{:S(2)}, u32[]{:S(2)}) collective-permute-start(bf16[4,64,512]{2,1,0:T(8,128)(2,1)S(1)} %bitcast.35), channel_id=1, source_target_pairs={{0,96},{16,112},{32,0},{48,16},{64,32},{80,48},{96,64},{112,80},{1... | collective-permute-start | bytes 786440 | tf_op jit(solution)/shard_map/ppermute | solution.py:357
  36.7 14.7 %product.2 = (s16[4,272,128]{2,1,0:T(8,128)(2,1)S(1)}, s16[4,272,128]{2,1,0:T(8,128)(2,1)S(1)}, s16[4,272,128]{2,1,0:T(8,128)(2,1)S(1)}, s16[4,272,128]{2,1,0:T(...) custom-call(s32[4]{0:T(128)S(1)} %pad_add_fusion.3.place_ref, ...), custom_call_target="tpu_custom_call" | custom-call | flops 8589934592 | bytes 4194304 | tf_op jit(solution)/shard_map/product/pallas_call | solution.py:217
  51.6 2.2 %collective-permute-start.14 = (s16[4,272,128]{2,1,0:T(8,128)(2,1)S(1)}, s16[4,272,128]{2,1,0:T(8,128)(2,1)S(1)}, u32[]{:S(2)}, u32[]{:S(2)}) collective-permute-start(s16[4,272,128]{2,1,0:T(8,128)(2,1)S(1)} %get-tuple-element.90), channel_id=1, source_target_pairs={{0,1},{1,2},{2,3},{3,0},{4,5},{5,6},{6,7},{7,4},{8,9},{9,10},{10,1... | collective-permute-start | bytes 835592 | tf_op jit(solution)/shard_map/ppermute | solution.py:348
  53.8 1.3 collective-permute-start.15
  55.1 2.1 %collective-permute-start.16 = (s16[4,272,128]{2,1,0:T(8,128)(2,1)S(1)}, s16[4,272,128]{2,1,0:T(8,128)(2,1)S(1)}, u32[]{:S(2)}, u32[]{:S(2)}) collective-permute-start(s16[4,272,128]{2,1,0:T(8,128)(2,1)S(1)} %get-tuple-element.92), channel_id=1, source_target_pairs={{0,3},{1,0},{2,1},{3,2},{4,7},{5,4},{6,5},{7,6},{8,11},{9,8},{10,9... | collective-permute-start | bytes 835592 | tf_op jit(solution)/shard_map/ppermute | solution.py:348
  57.2 0.6 collective-permute-start.17
  57.8 4.4 %collective-permute-done.14.refs_1_ = s16[4,272,128]{2,1,0:T(8,128)(2,1)S(1)} collective-permute-done((s16[4,272,128]{2,1,0:T(8,128)(2,1)S(1)}, s16[4,272,128]{2,1,0:T(8,128)(2,1)S(1)}, u32[]{:S(2)}, u32[]{:S(2)}) %collective-permute-start.14) | collective-permute-done | bytes 278560 | tf_op jit(solution)/shard_map/ppermute | solution.py:348
  62.2 6.5 %collective-permute-start.18 = (s16[4,272,128]{2,1,0:T(8,128)(2,1)S(1)}, s16[4,272,128]{2,1,0:T(8,128)(2,1)S(1)}, u32[]{:S(2)}, u32[]{:S(2)}) collective-permute-start(s16[4,272,128]{2,1,0:T(8,128)(2,1)S(1)} %get-tuple-element.95), channel_id=1, source_target_pairs={{0,8},{1,9},{2,10},{3,11},{4,12},{5,13},{6,14},{7,15},{8,0},{9,1},... | collective-permute-start | bytes 835592 | tf_op jit(solution)/shard_map/ppermute | solution.py:348
  68.7 14.9 %product.3 = (s16[4,288,128]{2,1,0:T(8,128)(2,1)S(1)}, s16[4,288,128]{2,1,0:T(8,128)(2,1)S(1)}, s16[4,288,128]{2,1,0:T(8,128)(2,1)S(1)}, s16[4,288,128]{2,1,0:T(...) custom-call(s32[4]{0:T(128)S(1)} %pad_add_fusion.3.place_ref, ...), custom_call_target="tpu_custom_call" | custom-call | flops 8589934592 | bytes 4194304 | tf_op jit(solution)/shard_map/product/pallas_call | solution.py:217
  83.8 1.1 collective-permute-start.21
  84.9 2.1 %collective-permute-start.22 = (s16[4,288,128]{2,1,0:T(8,128)(2,1)S(1)}, s16[4,288,128]{2,1,0:T(8,128)(2,1)S(1)}, u32[]{:S(2)}, u32[]{:S(2)}) collective-permute-start(s16[4,288,128]{2,1,0:T(8,128)(2,1)S(1)} %get-tuple-element.108), channel_id=1, source_target_pairs={{0,3},{1,0},{2,1},{3,2},{4,7},{5,4},{6,5},{7,6},{8,11},{9,8},{10,9... | collective-permute-start | bytes 884744 | tf_op jit(solution)/shard_map/ppermute | solution.py:348
  87.1 2.0 %collective-permute-start.23 = (s16[4,288,128]{2,1,0:T(8,128)(2,1)S(1)}, s16[4,288,128]{2,1,0:T(8,128)(2,1)S(1)}, u32[]{:S(2)}, u32[]{:S(2)}) collective-permute-start(s16[4,288,128]{2,1,0:T(8,128)(2,1)S(1)} %get-tuple-element.110), channel_id=1, source_target_pairs={{0,4},{1,5},{2,6},{3,7},{4,8},{5,9},{6,10},{7,11},{8,12},{9,13},{1... | collective-permute-start | bytes 884744 | tf_op jit(solution)/shard_map/ppermute | solution.py:348
  89.1 8.7 %collective-permute-done.20.refs_9_ = s16[4,288,128]{2,1,0:T(8,128)(2,1)S(1)} collective-permute-done((s16[4,288,128]{2,1,0:T(8,128)(2,1)S(1)}, s16[4,288,128]{2,1,0:T(8,128)(2,1)S(1)}, u32[]{:S(2)}, u32[]{:S(2)}) %collective-permute-start.20) | collective-permute-done | bytes 294944 | tf_op jit(solution)/shard_map/ppermute | solution.py:348
  97.8 0.6 collective-permute-start.25
  98.4 1.3 collective-permute-done.23.refs_13_
  99.6 7.7 %collective-permute-done.25.refs_15_ = s16[4,288,128]{2,1,0:T(8,128)(2,1)S(1)} collective-permute-done((s16[4,288,128]{2,1,0:T(8,128)(2,1)S(1)}, s16[4,288,128]{2,1,0:T(8,128)(2,1)S(1)}, u32[]{:S(2)}, u32[]{:S(2)}) %collective-permute-start.25) | collective-permute-done | bytes 294944 | tf_op jit(solution)/shard_map/ppermute | solution.py:348
  107.4 2.0 %relay.1 = (s16[560,128]{1,0:T(8,128)(2,1)S(1)}, s16[560,128]{1,0:T(8,128)(2,1)S(1)}, s16[560,128]{1,0:T(8,128)(2,1)S(1)}, s16[560,128]{1,0:T(8,128)(2,1)S(1)}, ...) custom-call(s32[4]{0:T(128)S(1)} %pad_add_fusion.3.place_ref, ...), custom_call_target="tpu_custom_call" | custom-call | tf_op jit(solution)/shard_map/relay/pallas_call | solution.py:256
  109.3 0.6 collective-permute-start.26
  110.0 2.9 %collective-permute-start.27 = (s16[560,128]{1,0:T(8,128)(2,1)S(1)}, s16[560,128]{1,0:T(8,128)(2,1)S(1)}, u32[]{:S(2)}, u32[]{:S(2)}) collective-permute-start(s16[560,128]{1,0:T(8,128)(2,1)S(1)} %get-tuple-element.115), channel_id=1, source_target_pairs={{0,8},{1,9},{2,10},{3,11},{4,12},{5,13},{6,14},{7,15},{8,0},{9,1},... | collective-permute-start | bytes 430088 | tf_op jit(solution)/shard_map/ppermute | solution.py:348
  112.9 2.8 %collective-permute-done.26.refs_1_ = s16[560,128]{1,0:T(8,128)(2,1)S(1)} collective-permute-done((s16[560,128]{1,0:T(8,128)(2,1)S(1)}, s16[560,128]{1,0:T(8,128)(2,1)S(1)}, u32[]{:S(2)}, u32[]{:S(2)}) %collective-permute-start.26) | collective-permute-done | bytes 143392 | tf_op jit(solution)/shard_map/ppermute | solution.py:348
  116.2 1.3 collective-permute-done.27.refs_2_
  117.5 0.7 collective-permute-done.28.refs_3_
  118.2 2.6 %collective-permute-done.29.refs_5_ = s16[560,128]{1,0:T(8,128)(2,1)S(1)} collective-permute-done((s16[560,128]{1,0:T(8,128)(2,1)S(1)}, s16[560,128]{1,0:T(8,128)(2,1)S(1)}, u32[]{:S(2)}, u32[]{:S(2)}) %collective-permute-start.29) | collective-permute-done | bytes 143392 | tf_op jit(solution)/shard_map/ppermute | solution.py:348
  120.7 2.7 %collective-permute-done.31.refs_7_ = s16[560,128]{1,0:T(8,128)(2,1)S(1)} collective-permute-done((s16[560,128]{1,0:T(8,128)(2,1)S(1)}, s16[560,128]{1,0:T(8,128)(2,1)S(1)}, u32[]{:S(2)}, u32[]{:S(2)}) %collective-permute-start.31) | collective-permute-done | bytes 143392 | tf_op jit(solution)/shard_map/ppermute | solution.py:348
  123.4 1.1 owner.1
  124.5 0.8 copy-done.1
  125.4 5.6 %all-to-all-start = ((s16[16,16,640]{2,1,0:T(8,128)(2,1)}), s16[16,16,640]{2,1,0:T(8,128)(2,1)S(1)}, u32[]{:S(2)}, u32[]{:S(2)}) async-start(s16[16,16,640]{2,1,0:T(8,128)(2,1)} %bitcast.21), calls=%async_computation | async-start | bytes 655360 | tf_op jit(solution)/shard_map/all_to_all | solution.py:417
  131.4 0.4 fusion.1.spread
  131.8 8.2 %all-to-all-done = s16[16,16,640]{2,1,0:T(8,128)(2,1)S(1)} async-done(((s16[16,16,640]{2,1,0:T(8,128)(2,1)}), s16[16,16,640]{2,1,0:T(8,128)(2,1)S(1)}, u32[]{:S(2)}, u32[]{:S(2)}) %all-to-all-start) | async-done | bytes 327712 | tf_op jit(solution)/shard_map/all_to_all | solution.py:417
  140.0 1.1 copy-done.2
  141.1 2.7 %close.1 = f32[256,1024]{1,0:T(8,128)} custom-call(f32[256,640]{1,0:T(8,128)S(1)} %copy-done.2, s16[256,640]{1,0:T(8,128)(2,1)S(1)} %bitcast.31, s32[256,2]{1,0:T(8,128)S(1)} %copy.15.ranks, f32[256,1]{1,0:T(8,128)S(1)} %copy.16.energy, f32[1,1024]{1,0:T(1,128)S(1)} %add.58.pair_sum, bf16[1024,1024]{1,0:T(8,128)(2,1)S(1)} %fusion.1.spread), custom_call_target="tpu_custom_call" | custom-call | tf_op jit(solution)/shard_map/close/pallas_call | solution.py:325
  (59 shorter events, 2.2 us)
Async XLA Ops:
  0.0 1.0 copy-start
  0.0 8.7 %copy-start.6 = (s32[256]{0:T(256)S(1)}, s32[256]{0:T(256)}, u32[]{:S(2)}) copy-start(s32[256]{0:T(256)} %param.15) | copy-start | bytes 3076
  0.0 21.1 %copy-start.7 = (s32[1,1,32]{2,1,0:T(1,128)S(1)}, s32[1,1,32]{2,1,0:T(1,128)}, u32[]{:S(2)}) copy-start(s32[1,1,32]{2,1,0:T(1,128)} %param.11) | copy-start | bytes 388
  2.7 14.7 %collective-permute-start.3 = (bf16[4,64,512]{2,1,0:T(8,128)(2,1)S(1)}, bf16[4,64,512]{2,1,0:T(8,128)(2,1)S(1)}, u32[]{:S(2)}, u32[]{:S(2)}) collective-permute-start(bf16[4,64,512]{2,1,0:T(8,128)(2,1)S(1)} %bitcast.37), channel_id=1, source_target_pairs={{0,32},{16,48},{32,64},{48,80},{64,96},{80,112},{96,0},{112,16},{1... | collective-permute-start | bytes 786440 | tf_op jit(solution)/shard_map/ppermute | solution.py:357
  4.4 14.5 %collective-permute-start.4 = (bf16[4,64,512]{2,1,0:T(8,128)(2,1)S(1)}, bf16[4,64,512]{2,1,0:T(8,128)(2,1)S(1)}, u32[]{:S(2)}, u32[]{:S(2)}) collective-permute-start(bf16[4,64,512]{2,1,0:T(8,128)(2,1)S(1)} %bitcast.38), channel_id=1, source_target_pairs={{0,64},{16,80},{32,96},{48,112},{64,0},{80,16},{96,32},{112,48},{1... | collective-permute-start | bytes 786440 | tf_op jit(solution)/shard_map/ppermute | solution.py:357
  7.3 11.6 %collective-permute-start.5 = (bf16[4,64,512]{2,1,0:T(8,128)(2,1)S(1)}, bf16[4,64,512]{2,1,0:T(8,128)(2,1)S(1)}, u32[]{:S(2)}, u32[]{:S(2)}) collective-permute-start(bf16[4,64,512]{2,1,0:T(8,128)(2,1)S(1)} %bitcast.39), channel_id=1, source_target_pairs={{0,96},{16,112},{32,0},{48,16},{64,32},{80,48},{96,64},{112,80},{1... | collective-permute-start | bytes 786440 | tf_op jit(solution)/shard_map/ppermute | solution.py:357
  9.0 4.9 %collective-permute-start = (s32[1,2,256]{2,0,1:T(1,128)S(1)}, s32[1,2,256]{2,0,1:T(1,128)S(1)}, u32[]{:S(2)}, u32[]{:S(2)}) collective-permute-start(s32[1,2,256]{2,0,1:T(1,128)S(1)} %bitcast.49), channel_id=1, source_target_pairs={{0,1},{1,2},{2,3},{3,0},{4,5},{5,6},{6,7},{7,4},{8,9},{9,10},{10,1... | collective-permute-start | bytes 6152 | tf_op jit(solution)/shard_map/ppermute | solution.py:390
  10.5 5.1 %collective-permute-start.1 = (s32[1,2,256]{2,0,1:T(1,128)S(1)}, s32[1,2,256]{2,0,1:T(1,128)S(1)}, u32[]{:S(2)}, u32[]{:S(2)}) collective-permute-start(s32[1,2,256]{2,0,1:T(1,128)S(1)} %bitcast.50), channel_id=1, source_target_pairs={{0,2},{1,3},{2,0},{3,1},{4,6},{5,7},{6,4},{7,5},{8,10},{9,11},{10,... | collective-permute-start | bytes 6152 | tf_op jit(solution)/shard_map/ppermute | solution.py:390
  13.8 3.6 %collective-permute-start.2 = (s32[1,2,256]{2,0,1:T(1,128)S(1)}, s32[1,2,256]{2,0,1:T(1,128)S(1)}, u32[]{:S(2)}, u32[]{:S(2)}) collective-permute-start(s32[1,2,256]{2,0,1:T(1,128)S(1)} %bitcast.51), channel_id=1, source_target_pairs={{0,3},{1,0},{2,1},{3,2},{4,7},{5,4},{6,5},{7,6},{8,11},{9,8},{10,9... | collective-permute-start | bytes 6152 | tf_op jit(solution)/shard_map/ppermute | solution.py:390
  19.1 17.6 %collective-permute-start.9 = (bf16[4,4,64,512]{3,2,1,0:T(8,128)(2,1)S(1)}, bf16[4,4,64,512]{3,2,1,0:T(8,128)(2,1)S(1)}, u32[]{:S(2)}, u32[]{:S(2)}) collective-permute-start(bf16[4,4,64,512]{3,2,1,0:T(8,128)(2,1)S(1)} %pad_maximum_fusion.rest_0_), channel_id=1, source_target_pairs={{0,16},{16,0},{32,48},{48,32},{64,80},{80,64},{96,112},{112,96},{1... | collective-permute-start | bytes 3145736 | tf_op jit(solution)/shard_map/ppermute | solution.py:362
  19.2 32.2 %collective-permute-start.10 = (bf16[4,64,512]{2,1,0:T(8,128)(2,1)S(1)}, bf16[4,64,512]{2,1,0:T(8,128)(2,1)S(1)}, u32[]{:S(2)}, u32[]{:S(2)}) collective-permute-start(bf16[4,64,512]{2,1,0:T(8,128)(2,1)S(1)} %bitcast.33), channel_id=1, source_target_pairs={{0,32},{16,48},{32,64},{48,80},{64,96},{80,112},{96,0},{112,16},{1... | collective-permute-start | bytes 786440 | tf_op jit(solution)/shard_map/ppermute | solution.py:357
  21.3 11.3 %collective-permute-start.6 = (s32[4,2,256]{2,0,1:T(4,128)S(1)}, s32[4,2,256]{2,0,1:T(4,128)S(1)}, u32[]{:S(2)}, u32[]{:S(2)}) collective-permute-start(s32[4,2,256]{2,0,1:T(4,128)S(1)} %pad_add_fusion), channel_id=1, source_target_pairs={{0,4},{1,5},{2,6},{3,7},{4,8},{5,9},{6,10},{7,11},{8,12},{9,13},{1... | collective-permute-start | bytes 24584 | tf_op jit(solution)/shard_map/ppermute | solution.py:390
  23.3 10.0 %collective-permute-start.7 = (s32[4,2,256]{2,0,1:T(4,128)S(1)}, s32[4,2,256]{2,0,1:T(4,128)S(1)}, u32[]{:S(2)}, u32[]{:S(2)}) collective-permute-start(s32[4,2,256]{2,0,1:T(4,128)S(1)} %pad_add_fusion), channel_id=1, source_target_pairs={{0,8},{1,9},{2,10},{3,11},{4,12},{5,13},{6,14},{7,15},{8,0},{9,1},... | collective-permute-start | bytes 24584 | tf_op jit(solution)/shard_map/ppermute | solution.py:390
  26.8 9.8 %collective-permute-start.8 = (s32[4,2,256]{2,0,1:T(4,128)S(1)}, s32[4,2,256]{2,0,1:T(4,128)S(1)}, u32[]{:S(2)}, u32[]{:S(2)}) collective-permute-start(s32[4,2,256]{2,0,1:T(4,128)S(1)} %pad_add_fusion), channel_id=1, source_target_pairs={{0,12},{1,13},{2,14},{3,15},{4,0},{5,1},{6,2},{7,3},{8,4},{9,5},{1... | collective-permute-start | bytes 24584 | tf_op jit(solution)/shard_map/ppermute | solution.py:390
  32.6 18.8 %collective-permute-start.11 = (bf16[4,64,512]{2,1,0:T(8,128)(2,1)S(1)}, bf16[4,64,512]{2,1,0:T(8,128)(2,1)S(1)}, u32[]{:S(2)}, u32[]{:S(2)}) collective-permute-start(bf16[4,64,512]{2,1,0:T(8,128)(2,1)S(1)} %bitcast.34), channel_id=1, source_target_pairs={{0,64},{16,80},{32,96},{48,112},{64,0},{80,16},{96,32},{112,48},{1... | collective-permute-start | bytes 786440 | tf_op jit(solution)/shard_map/ppermute | solution.py:357
  33.3 18.1 %collective-permute-start.12 = (bf16[4,64,512]{2,1,0:T(8,128)(2,1)S(1)}, bf16[4,64,512]{2,1,0:T(8,128)(2,1)S(1)}, u32[]{:S(2)}, u32[]{:S(2)}) collective-permute-start(bf16[4,64,512]{2,1,0:T(8,128)(2,1)S(1)} %bitcast.35), channel_id=1, source_target_pairs={{0,96},{16,112},{32,0},{48,16},{64,32},{80,48},{96,64},{112,80},{1... | collective-permute-start | bytes 786440 | tf_op jit(solution)/shard_map/ppermute | solution.py:357
  51.5 17.2 %collective-permute-start.13 = (bf16[4,4,64,512]{3,2,1,0:T(8,128)(2,1)S(1)}, bf16[4,4,64,512]{3,2,1,0:T(8,128)(2,1)S(1)}, u32[]{:S(2)}, u32[]{:S(2)}) collective-permute-start(bf16[4,4,64,512]{3,2,1,0:T(8,128)(2,1)S(1)} %pad_maximum_fusion.1.rest_0_), channel_id=1, source_target_pairs={{0,16},{16,0},{32,48},{48,32},{64,80},{80,64},{96,112},{112,96},{1... | collective-permute-start | bytes 3145736 | tf_op jit(solution)/shard_map/ppermute | solution.py:362
  51.6 10.6 %collective-permute-start.14 = (s16[4,272,128]{2,1,0:T(8,128)(2,1)S(1)}, s16[4,272,128]{2,1,0:T(8,128)(2,1)S(1)}, u32[]{:S(2)}, u32[]{:S(2)}) collective-permute-start(s16[4,272,128]{2,1,0:T(8,128)(2,1)S(1)} %get-tuple-element.90), channel_id=1, source_target_pairs={{0,1},{1,2},{2,3},{3,0},{4,5},{5,6},{6,7},{7,4},{8,9},{9,10},{10,1... | collective-permute-start | bytes 835592 | tf_op jit(solution)/shard_map/ppermute | solution.py:348
  53.8 29.9 %collective-permute-start.15 = (s16[4,272,128]{2,1,0:T(8,128)(2,1)S(1)}, s16[4,272,128]{2,1,0:T(8,128)(2,1)S(1)}, u32[]{:S(2)}, u32[]{:S(2)}) collective-permute-start(s16[4,272,128]{2,1,0:T(8,128)(2,1)S(1)} %get-tuple-element.91), channel_id=1, source_target_pairs={{0,2},{1,3},{2,0},{3,1},{4,6},{5,7},{6,4},{7,5},{8,10},{9,11},{10,... | collective-permute-start | bytes 835592 | tf_op jit(solution)/shard_map/ppermute | solution.py:348
  55.1 28.6 %collective-permute-start.16 = (s16[4,272,128]{2,1,0:T(8,128)(2,1)S(1)}, s16[4,272,128]{2,1,0:T(8,128)(2,1)S(1)}, u32[]{:S(2)}, u32[]{:S(2)}) collective-permute-start(s16[4,272,128]{2,1,0:T(8,128)(2,1)S(1)} %get-tuple-element.92), channel_id=1, source_target_pairs={{0,3},{1,0},{2,1},{3,2},{4,7},{5,4},{6,5},{7,6},{8,11},{9,8},{10,9... | collective-permute-start | bytes 835592 | tf_op jit(solution)/shard_map/ppermute | solution.py:348
  57.2 26.5 %collective-permute-start.17 = (s16[4,272,128]{2,1,0:T(8,128)(2,1)S(1)}, s16[4,272,128]{2,1,0:T(8,128)(2,1)S(1)}, u32[]{:S(2)}, u32[]{:S(2)}) collective-permute-start(s16[4,272,128]{2,1,0:T(8,128)(2,1)S(1)} %get-tuple-element.94), channel_id=1, source_target_pairs={{0,4},{1,5},{2,6},{3,7},{4,8},{5,9},{6,10},{7,11},{8,12},{9,13},{1... | collective-permute-start | bytes 835592 | tf_op jit(solution)/shard_map/ppermute | solution.py:348
  62.2 21.5 %collective-permute-start.18 = (s16[4,272,128]{2,1,0:T(8,128)(2,1)S(1)}, s16[4,272,128]{2,1,0:T(8,128)(2,1)S(1)}, u32[]{:S(2)}, u32[]{:S(2)}) collective-permute-start(s16[4,272,128]{2,1,0:T(8,128)(2,1)S(1)} %get-tuple-element.95), channel_id=1, source_target_pairs={{0,8},{1,9},{2,10},{3,11},{4,12},{5,13},{6,14},{7,15},{8,0},{9,1},... | collective-permute-start | bytes 835592 | tf_op jit(solution)/shard_map/ppermute | solution.py:348
  68.7 15.0 %collective-permute-start.19 = (s16[4,272,128]{2,1,0:T(8,128)(2,1)S(1)}, s16[4,272,128]{2,1,0:T(8,128)(2,1)S(1)}, u32[]{:S(2)}, u32[]{:S(2)}) collective-permute-start(s16[4,272,128]{2,1,0:T(8,128)(2,1)S(1)} %get-tuple-element.96), channel_id=1, source_target_pairs={{0,12},{1,13},{2,14},{3,15},{4,0},{5,1},{6,2},{7,3},{8,4},{9,5},{1... | collective-permute-start | bytes 835592 | tf_op jit(solution)/shard_map/ppermute | solution.py:348
  83.7 32.5 %copy-start.4 = (f32[32]{0:T(128)S(1)}, f32[32]{0:T(128)}, u32[]{:S(2)}) copy-start(f32[32]{0:T(128)} %param.14) | copy-start | bytes 388
  83.7 47.5 %copy-start.5 = (f32[256]{0:T(256)S(1)}, f32[256]{0:T(256)}, u32[]{:S(2)}) copy-start(f32[256]{0:T(256)} %param.13) | copy-start | bytes 3076
  83.7 47.7 %copy-start.3 = (s32[1024]{0:T(1024)S(1)}, s32[1024]{0:T(1024)}, u32[]{:S(2)}) copy-start(s32[1024]{0:T(1024)} %constant.94.clone) | copy-start | bytes 12292
  83.7 14.0 %collective-permute-start.20 = (s16[4,288,128]{2,1,0:T(8,128)(2,1)S(1)}, s16[4,288,128]{2,1,0:T(8,128)(2,1)S(1)}, u32[]{:S(2)}, u32[]{:S(2)}) collective-permute-start(s16[4,288,128]{2,1,0:T(8,128)(2,1)S(1)} %get-tuple-element.106), channel_id=1, source_target_pairs={{0,1},{1,2},{2,3},{3,0},{4,5},{5,6},{6,7},{7,4},{8,9},{9,10},{10,1... | collective-permute-start | bytes 884744 | tf_op jit(solution)/shard_map/ppermute | solution.py:348
  83.8 14.5 %collective-permute-start.21 = (s16[4,288,128]{2,1,0:T(8,128)(2,1)S(1)}, s16[4,288,128]{2,1,0:T(8,128)(2,1)S(1)}, u32[]{:S(2)}, u32[]{:S(2)}) collective-permute-start(s16[4,288,128]{2,1,0:T(8,128)(2,1)S(1)} %get-tuple-element.107), channel_id=1, source_target_pairs={{0,2},{1,3},{2,0},{3,1},{4,6},{5,7},{6,4},{7,5},{8,10},{9,11},{10,... | collective-permute-start | bytes 884744 | tf_op jit(solution)/shard_map/ppermute | solution.py:348
  84.9 13.4 %collective-permute-start.22 = (s16[4,288,128]{2,1,0:T(8,128)(2,1)S(1)}, s16[4,288,128]{2,1,0:T(8,128)(2,1)S(1)}, u32[]{:S(2)}, u32[]{:S(2)}) collective-permute-start(s16[4,288,128]{2,1,0:T(8,128)(2,1)S(1)} %get-tuple-element.108), channel_id=1, source_target_pairs={{0,3},{1,0},{2,1},{3,2},{4,7},{5,4},{6,5},{7,6},{8,11},{9,8},{10,9... | collective-permute-start | bytes 884744 | tf_op jit(solution)/shard_map/ppermute | solution.py:348
  87.1 12.6 %collective-permute-start.23 = (s16[4,288,128]{2,1,0:T(8,128)(2,1)S(1)}, s16[4,288,128]{2,1,0:T(8,128)(2,1)S(1)}, u32[]{:S(2)}, u32[]{:S(2)}) collective-permute-start(s16[4,288,128]{2,1,0:T(8,128)(2,1)S(1)} %get-tuple-element.110), channel_id=1, source_target_pairs={{0,4},{1,5},{2,6},{3,7},{4,8},{5,9},{6,10},{7,11},{8,12},{9,13},{1... | collective-permute-start | bytes 884744 | tf_op jit(solution)/shard_map/ppermute | solution.py:348
  89.1 10.6 %collective-permute-start.24 = (s16[4,288,128]{2,1,0:T(8,128)(2,1)S(1)}, s16[4,288,128]{2,1,0:T(8,128)(2,1)S(1)}, u32[]{:S(2)}, u32[]{:S(2)}) collective-permute-start(s16[4,288,128]{2,1,0:T(8,128)(2,1)S(1)} %get-tuple-element.111), channel_id=1, source_target_pairs={{0,8},{1,9},{2,10},{3,11},{4,12},{5,13},{6,14},{7,15},{8,0},{9,1},... | collective-permute-start | bytes 884744 | tf_op jit(solution)/shard_map/ppermute | solution.py:348
  97.8 9.6 %collective-permute-start.25 = (s16[4,288,128]{2,1,0:T(8,128)(2,1)S(1)}, s16[4,288,128]{2,1,0:T(8,128)(2,1)S(1)}, u32[]{:S(2)}, u32[]{:S(2)}) collective-permute-start(s16[4,288,128]{2,1,0:T(8,128)(2,1)S(1)} %get-tuple-element.112), channel_id=1, source_target_pairs={{0,12},{1,13},{2,14},{3,15},{4,0},{5,1},{6,2},{7,3},{8,4},{9,5},{1... | collective-permute-start | bytes 884744 | tf_op jit(solution)/shard_map/ppermute | solution.py:348
  109.3 6.4 %collective-permute-start.26 = (s16[560,128]{1,0:T(8,128)(2,1)S(1)}, s16[560,128]{1,0:T(8,128)(2,1)S(1)}, u32[]{:S(2)}, u32[]{:S(2)}) collective-permute-start(s16[560,128]{1,0:T(8,128)(2,1)S(1)} %get-tuple-element.114), channel_id=1, source_target_pairs={{0,4},{1,5},{2,6},{3,7},{4,8},{5,9},{6,10},{7,11},{8,12},{9,13},{1... | collective-permute-start | bytes 430088 | tf_op jit(solution)/shard_map/ppermute | solution.py:348
  110.0 7.5 %collective-permute-start.27 = (s16[560,128]{1,0:T(8,128)(2,1)S(1)}, s16[560,128]{1,0:T(8,128)(2,1)S(1)}, u32[]{:S(2)}, u32[]{:S(2)}) collective-permute-start(s16[560,128]{1,0:T(8,128)(2,1)S(1)} %get-tuple-element.115), channel_id=1, source_target_pairs={{0,8},{1,9},{2,10},{3,11},{4,12},{5,13},{6,14},{7,15},{8,0},{9,1},... | collective-permute-start | bytes 430088 | tf_op jit(solution)/shard_map/ppermute | solution.py:348
  112.9 5.3 %collective-permute-start.28 = (s16[560,128]{1,0:T(8,128)(2,1)S(1)}, s16[560,128]{1,0:T(8,128)(2,1)S(1)}, u32[]{:S(2)}, u32[]{:S(2)}) collective-permute-start(s16[560,128]{1,0:T(8,128)(2,1)S(1)} %get-tuple-element.116), channel_id=1, source_target_pairs={{0,12},{1,13},{2,14},{3,15},{4,0},{5,1},{6,2},{7,3},{8,4},{9,5},{1... | collective-permute-start | bytes 430088 | tf_op jit(solution)/shard_map/ppermute | solution.py:348
  112.9 7.8 %collective-permute-start.29 = (s16[560,128]{1,0:T(8,128)(2,1)S(1)}, s16[560,128]{1,0:T(8,128)(2,1)S(1)}, u32[]{:S(2)}, u32[]{:S(2)}) collective-permute-start(s16[560,128]{1,0:T(8,128)(2,1)S(1)} %get-tuple-element.118), channel_id=1, source_target_pairs={{0,1},{1,2},{2,3},{3,0},{4,5},{5,6},{6,7},{7,4},{8,9},{9,10},{10,1... | collective-permute-start | bytes 430088 | tf_op jit(solution)/shard_map/ppermute | solution.py:348
  112.9 7.8 %collective-permute-start.30 = (s16[560,128]{1,0:T(8,128)(2,1)S(1)}, s16[560,128]{1,0:T(8,128)(2,1)S(1)}, u32[]{:S(2)}, u32[]{:S(2)}) collective-permute-start(s16[560,128]{1,0:T(8,128)(2,1)S(1)} %get-tuple-element.119), channel_id=1, source_target_pairs={{0,2},{1,3},{2,0},{3,1},{4,6},{5,7},{6,4},{7,5},{8,10},{9,11},{10,... | collective-permute-start | bytes 430088 | tf_op jit(solution)/shard_map/ppermute | solution.py:348
  115.7 7.7 %collective-permute-start.31 = (s16[560,128]{1,0:T(8,128)(2,1)S(1)}, s16[560,128]{1,0:T(8,128)(2,1)S(1)}, u32[]{:S(2)}, u32[]{:S(2)}) collective-permute-start(s16[560,128]{1,0:T(8,128)(2,1)S(1)} %get-tuple-element.120), channel_id=1, source_target_pairs={{0,3},{1,0},{2,1},{3,2},{4,7},{5,4},{6,5},{7,6},{8,11},{9,8},{10,9... | collective-permute-start | bytes 430088 | tf_op jit(solution)/shard_map/ppermute | solution.py:348
  124.5 0.8 copy-start.1
  125.4 14.7 %all-to-all-start = ((s16[16,16,640]{2,1,0:T(8,128)(2,1)}), s16[16,16,640]{2,1,0:T(8,128)(2,1)S(1)}, u32[]{:S(2)}, u32[]{:S(2)}) async-start(s16[16,16,640]{2,1,0:T(8,128)(2,1)} %bitcast.21), calls=%async_computation | async-start | bytes 655360 | tf_op jit(solution)/shard_map/all_to_all | solution.py:417
  140.0 1.1 copy-start.2

commit v4 on v2

--- a/solution.py
+++ b/solution.py
@@ -20,7 +20,7 @@
 LOG_GRID = 200.0
 FULL = 32760.0
 TINY = 1e-37
-VMEM = 28 * 1024 * 1024
+VMEM = 20 * 1024 * 1024
 SMALL = 16 * 1024 * 1024
 
 
@@ -49,17 +49,17 @@
 
 
 def pack(out_ref, values, far):
-    rows = values.shape[0]
+    rows, wide = values.shape
     scale = column_scale(jnp.max(jnp.abs(values), axis=0, keepdims=True))
     out_ref[pl.ds(0, rows), :] = encode(values, scale)
-    heads = jnp.broadcast_to(scale, (PAD, LANES))
+    heads = jnp.broadcast_to(scale, (PAD, wide))
     if far is None:
         out_ref[pl.ds(rows, PAD), :] = heads.astype(S32).astype(S16)
         return
     far_scale = column_scale(jnp.max(jnp.abs(far), axis=0, keepdims=True))
     out_ref[pl.ds(rows, PAD), :] = encode(far, far_scale)
-    which = lax.broadcasted_iota(S32, (PAD, LANES), 0)
-    heads = jnp.where(which == 0, heads, jnp.broadcast_to(far_scale, (PAD, LANES)))
+    which = lax.broadcasted_iota(S32, (PAD, wide), 0)
+    heads = jnp.where(which == 0, heads, jnp.broadcast_to(far_scale, (PAD, wide)))
     out_ref[pl.ds(rows + PAD, PAD), :] = heads.astype(S32).astype(S16)
 
 
@@ -124,14 +124,14 @@
 
 
 def product_kernel(has_far, rows, place_ref, v_ref, rank_ref, *rest):
-    amps, outs, (first, mates, table, raw) = rest[:2], rest[2:10], rest[10:]
+    amps, outs, (first, mates, table, raw) = rest[:2], rest[2:6], rest[6:]
     tiles, tile, _ = v_ref.shape
     steps = tiles // 4
     half = CW // 2
     groups = SIDE * SIDE
     peer = rows // groups
 
-    y, core = place_ref[2], place_ref[3]
+    y, core, here, there = (place_ref[k] for k in range(4))
     depth = amps[0].shape[2]
     for k in range(SIDE):
         chip = lax.rem(y + SIDE - k, SIDE) * 2
@@ -180,26 +180,19 @@
     for part in range(2):
         sort(steps - 1, part, raw[pl.ds((steps - 1) % 2 * tile, tile), columns(part)])
 
-    z, x = place_ref[0], place_ref[1]
-    for kx in range(SIDE):
-        for kz in range(SIDE):
-            zt = lax.rem(z + kz, SIDE)
-            xt = lax.rem(x + kx, SIDE)
-            owner_id = zt * SIDE + xt
+    for k in range(SIDE):
+        for m in range(SIDE):
+            near, later = lax.rem(here + k, SIDE), lax.rem(there + m, SIDE)
+            owner_id = jnp.where(core == 0, later * SIDE + near, near * SIDE + later)
             base = pl.multiple_of(owner_id * rows, rows)
-            far_parts = [None, None]
-            sums = []
-            for side in range(2):
-                mine = first[pl.ds(base, rows), pl.ds(side * LANES, LANES)]
-                other = mates[:, pl.ds(owner_id, 1), :, pl.ds(side * LANES, LANES)].reshape(rows, LANES)
-                if has_far and side == 1:
-                    far = other.T[LANES - NO // 2 :]
-                    far_parts = [far[:, :LANES], far[:, LANES:]]
-                    lane = lax.broadcasted_iota(S32, (rows, LANES), 1)
-                    other = jnp.where(lane < LANES - NO // 2, other, 0.0)
-                sums.append(mine + other)
-            pack(outs[kx].at[zt], sums[0], far_parts[0])
-            pack(outs[4 + kz].at[xt], sums[1], far_parts[1])
+            mine = first[pl.ds(base, rows), :]
+            other = mates[:, pl.ds(owner_id, 1)].reshape(rows, half)
+            far = None
+            if has_far:
+                far = other[:, half - LANES :].T[LANES - NO // 2 :]
+                lane = lax.broadcasted_iota(S32, (rows, half), 1)
+                other = jnp.where(lane < half - NO // 2, other, 0.0)
+            pack(outs[k].at[m], mine + other, far)
 
 
 def packed_rows(rows, has_far):
@@ -211,12 +204,12 @@
     groups = SIDE * SIDE
     half = CW // 2
     vmem, smem = pl.BlockSpec(memory_space=pltpu.VMEM), pl.BlockSpec(memory_space=pltpu.SMEM)
-    out = (SIDE, packed_rows(rows, has_far), LANES)
+    out = (SIDE, packed_rows(rows, has_far), half)
     return pl.pallas_call(
         functools.partial(product_kernel, has_far, rows),
-        out_shape=[jax.ShapeDtypeStruct(out, S16)] * 8,
+        out_shape=[jax.ShapeDtypeStruct(out, S16)] * SIDE,
         in_specs=[smem] + [vmem] * (2 + len(amps)),
-        out_specs=[vmem] * 8,
+        out_specs=[vmem] * SIDE,
         scratch_shapes=[
             pltpu.VMEM((groups * rows, half), F32),
             pltpu.VMEM((groups, groups, rows // groups, half), F32),
@@ -236,43 +229,37 @@
     return [(sum(heights[:c]), heights[c]) for c in range(len(heights))]
 
 
-def relay_kernel(rows, far_flags, place_ref, *refs):
-    count = 8 * len(far_flags)
-    ins, outs = refs[:count], refs[count:]
+def relay_kernel(rows, far_flags, *refs):
+    ins, outs = refs[:-SIDE], refs[-SIDE:]
     for c, (top, height) in enumerate(chunk_rows(rows, far_flags)):
-        for side in range(2):
-            for k in range(SIDE):
-                at = lax.rem(place_ref[side] + k, SIDE)
-                blocks = [r.at[at] for r in ins[c * 8 + side * 4 :][:4]]
-                total, far = unpack_sum(blocks, rows, far_flags[c])
-                pack(outs[side * 4 + k].at[pl.ds(top, height)], total, far)
-
-
-def relay(pieces, place, rows, far_flags):
+        for m in range(SIDE):
+            blocks = [r.at[m] for r in ins[c * SIDE :][:SIDE]]
+            total, far = unpack_sum(blocks, rows, far_flags[c])
+            pack(outs[m].at[pl.ds(top, height)], total, far)
+
+
+def relay(came, rows, far_flags):
     height = sum(h for _, h in chunk_rows(rows, far_flags))
     vmem = pl.BlockSpec(memory_space=pltpu.VMEM)
     return pl.pallas_call(
         functools.partial(relay_kernel, rows, far_flags),
-        out_shape=[jax.ShapeDtypeStruct((height, LANES), S16)] * 8,
-        in_specs=[pl.BlockSpec(memory_space=pltpu.SMEM)] + [vmem] * len(pieces),
-        out_specs=[vmem] * 8,
+        out_shape=[jax.ShapeDtypeStruct((height, CW // 2), S16)] * SIDE,
+        in_specs=[vmem] * len(came),
+        out_specs=[vmem] * SIDE,
         compiler_params=pltpu.CompilerParams(vmem_limit_bytes=SMALL),
         name="relay",
-    )(place, *pieces)
+    )(*came)
 
 
 def owner_kernel(rows, far_flags, *refs):
-    ins, own, send = refs[:8], refs[8], refs[9]
+    came, (own, send) = refs[:SIDE], refs[SIDE:]
+    half = CW // 2
     for c, (top, height) in enumerate(chunk_rows(rows, far_flags)):
-        has_far = far_flags[c]
-        fars = []
-        for side in range(2):
-            blocks = [r.at[pl.ds(top, height)] for r in ins[side * 4 :][:4]]
-            total, far = unpack_sum(blocks, rows, has_far)
-            own[:, pl.ds((c * 2 + side) * LANES, LANES)] = total
-            fars.append(far)
-        if has_far:
-            far = jnp.concatenate([jnp.zeros((LANES - NO // 2, rows), F32), jnp.concatenate(fars, axis=1)], axis=0)
+        blocks = [r.at[pl.ds(top, height)] for r in came]
+        total, far = unpack_sum(blocks, rows, far_flags[c])
+        own[:, pl.ds(c * half, half)] = total
+        if far_flags[c]:
+            far = jnp.concatenate([jnp.zeros((LANES - NO // 2, rows), F32), far], axis=0)
             own[:, pl.ds(HALF, LANES)] = far.T
     scale = column_scale(jnp.max(jnp.abs(own[...]), axis=1, keepdims=True))
     send[:, pl.ds(0, HALF)] = encode(own[:, pl.ds(0, HALF)], scale)
@@ -282,17 +269,17 @@
     send[:, pl.ds(HALF, LANES)] = far.astype(S32).astype(S16)
 
 
-def owner(pieces, rows, far_flags):
+def owner(came, rows, far_flags):
     vmem = pl.BlockSpec(memory_space=pltpu.VMEM)
     width = HALF + LANES
     return pl.pallas_call(
         functools.partial(owner_kernel, rows, far_flags),
-        out_shape=[jax.ShapeDtypeStruct((rows, width), F32), jax.ShapeDtypeStruct((rows, width), S16)],
-        in_specs=[vmem] * len(pieces),
+        out_shape=[pltpu.HBM((rows, width), F32), jax.ShapeDtypeStruct((rows, width), S16)],
+        in_specs=[vmem] * SIDE,
         out_specs=[vmem] * 2,
         compiler_params=pltpu.CompilerParams(vmem_limit_bytes=SMALL),
         name="owner",
-    )(*pieces)
+    )(*came)
 
 
 def close_kernel(rows, own, came, ranks, energy, pair_sum, spread, out, joined):
@@ -331,19 +318,16 @@
     )(own, came, ranks, energy, pair_sum, spread)
 
 
-def shifted(dz, dx):
-    return [
-        (z * SIDE + x, (z + dz) % SIDE * SIDE + (x + dx) % SIDE) for z in range(SIDE) for x in range(SIDE)
-    ]
-
-
-def spread_out(pieces, across_x_first):
-    got = list(pieces)
+def trade(pieces, x_core):
+    got = [pieces[0]]
     for k in (2, 1, 3):
-        for side in range(2):
-            along_x = (side == 0) == across_x_first
-            perm = shifted(0, k) if along_x else shifted(k, 0)
-            got[side * 4 + k] = lax.ppermute(pieces[side * 4 + k], "col", perm)
+        perm = []
+        for row in range(2 * SIDE):
+            for z in range(SIDE):
+                for x in range(SIDE):
+                    zt, xt = (z, (x + k) % SIDE) if row % 2 == x_core else ((z + k) % SIDE, x)
+                    perm.append(((row * SIDE + z) * SIDE + x, (row * SIDE + zt) * SIDE + xt))
+        got.append(lax.ppermute(pieces[k], ("row", "col"), perm))
     return got
 
 
@@ -390,9 +374,10 @@
     ranks, along[0] = lax.optimization_barrier((ranks, along[0]))
     ranks = jnp.stack([ranks[:, :rows], ranks[:, rows:]])
 
+    row = lax.axis_index("row")
     col = lax.axis_index("col")
-    row = lax.axis_index("row")
-    place = jnp.stack([col // SIDE, col % SIDE, row // 2, row % 2]).astype(S32)
+    z, x, core = col // SIDE, col % SIDE, row % 2
+    place = jnp.stack([row // 2, core, jnp.where(core == 0, x, z), jnp.where(core == 0, z, x)]).astype(S32)
     slots = tile_list[0, 0]
     slot_ids = jnp.arange(slots.shape[0], dtype=S32)
     order = jnp.sum(jnp.where(slots[None, :] == slot_ids[:, None], slot_ids[None, :], 0), axis=1)
@@ -403,11 +388,12 @@
     landed = []
     for c in range(CHUNKS):
         sent = product(tiles, share(along[c]), ranks, place, rows, far_flags[c])
+        if c > 0:
+            sent, landed = lax.optimization_barrier((sent, landed))
         if c + 1 < CHUNKS:
             sent, along[c + 1] = lax.optimization_barrier((sent, along[c + 1]))
-        landed += spread_out(sent, True)
-    landed = spread_out(relay(landed, place, rows, far_flags), False)
-    own, send = owner(landed, rows, far_flags)
+        landed += trade(sent, 0)
+    own, send = owner(trade(relay(landed, rows, far_flags), 1), rows, far_flags)
     came = lax.all_to_all(send, "col", split_axis=0, concat_axis=0, tiled=True)
     pair_sum = (occ_energy[:, None] + occ_energy[None, :]).reshape(1, OCC)
     back = jnp.stack([own_rank, mate_rank], axis=1).astype(S32)

time: 140 us -> 119 us (0.85)
  starting transfers between devices: 40.6 us -> 27.2 us
  waiting for transfers between devices: 36.9 us -> 28.1 us
  Pallas kernels: 38.3 us -> 40.2 us
    ppermute x18 -> x9, starting transfers between devices: 25.3 us -> 13.2 us  [trade(): got.append(lax.ppermute(pieces[k], ('row', 'col'), perm))]
    ppermute x18 -> x9, waiting for transfers between devices: 28.6 us -> 19.9 us  [trade(): got.append(lax.ppermute(pieces[k], ('row', 'col'), perm))]
    pallas_call x1, Pallas kernels: 3.16 us -> 5.41 us  [stage(): pl.pallas_call(stage_kernel, out_shape=pltpu.VMEM(tiles.shape, tiles.dtyp...]
    unnamed x17 -> x15, local copies, waits for them, and re-layouts: 2.99 us -> 2.15 us
  transfers between devices with their start and end apart: 27 -> 18, of which waited for: 11 -> 6; matrix products, arithmetic and copies ran while one was open for 1% -> 1% of each run, Pallas kernels for 23% -> 30%
where the time goes in v4:
time: 119 us; the launch traced here: 118 us
  Pallas kernels  40.2 us (34%)
  waiting for transfers between devices  28.1 us (24%)
  starting transfers between devices  27.2 us (23%)
  blocking collectives  15.3 us (13%)
  local copies, waits for them, and re-layouts  2.56 us (2%)
  other arithmetic  2.2 us (2%)
  matrix products  1.58 us (1%)
    pallas_call x2, Pallas kernels, product(): pl.pallas_call(functools.partial(product_kernel, has_far, rows), out_shap...  29.5 us
    ppermute x9, waiting for transfers between devices, trade(): got.append(lax.ppermute(pieces[k], ('row', 'col'), perm))  19.9 us
    all_to_all x1, blocking collectives, body(): lax.all_to_all(spoken, 'col', split_axis=0, concat_axis=0, tiled=True)  15.3 us
    ppermute x9, starting transfers between devices, trade(): got.append(lax.ppermute(pieces[k], ('row', 'col'), perm))  13.2 us
    ppermute x6, starting transfers between devices, fetch_along(): lax.ppermute(part, 'row', shifted_rows(k, 0))  9.49 us
    all_to_all x1, waiting for transfers between devices, body(): came = lax.all_to_all(send, 'col', split_axis=0, concat_axis=0, tiled=True)  8.23 us
    pallas_call x1, Pallas kernels, stage(): pl.pallas_call(stage_kernel, out_shape=pltpu.VMEM(tiles.shape, tiles.dtyp...  5.41 us
    all_to_all x1, starting transfers between devices, body(): came = lax.all_to_all(send, 'col', split_axis=0, concat_axis=0, tiled=True)  4.42 us
  transfers between devices with their start and end apart: 18, of which 6 were waited for; matrix products, arithmetic and copies ran while one was open for 1% of the time, Pallas kernels for 30%

profile of v4, /device:TPU:0, one launch (start us, length us, event | category | flops | bytes accessed | tf_op | source)
XLA Modules:
  0.0 118.1 jit_solution(4461651450336305318)
XLA Ops:
  0.0 1.0 copy-done
  1.0 1.6 %fusion.4 = bf16[256,1024]{1,0:T(8,128)(2,1)S(1)} fusion(bf16[256,1024]{1,0:T(8,128)(2,1)S(1)} %bitcast.34, s32[1024]{0:T(1024)} %constant.93.clone), kind=kOutput, calls=%fused_computation.6 | convolution fusion | flops 538181632 | bytes 1052672 | tf_op jit(solution)/shard_map/dot_general | solution.py:360
  2.7 1.7 %collective-permute-start = (bf16[4,64,512]{2,1,0:T(8,128)(2,1)S(1)}, bf16[4,64,512]{2,1,0:T(8,128)(2,1)S(1)}, u32[]{:S(2)}, u32[]{:S(2)}) collective-permute-start(bf16[4,64,512]{2,1,0:T(8,128)(2,1)S(1)} %bitcast.41), channel_id=1, source_target_pairs={{0,32},{16,48},{32,64},{48,80},{64,96},{80,112},{96,0},{112,16},{1... | collective-permute-start | bytes 786440 | tf_op jit(solution)/shard_map/ppermute | solution.py:339
  4.4 2.9 %collective-permute-start.1 = (bf16[4,64,512]{2,1,0:T(8,128)(2,1)S(1)}, bf16[4,64,512]{2,1,0:T(8,128)(2,1)S(1)}, u32[]{:S(2)}, u32[]{:S(2)}) collective-permute-start(bf16[4,64,512]{2,1,0:T(8,128)(2,1)S(1)} %bitcast.42), channel_id=1, source_target_pairs={{0,64},{16,80},{32,96},{48,112},{64,0},{80,16},{96,32},{112,48},{1... | collective-permute-start | bytes 786440 | tf_op jit(solution)/shard_map/ppermute | solution.py:339
  7.3 1.3 %collective-permute-start.2 = (bf16[4,64,512]{2,1,0:T(8,128)(2,1)S(1)}, bf16[4,64,512]{2,1,0:T(8,128)(2,1)S(1)}, u32[]{:S(2)}, u32[]{:S(2)}) collective-permute-start(bf16[4,64,512]{2,1,0:T(8,128)(2,1)S(1)} %bitcast.43), channel_id=1, source_target_pairs={{0,96},{16,112},{32,0},{48,16},{64,32},{80,48},{96,64},{112,80},{1... | collective-permute-start | bytes 786440 | tf_op jit(solution)/shard_map/ppermute | solution.py:339
  8.7 0.3 convert_reduce_fusion.1
  9.0 15.3 %all_to_all.20 = s32[16,1,512]{2,1,0:T(1,128)S(1)} all-to-all(s32[16,1,512]{2,1,0:T(1,128)S(1)} %broadcast_in_dim.14), channel_id=1, replica_groups=mesh['row'=8,'col'=16] {'col'}, dimensions={0} | all-to-all | bytes 65536 | tf_op jit(solution)/shard_map/all_to_all | solution.py:372
  24.3 0.0 collective-permute-done
  24.3 0.1 pad_maximum_fusion.rest_0_
  24.4 0.1 collective-permute-start.3
  24.5 0.7 collective-permute-start.4
  25.3 0.8 collective-permute-start.5
  26.1 2.0 %collective-permute-start.6 = (bf16[4,64,512]{2,1,0:T(8,128)(2,1)S(1)}, bf16[4,64,512]{2,1,0:T(8,128)(2,1)}, u32[]{:S(2)}, u32[]{:S(2)}) collective-permute-start(bf16[4,64,512]{2,1,0:T(8,128)(2,1)S(1)} %bitcast.39), channel_id=1, source_target_pairs={{0,96},{16,112},{32,0},{48,16},{64,32},{80,48},{96,64},{112,80},{1... | collective-permute-start | bytes 786440 | tf_op jit(solution)/shard_map/ppermute | solution.py:339
  28.7 0.1 select_reduce_fusion.order_ref
  28.8 5.4 %stage.1.v_ref = bf16[32,512,512]{2,1,0:T(8,128)(2,1)S(1)} custom-call(s32[32]{0:T(128)S(1)} %select_reduce_fusion.order_ref, s32[32]{0:T(128)S(1)} %compare_convert_fusion.live_ref, bf16[32,512,512]{2,1,0:T(8,128)(2,1)} %bitcast.36), custom_call_target="tpu_custom_call" | custom-call | bytes 16777216 | tf_op jit(solution)/shard_map/stage/pallas_call | solution.py:114
  34.2 0.1 pad_add_fusion.3.place_ref
  34.3 14.6 %product.2 = (s16[4,272,256]{2,1,0:T(8,128)(2,1)S(1)}, s16[4,272,256]{2,1,0:T(8,128)(2,1)S(1)}, s16[4,272,256]{2,1,0:T(8,128)(2,1)S(1)}, s16[4,272,256]{2,1,0:T(8,128)(2,1)S(1)}) custom-call(s32[4]{0:T(128)S(1)} %pad_add_fusion.3.place_ref, bf16[32,512,512]{2,1,0:T(8,128)(2,1)S(1)} %stage.1.v_ref, s32[2,16,256]{2,1,0:T(8,128)S(1)} %pad_add_fusion.rank_ref, ...), custom_call_target="tpu_custom_call" | custom-call | flops 8589934592 | bytes 4194304 | tf_op jit(solution)/shard_map/product/pallas_call | solution.py:208
  49.0 1.1 pad_maximum_fusion.1.rest_0_
  50.0 0.1 collective-permute-start.7
  50.1 0.1 collective-permute-start.10
  50.2 3.4 %collective-permute-start.8 = (s16[4,272,256]{2,1,0:T(8,128)(2,1)S(1)}, s16[4,272,256]{2,1,0:T(8,128)(2,1)S(1)}, u32[]{:S(2)}, u32[]{:S(2)}) collective-permute-start(s16[4,272,256]{2,1,0:T(8,128)(2,1)S(1)} %get-tuple-element.58), channel_id=1, source_target_pairs={{0,2},{1,3},{2,0},{3,1},{4,6},{5,7},{6,4},{7,5},{8,10},{9,11},{10,... | collective-permute-start | bytes 1671176 | tf_op jit(solution)/shard_map/ppermute | solution.py:330
  53.6 0.0 collective-permute-start.9
  53.6 14.9 %product.3 = (s16[4,288,256]{2,1,0:T(8,128)(2,1)S(1)}, s16[4,288,256]{2,1,0:T(8,128)(2,1)S(1)}, s16[4,288,256]{2,1,0:T(8,128)(2,1)S(1)}, s16[4,288,256]{2,1,0:T(8,128)(2,1)S(1)}) custom-call(s32[4]{0:T(128)S(1)} %pad_add_fusion.3.place_ref, bf16[32,512,512]{2,1,0:T(8,128)(2,1)S(1)} %stage.1.v_ref, s32[2,16,256]{2,1,0:T(8,128)S(1)} %pad_add_fusion.rank_ref, ...), custom_call_target="tpu_custom_call" | custom-call | flops 8589934592 | bytes 4194304 | tf_op jit(solution)/shard_map/product/pallas_call | solution.py:208
  68.5 0.0 copy-start.3
  68.5 0.0 copy-start.4
  68.5 0.0 copy-start.2
  68.5 2.9 %collective-permute-start.11 = (s16[4,288,256]{2,1,0:T(8,128)(2,1)S(1)}, s16[4,288,256]{2,1,0:T(8,128)(2,1)S(1)}, u32[]{:S(2)}, u32[]{:S(2)}) collective-permute-start(s16[4,288,256]{2,1,0:T(8,128)(2,1)S(1)} %get-tuple-element.66), channel_id=1, source_target_pairs={{0,2},{1,3},{2,0},{3,1},{4,6},{5,7},{6,4},{7,5},{8,10},{9,11},{10,... | collective-permute-start | bytes 1769480 | tf_op jit(solution)/shard_map/ppermute | solution.py:330
  71.4 1.3 %collective-permute-start.12 = (s16[4,288,256]{2,1,0:T(8,128)(2,1)S(1)}, s16[4,288,256]{2,1,0:T(8,128)(2,1)S(1)}, u32[]{:S(2)}, u32[]{:S(2)}) collective-permute-start(s16[4,288,256]{2,1,0:T(8,128)(2,1)S(1)} %get-tuple-element.67), channel_id=1, source_target_pairs={{0,1},{1,2},{2,3},{3,0},{4,5},{5,6},{6,7},{7,4},{8,9},{9,10},{10,1... | collective-permute-start | bytes 1769480 | tf_op jit(solution)/shard_map/ppermute | solution.py:330
  72.7 1.9 %collective-permute-start.13 = (s16[4,288,256]{2,1,0:T(8,128)(2,1)S(1)}, s16[4,288,256]{2,1,0:T(8,128)(2,1)S(1)}, u32[]{:S(2)}, u32[]{:S(2)}) collective-permute-start(s16[4,288,256]{2,1,0:T(8,128)(2,1)S(1)} %get-tuple-element.68), channel_id=1, source_target_pairs={{0,3},{1,0},{2,1},{3,2},{4,7},{5,4},{6,5},{7,6},{8,11},{9,8},{10,9... | collective-permute-start | bytes 1769480 | tf_op jit(solution)/shard_map/ppermute | solution.py:330
  74.6 5.5 %collective-permute-done.11.refs_5_ = s16[4,288,256]{2,1,0:T(8,128)(2,1)S(1)} collective-permute-done((s16[4,288,256]{2,1,0:T(8,128)(2,1)S(1)}, s16[4,288,256]{2,1,0:T(8,128)(2,1)S(1)}, u32[]{:S(2)}, u32[]{:S(2)}) %collective-permute-start.11) | collective-permute-done | bytes 589856 | tf_op jit(solution)/shard_map/ppermute | solution.py:330
  80.1 6.2 %collective-permute-done.12.refs_6_ = s16[4,288,256]{2,1,0:T(8,128)(2,1)S(1)} collective-permute-done((s16[4,288,256]{2,1,0:T(8,128)(2,1)S(1)}, s16[4,288,256]{2,1,0:T(8,128)(2,1)S(1)}, u32[]{:S(2)}, u32[]{:S(2)}) %collective-permute-start.12) | collective-permute-done | bytes 589856 | tf_op jit(solution)/shard_map/ppermute | solution.py:330
  86.3 0.6 collective-permute-done.13.refs_7_
  86.9 1.4 %relay.1 = (s16[560,256]{1,0:T(8,128)(2,1)S(1)}, s16[560,256]{1,0:T(8,128)(2,1)S(1)}, s16[560,256]{1,0:T(8,128)(2,1)S(1)}, s16[560,256]{1,0:T(8,128)(2,1)S(1)}) custom-call(s16[4,272,256]{2,1,0:T(8,128)(2,1)S(1)} %get-tuple-element.61.refs_0_, s16[4,272,256]{2,1,0:T(8,128)(2,1)S(1)} %collective-permute-done.8.refs_1_, ...), custom_call_target="tpu_custom_call" | custom-call | tf_op jit(solution)/shard_map/relay/pallas_call | solution.py:244
  88.3 0.4 collective-permute-start.14
  88.7 1.9 %collective-permute-start.15 = (s16[560,256]{1,0:T(8,128)(2,1)S(1)}, s16[560,256]{1,0:T(8,128)(2,1)S(1)}, u32[]{:S(2)}, u32[]{:S(2)}) collective-permute-start(s16[560,256]{1,0:T(8,128)(2,1)S(1)} %get-tuple-element.71), channel_id=1, source_target_pairs={{0,4},{1,5},{2,6},{3,7},{4,8},{5,9},{6,10},{7,11},{8,12},{9,13},{1... | collective-permute-start | bytes 860168 | tf_op jit(solution)/shard_map/ppermute | solution.py:330
  90.6 1.3 %collective-permute-start.16 = (s16[560,256]{1,0:T(8,128)(2,1)S(1)}, s16[560,256]{1,0:T(8,128)(2,1)S(1)}, u32[]{:S(2)}, u32[]{:S(2)}) collective-permute-start(s16[560,256]{1,0:T(8,128)(2,1)S(1)} %get-tuple-element.72), channel_id=1, source_target_pairs={{0,12},{1,13},{2,14},{3,15},{4,0},{5,1},{6,2},{7,3},{8,4},{9,5},{1... | collective-permute-start | bytes 860168 | tf_op jit(solution)/shard_map/ppermute | solution.py:330
  92.0 0.1 broadcast_add_fusion
  92.0 4.6 %collective-permute-done.14.refs_1_ = s16[560,256]{1,0:T(8,128)(2,1)S(1)} collective-permute-done((s16[560,256]{1,0:T(8,128)(2,1)S(1)}, s16[560,256]{1,0:T(8,128)(2,1)S(1)}, u32[]{:S(2)}, u32[]{:S(2)}) %collective-permute-start.14) | collective-permute-done | bytes 286752 | tf_op jit(solution)/shard_map/ppermute | solution.py:330
  96.7 3.0 %collective-permute-done.15.refs_2_ = s16[560,256]{1,0:T(8,128)(2,1)S(1)} collective-permute-done((s16[560,256]{1,0:T(8,128)(2,1)S(1)}, s16[560,256]{1,0:T(8,128)(2,1)S(1)}, u32[]{:S(2)}, u32[]{:S(2)}) %collective-permute-start.15) | collective-permute-done | bytes 286752 | tf_op jit(solution)/shard_map/ppermute | solution.py:330
  99.6 1.2 %owner.1 = (f32[256,640]{1,0:T(8,128)}, s16[256,640]{1,0:T(8,128)(2,1)}) custom-call(s16[560,256]{1,0:T(8,128)(2,1)S(1)} %get-tuple-element.69.refs_0_, s16[560,256]{1,0:T(8,128)(2,1)S(1)} %collective-permute-done.14.refs_1_, s16[560,256]{1,0:T(8,128)(2,1)S(1)} %collective-permute-done.15.refs_2_, s16[560,256]{1,0:T(8,128)(2,1)S(1)} %collective-permute-done.16.refs_3_), custom_call_target="tpu_custom_call" | custom-call | tf_op jit(solution)/shard_map/owner/pallas_call | solution.py:275
  100.9 4.4 %all-to-all-start.1 = ((s16[16,16,640]{2,1,0:T(8,128)(2,1)}), s16[16,16,640]{2,1,0:T(8,128)(2,1)S(1)}, u32[]{:S(2)}, u32[]{:S(2)}) async-start(s16[16,16,640]{2,1,0:T(8,128)(2,1)} %bitcast.21), calls=%async_computation.1 | async-start | bytes 655360 | tf_op jit(solution)/shard_map/all_to_all | solution.py:397
  105.3 0.1 copy.15.ranks
  105.5 0.1 copy.16.energy
  105.6 0.1 add.58.pair_sum
  105.7 0.4 fusion.1.spread
  106.1 8.2 %all-to-all-done.1 = s16[16,16,640]{2,1,0:T(8,128)(2,1)S(1)} async-done(((s16[16,16,640]{2,1,0:T(8,128)(2,1)}), s16[16,16,640]{2,1,0:T(8,128)(2,1)S(1)}, u32[]{:S(2)}, u32[]{:S(2)}) %all-to-all-start.1) | async-done | bytes 327712 | tf_op jit(solution)/shard_map/all_to_all | solution.py:397
  114.4 1.1 copy-done.1
  115.4 2.7 %close.1 = f32[256,1024]{1,0:T(8,128)} custom-call(f32[256,640]{1,0:T(8,128)S(1)} %copy-done.1, s16[256,640]{1,0:T(8,128)(2,1)S(1)} %bitcast.35, s32[256,2]{1,0:T(8,128)S(1)} %copy.15.ranks, f32[256,1]{1,0:T(8,128)S(1)} %copy.16.energy, f32[1,1024]{1,0:T(1,128)S(1)} %add.58.pair_sum, bf16[1024,1024]{1,0:T(8,128)(2,1)S(1)} %fusion.1.spread), custom_call_target="tpu_custom_call" | custom-call | tf_op jit(solution)/shard_map/close/pallas_call | solution.py:310
  (30 shorter events, 0.2 us)
Async XLA Ops:
  0.0 1.0 copy-start
  0.0 8.7 %copy-start.5 = (s32[256]{0:T(256)S(1)}, s32[256]{0:T(256)}, u32[]{:S(2)}) copy-start(s32[256]{0:T(256)} %param.15) | copy-start | bytes 3076
  0.0 28.7 %copy-start.6 = (s32[1,1,32]{2,1,0:T(1,128)S(1)}, s32[1,1,32]{2,1,0:T(1,128)}, u32[]{:S(2)}) copy-start(s32[1,1,32]{2,1,0:T(1,128)} %param.11) | copy-start | bytes 388
  2.7 21.6 %collective-permute-start = (bf16[4,64,512]{2,1,0:T(8,128)(2,1)S(1)}, bf16[4,64,512]{2,1,0:T(8,128)(2,1)S(1)}, u32[]{:S(2)}, u32[]{:S(2)}) collective-permute-start(bf16[4,64,512]{2,1,0:T(8,128)(2,1)S(1)} %bitcast.41), channel_id=1, source_target_pairs={{0,32},{16,48},{32,64},{48,80},{64,96},{80,112},{96,0},{112,16},{1... | collective-permute-start | bytes 786440 | tf_op jit(solution)/shard_map/ppermute | solution.py:339
  4.4 19.9 %collective-permute-start.1 = (bf16[4,64,512]{2,1,0:T(8,128)(2,1)S(1)}, bf16[4,64,512]{2,1,0:T(8,128)(2,1)S(1)}, u32[]{:S(2)}, u32[]{:S(2)}) collective-permute-start(bf16[4,64,512]{2,1,0:T(8,128)(2,1)S(1)} %bitcast.42), channel_id=1, source_target_pairs={{0,64},{16,80},{32,96},{48,112},{64,0},{80,16},{96,32},{112,48},{1... | collective-permute-start | bytes 786440 | tf_op jit(solution)/shard_map/ppermute | solution.py:339
  7.3 17.0 %collective-permute-start.2 = (bf16[4,64,512]{2,1,0:T(8,128)(2,1)S(1)}, bf16[4,64,512]{2,1,0:T(8,128)(2,1)S(1)}, u32[]{:S(2)}, u32[]{:S(2)}) collective-permute-start(bf16[4,64,512]{2,1,0:T(8,128)(2,1)S(1)} %bitcast.43), channel_id=1, source_target_pairs={{0,96},{16,112},{32,0},{48,16},{64,32},{80,48},{96,64},{112,80},{1... | collective-permute-start | bytes 786440 | tf_op jit(solution)/shard_map/ppermute | solution.py:339
  24.4 9.9 %collective-permute-start.3 = (bf16[4,4,64,512]{3,2,1,0:T(8,128)(2,1)S(1)}, bf16[4,4,64,512]{3,2,1,0:T(8,128)(2,1)S(1)}, u32[]{:S(2)}, u32[]{:S(2)}) collective-permute-start(bf16[4,4,64,512]{3,2,1,0:T(8,128)(2,1)S(1)} %pad_maximum_fusion.rest_0_), channel_id=1, source_target_pairs={{0,16},{16,0},{32,48},{48,32},{64,80},{80,64},{96,112},{112,96},{1... | collective-permute-start | bytes 3145736 | tf_op jit(solution)/shard_map/ppermute | solution.py:344
  24.5 24.4 %collective-permute-start.4 = (bf16[4,64,512]{2,1,0:T(8,128)(2,1)S(1)}, bf16[4,64,512]{2,1,0:T(8,128)(2,1)S(1)}, u32[]{:S(2)}, u32[]{:S(2)}) collective-permute-start(bf16[4,64,512]{2,1,0:T(8,128)(2,1)S(1)} %bitcast.37), channel_id=1, source_target_pairs={{0,32},{16,48},{32,64},{48,80},{64,96},{80,112},{96,0},{112,16},{1... | collective-permute-start | bytes 786440 | tf_op jit(solution)/shard_map/ppermute | solution.py:339
  25.3 23.7 %collective-permute-start.5 = (bf16[4,64,512]{2,1,0:T(8,128)(2,1)S(1)}, bf16[4,64,512]{2,1,0:T(8,128)(2,1)S(1)}, u32[]{:S(2)}, u32[]{:S(2)}) collective-permute-start(bf16[4,64,512]{2,1,0:T(8,128)(2,1)S(1)} %bitcast.38), channel_id=1, source_target_pairs={{0,64},{16,80},{32,96},{48,112},{64,0},{80,16},{96,32},{112,48},{1... | collective-permute-start | bytes 786440 | tf_op jit(solution)/shard_map/ppermute | solution.py:339
  26.1 22.9 %collective-permute-start.6 = (bf16[4,64,512]{2,1,0:T(8,128)(2,1)S(1)}, bf16[4,64,512]{2,1,0:T(8,128)(2,1)}, u32[]{:S(2)}, u32[]{:S(2)}) collective-permute-start(bf16[4,64,512]{2,1,0:T(8,128)(2,1)S(1)} %bitcast.39), channel_id=1, source_target_pairs={{0,96},{16,112},{32,0},{48,16},{64,32},{80,48},{96,64},{112,80},{1... | collective-permute-start | bytes 786440 | tf_op jit(solution)/shard_map/ppermute | solution.py:339
  50.0 3.5 %collective-permute-start.7 = (bf16[4,4,64,512]{3,2,1,0:T(8,128)(2,1)S(1)}, bf16[4,4,64,512]{3,2,1,0:T(8,128)(2,1)S(1)}, u32[]{:S(2)}, u32[]{:S(2)}) collective-permute-start(bf16[4,4,64,512]{3,2,1,0:T(8,128)(2,1)S(1)} %pad_maximum_fusion.1.rest_0_), channel_id=1, source_target_pairs={{0,16},{16,0},{32,48},{48,32},{64,80},{80,64},{96,112},{112,96},{1... | collective-permute-start | bytes 3145736 | tf_op jit(solution)/shard_map/ppermute | solution.py:344
  50.1 18.4 %collective-permute-start.10 = (s16[4,272,256]{2,1,0:T(8,128)(2,1)S(1)}, s16[4,272,256]{2,1,0:T(8,128)(2,1)S(1)}, u32[]{:S(2)}, u32[]{:S(2)}) collective-permute-start(s16[4,272,256]{2,1,0:T(8,128)(2,1)S(1)} %get-tuple-element.60), channel_id=1, source_target_pairs={{0,3},{1,0},{2,1},{3,2},{4,7},{5,4},{6,5},{7,6},{8,11},{9,8},{10,9... | collective-permute-start | bytes 1671176 | tf_op jit(solution)/shard_map/ppermute | solution.py:330
  50.2 18.3 %collective-permute-start.8 = (s16[4,272,256]{2,1,0:T(8,128)(2,1)S(1)}, s16[4,272,256]{2,1,0:T(8,128)(2,1)S(1)}, u32[]{:S(2)}, u32[]{:S(2)}) collective-permute-start(s16[4,272,256]{2,1,0:T(8,128)(2,1)S(1)} %get-tuple-element.58), channel_id=1, source_target_pairs={{0,2},{1,3},{2,0},{3,1},{4,6},{5,7},{6,4},{7,5},{8,10},{9,11},{10,... | collective-permute-start | bytes 1671176 | tf_op jit(solution)/shard_map/ppermute | solution.py:330
  53.6 14.9 %collective-permute-start.9 = (s16[4,272,256]{2,1,0:T(8,128)(2,1)S(1)}, s16[4,272,256]{2,1,0:T(8,128)(2,1)S(1)}, u32[]{:S(2)}, u32[]{:S(2)}) collective-permute-start(s16[4,272,256]{2,1,0:T(8,128)(2,1)S(1)} %get-tuple-element.59), channel_id=1, source_target_pairs={{0,1},{1,2},{2,3},{3,0},{4,5},{5,6},{6,7},{7,4},{8,9},{9,10},{10,1... | collective-permute-start | bytes 1671176 | tf_op jit(solution)/shard_map/ppermute | solution.py:330
  68.5 23.5 %copy-start.3 = (f32[32]{0:T(128)S(1)}, f32[32]{0:T(128)}, u32[]{:S(2)}) copy-start(f32[32]{0:T(128)} %param.14) | copy-start | bytes 388
  68.5 37.0 %copy-start.4 = (f32[256]{0:T(256)S(1)}, f32[256]{0:T(256)}, u32[]{:S(2)}) copy-start(f32[256]{0:T(256)} %param.13) | copy-start | bytes 3076
  68.5 37.2 %copy-start.2 = (s32[1024]{0:T(1024)S(1)}, s32[1024]{0:T(1024)}, u32[]{:S(2)}) copy-start(s32[1024]{0:T(1024)} %constant.94.clone) | copy-start | bytes 12292
  68.5 11.6 %collective-permute-start.11 = (s16[4,288,256]{2,1,0:T(8,128)(2,1)S(1)}, s16[4,288,256]{2,1,0:T(8,128)(2,1)S(1)}, u32[]{:S(2)}, u32[]{:S(2)}) collective-permute-start(s16[4,288,256]{2,1,0:T(8,128)(2,1)S(1)} %get-tuple-element.66), channel_id=1, source_target_pairs={{0,2},{1,3},{2,0},{3,1},{4,6},{5,7},{6,4},{7,5},{8,10},{9,11},{10,... | collective-permute-start | bytes 1769480 | tf_op jit(solution)/shard_map/ppermute | solution.py:330
  71.4 14.9 %collective-permute-start.12 = (s16[4,288,256]{2,1,0:T(8,128)(2,1)S(1)}, s16[4,288,256]{2,1,0:T(8,128)(2,1)S(1)}, u32[]{:S(2)}, u32[]{:S(2)}) collective-permute-start(s16[4,288,256]{2,1,0:T(8,128)(2,1)S(1)} %get-tuple-element.67), channel_id=1, source_target_pairs={{0,1},{1,2},{2,3},{3,0},{4,5},{5,6},{6,7},{7,4},{8,9},{9,10},{10,1... | collective-permute-start | bytes 1769480 | tf_op jit(solution)/shard_map/ppermute | solution.py:330
  72.7 14.2 %collective-permute-start.13 = (s16[4,288,256]{2,1,0:T(8,128)(2,1)S(1)}, s16[4,288,256]{2,1,0:T(8,128)(2,1)S(1)}, u32[]{:S(2)}, u32[]{:S(2)}) collective-permute-start(s16[4,288,256]{2,1,0:T(8,128)(2,1)S(1)} %get-tuple-element.68), channel_id=1, source_target_pairs={{0,3},{1,0},{2,1},{3,2},{4,7},{5,4},{6,5},{7,6},{8,11},{9,8},{10,9... | collective-permute-start | bytes 1769480 | tf_op jit(solution)/shard_map/ppermute | solution.py:330
  88.3 8.3 %collective-permute-start.14 = (s16[560,256]{1,0:T(8,128)(2,1)S(1)}, s16[560,256]{1,0:T(8,128)(2,1)S(1)}, u32[]{:S(2)}, u32[]{:S(2)}) collective-permute-start(s16[560,256]{1,0:T(8,128)(2,1)S(1)} %get-tuple-element.70), channel_id=1, source_target_pairs={{0,8},{1,9},{2,10},{3,11},{4,12},{5,13},{6,14},{7,15},{8,0},{9,1},... | collective-permute-start | bytes 860168 | tf_op jit(solution)/shard_map/ppermute | solution.py:330
  88.7 10.9 %collective-permute-start.15 = (s16[560,256]{1,0:T(8,128)(2,1)S(1)}, s16[560,256]{1,0:T(8,128)(2,1)S(1)}, u32[]{:S(2)}, u32[]{:S(2)}) collective-permute-start(s16[560,256]{1,0:T(8,128)(2,1)S(1)} %get-tuple-element.71), channel_id=1, source_target_pairs={{0,4},{1,5},{2,6},{3,7},{4,8},{5,9},{6,10},{7,11},{8,12},{9,13},{1... | collective-permute-start | bytes 860168 | tf_op jit(solution)/shard_map/ppermute | solution.py:330
  90.6 9.0 %collective-permute-start.16 = (s16[560,256]{1,0:T(8,128)(2,1)S(1)}, s16[560,256]{1,0:T(8,128)(2,1)S(1)}, u32[]{:S(2)}, u32[]{:S(2)}) collective-permute-start(s16[560,256]{1,0:T(8,128)(2,1)S(1)} %get-tuple-element.72), channel_id=1, source_target_pairs={{0,12},{1,13},{2,14},{3,15},{4,0},{5,1},{6,2},{7,3},{8,4},{9,5},{1... | collective-permute-start | bytes 860168 | tf_op jit(solution)/shard_map/ppermute | solution.py:330
  100.9 13.5 %all-to-all-start.1 = ((s16[16,16,640]{2,1,0:T(8,128)(2,1)}), s16[16,16,640]{2,1,0:T(8,128)(2,1)S(1)}, u32[]{:S(2)}, u32[]{:S(2)}) async-start(s16[16,16,640]{2,1,0:T(8,128)(2,1)} %bitcast.21), calls=%async_computation.1 | async-start | bytes 655360 | tf_op jit(solution)/shard_map/all_to_all | solution.py:397
  114.4 1.1 copy-start.1

commit v5 on v4

--- a/solution.py
+++ b/solution.py
@@ -31,8 +31,9 @@
             j = (i + gap) % NO
             first.append(i * NO + j)
             mates.append(j * NO + i)
-    first += [i * NO + i for i in range(NO // 2)]
-    mates += [i * NO + i for i in range(NO // 2, NO)]
+    at = CW // 2 - NO // 2
+    first[at:at] = [i * NO + i for i in range(NO // 2)]
+    mates[at:at] = [i * NO + i for i in range(NO // 2, NO)]
     return np.array(first, np.int32), np.array(mates, np.int32)
 
 
@@ -85,51 +86,44 @@
     return jnp.dot(matrix, high, preferred_element_type=F32) + jnp.dot(matrix, low, preferred_element_type=F32)
 
 
-def stage_kernel(order_ref, live_ref, tiles_ref, out_ref, arrived):
-    def copy(p):
-        return pltpu.make_async_copy(tiles_ref.at[order_ref[p]], out_ref.at[p], arrived.at[p])
-
-    for p in range(tiles_ref.shape[0]):
-
-        @pl.when(live_ref[p] > 0)
-        def _():
-            copy(p).start()
-
-    for p in range(tiles_ref.shape[0]):
-
-        @pl.when(live_ref[p] <= 0)
-        def _():
-            out_ref[p] = jnp.zeros(out_ref.shape[1:], out_ref.dtype)
-
-    for p in range(tiles_ref.shape[0]):
-
-        @pl.when(live_ref[p] > 0)
-        def _():
-            copy(p).wait()
-
-
-def stage(tiles, order, live):
-    smem = pl.BlockSpec(memory_space=pltpu.SMEM)
-    tiles = pltpu.with_memory_space_constraint(tiles, pltpu.HBM)
-    return pl.pallas_call(
-        stage_kernel,
-        out_shape=pltpu.VMEM(tiles.shape, tiles.dtype),
-        in_specs=[smem, smem, pl.BlockSpec(memory_space=pl.ANY)],
-        out_specs=pl.BlockSpec(memory_space=pltpu.VMEM),
-        scratch_shapes=[pltpu.SemaphoreType.DMA((tiles.shape[0],))],
-        compiler_params=pltpu.CompilerParams(vmem_limit_bytes=4 * 1024 * 1024),
-        cost_estimate=pl.CostEstimate(flops=0, bytes_accessed=tiles.size * 2, transcendentals=0),
-        name="stage",
-    )(order, live, tiles)
-
-
-def product_kernel(has_far, rows, place_ref, v_ref, rank_ref, *rest):
-    amps, outs, (first, mates, table, raw) = rest[:2], rest[2:6], rest[6:]
+def product_kernel(has_far, rows, fetch, place_ref, *rest):
+    if fetch:
+        order_ref, live_ref, tiles_ref, rank_ref = rest[:4]
+        amps, outs, v_ref, (first, mates, table, raw, arrived) = rest[4:6], rest[6:10], rest[10], rest[11:]
+    else:
+        v_ref, rank_ref = rest[:2]
+        amps, outs, (first, mates, table, raw) = rest[2:4], rest[4:8], rest[8:]
     tiles, tile, _ = v_ref.shape
     steps = tiles // 4
     half = CW // 2
     groups = SIDE * SIDE
     peer = rows // groups
+
+    def copy(p):
+        return pltpu.make_async_copy(tiles_ref.at[order_ref[p]], v_ref.at[p], arrived.at[p])
+
+    def await_tiles(step):
+        for j in range(4):
+
+            @pl.when(live_ref[step * 4 + j] > 0)
+            def _():
+                copy(step * 4 + j).wait()
+
+    if fetch:
+        for p in range(tiles):
+
+            @pl.when(live_ref[p] > 0)
+            def _():
+                copy(p).start()
+
+        def clear(p, carry):
+            @pl.when(live_ref[p] <= 0)
+            def _():
+                v_ref[p] = jnp.zeros((tile, tile), BF16)
+
+            return carry
+
+        lax.fori_loop(0, tiles, clear, 0)
 
     y, core, here, there = (place_ref[k] for k in range(4))
     depth = amps[0].shape[2]
@@ -163,10 +157,14 @@
     def columns(part):
         return pl.ds(part * half, half)
 
+    if fetch:
+        await_tiles(0)
     for part in range(2):
         raw[pl.ds(0, tile), columns(part)] = multiply(0, part)
 
     def turn(step, carry):
+        if fetch:
+            await_tiles(step)
         before = pl.multiple_of(lax.rem(step + 1, 2) * tile, tile)
         now = pl.multiple_of(lax.rem(step, 2) * tile, tile)
         held = [raw[pl.ds(before, tile), columns(part)] for part in range(2)]
@@ -199,29 +197,41 @@
     return rows + PAD * (2 if has_far else 1)
 
 
-def product(integrals, amps, ranks, place, rows, has_far):
-    tiles, tile, _ = integrals.shape
+def product(tiles, amps, ranks, place, rows, has_far, order=None, live=None):
+    count, tile, _ = tiles.shape
     groups = SIDE * SIDE
     half = CW // 2
+    fetch = order is not None
     vmem, smem = pl.BlockSpec(memory_space=pltpu.VMEM), pl.BlockSpec(memory_space=pltpu.SMEM)
-    out = (SIDE, packed_rows(rows, has_far), half)
+    out_shape = [jax.ShapeDtypeStruct((SIDE, packed_rows(rows, has_far), half), S16)] * SIDE
+    out_specs = [vmem] * SIDE
+    scratch = [
+        pltpu.VMEM((groups * rows, half), F32),
+        pltpu.VMEM((groups, groups, rows // groups, half), F32),
+        pltpu.VMEM((4 * tile, CW), BF16),
+        pltpu.VMEM((2 * tile, CW), F32),
+    ]
+    if fetch:
+        args = (place, order, live, pltpu.with_memory_space_constraint(tiles, pltpu.HBM), ranks, *amps)
+        in_specs = [smem] * 3 + [pl.BlockSpec(memory_space=pl.ANY)] + [vmem] * (1 + len(amps))
+        out_shape.append(pltpu.VMEM(tiles.shape, tiles.dtype))
+        out_specs.append(vmem)
+        scratch.append(pltpu.SemaphoreType.DMA((count,)))
+    else:
+        args = (place, tiles, ranks, *amps)
+        in_specs = [smem] + [vmem] * (2 + len(amps))
     return pl.pallas_call(
-        functools.partial(product_kernel, has_far, rows),
-        out_shape=[jax.ShapeDtypeStruct(out, S16)] * SIDE,
-        in_specs=[smem] + [vmem] * (2 + len(amps)),
-        out_specs=[vmem] * SIDE,
-        scratch_shapes=[
-            pltpu.VMEM((groups * rows, half), F32),
-            pltpu.VMEM((groups, groups, rows // groups, half), F32),
-            pltpu.VMEM((4 * tile, CW), BF16),
-            pltpu.VMEM((2 * tile, CW), F32),
-        ],
+        functools.partial(product_kernel, has_far, rows, fetch),
+        out_shape=out_shape,
+        in_specs=in_specs,
+        out_specs=out_specs,
+        scratch_shapes=scratch,
         compiler_params=pltpu.CompilerParams(vmem_limit_bytes=VMEM),
         cost_estimate=pl.CostEstimate(
-            flops=2 * tiles * tile * tile * CW, bytes_accessed=4 * tile * CW * 4, transcendentals=0
+            flops=2 * count * tile * tile * CW, bytes_accessed=4 * tile * CW * 4, transcendentals=0
         ),
         name="product",
-    )(place, integrals, ranks, *amps)
+    )(*args)
 
 
 def chunk_rows(rows, far_flags):
@@ -290,12 +300,11 @@
     back = [(slot == ranks[:, k : k + 1]).astype(F32).astype(BF16) for k in range(2)]
     mine = sort_rows(back[0], own[...])
     other = sort_rows(back[1], plain)
-    lane = lax.broadcasted_iota(S32, (rows, LANES), 1)
-    off_diagonal = lane < LANES - NO // 2
-    edge = HALF - LANES
-    joined[:, pl.ds(0, edge)] = mine[:, :edge]
-    joined[:, pl.ds(HALF, edge)] = other[:, :edge]
-    last_mine, last_other = mine[:, edge:HALF], other[:, edge:HALF]
+    joined[:, pl.ds(0, HALF)] = mine[:, :HALF]
+    joined[:, pl.ds(HALF, HALF)] = other[:, :HALF]
+    off_diagonal = lax.broadcasted_iota(S32, (rows, LANES), 1) < LANES - NO // 2
+    edge = CW // 2 - LANES
+    last_mine, last_other = mine[:, edge : edge + LANES], other[:, edge : edge + LANES]
     joined[:, pl.ds(edge, LANES)] = last_mine + jnp.where(off_diagonal, 0.0, last_other)
     joined[:, pl.ds(HALF + edge, LANES)] = jnp.where(off_diagonal, last_other, mine[:, HALF:] + other[:, HALF:])
     total = None
@@ -383,17 +392,21 @@
     order = jnp.sum(jnp.where(slots[None, :] == slot_ids[:, None], slot_ids[None, :], 0), axis=1)
     live = (order < tile_count[0, 0]).astype(S32)
 
-    tiles = stage(integrals[0, 0], order, live)
-    far_flags = tuple(c == CHUNKS - 1 for c in range(CHUNKS))
+    tiles = integrals[0, 0]
+    far_flags = tuple(c == 0 for c in range(CHUNKS))
     landed = []
     for c in range(CHUNKS):
-        sent = product(tiles, share(along[c]), ranks, place, rows, far_flags[c])
+        if c == 0:
+            *sent, tiles = product(tiles, share(along[c]), ranks, place, rows, far_flags[c], order, live)
+        else:
+            sent = product(tiles, share(along[c]), ranks, place, rows, far_flags[c])
         if c > 0:
             sent, landed = lax.optimization_barrier((sent, landed))
         if c + 1 < CHUNKS:
             sent, along[c + 1] = lax.optimization_barrier((sent, along[c + 1]))
         landed += trade(sent, 0)
     own, send = owner(trade(relay(landed, rows, far_flags), 1), rows, far_flags)
+    own = pltpu.with_memory_space_constraint(own, pltpu.HBM)
     came = lax.all_to_all(send, "col", split_axis=0, concat_axis=0, tiled=True)
     pair_sum = (occ_energy[:, None] + occ_energy[None, :]).reshape(1, OCC)
     back = jnp.stack([own_rank, mate_rank], axis=1).astype(S32)

time: 119 us -> 114 us (0.958)
  Pallas kernels: 40.2 us -> 37.5 us
    pallas_call x3 -> x2, Pallas kernels: 34.9 us -> 31 us  [product(): pl.pallas_call(functools.partial(product_kernel, has_far, rows, fetch), o...]
  transfers between devices with their start and end apart: 18 -> 18, of which waited for: 6 -> 7; matrix products, arithmetic and copies ran while one was open for 1% -> 1% of each run, Pallas kernels for 30% -> 27%
where the time goes in v5:
time: 114 us; the launch traced here: 113 us
  Pallas kernels  37.5 us (33%)
  waiting for transfers between devices  27.4 us (24%)
  starting transfers between devices  27.1 us (24%)
  blocking collectives  15.3 us (13%)
  other arithmetic  2.19 us (2%)
  matrix products  1.58 us (1%)
  local copies, waits for them, and re-layouts  1.47 us (1%)
    pallas_call x2, Pallas kernels, product(): pl.pallas_call(functools.partial(product_kernel, has_far, rows, fetch), o...  31 us
    ppermute x9, waiting for transfers between devices, trade(): got.append(lax.ppermute(pieces[k], ('row', 'col'), perm))  18.9 us
    all_to_all x1, blocking collectives, body(): lax.all_to_all(spoken, 'col', split_axis=0, concat_axis=0, tiled=True)  15.3 us
    ppermute x9, starting transfers between devices, trade(): got.append(lax.ppermute(pieces[k], ('row', 'col'), perm))  13.2 us
    ppermute x6, starting transfers between devices, fetch_along(): lax.ppermute(part, 'row', shifted_rows(k, 0))  9.49 us
    all_to_all x1, waiting for transfers between devices, body(): came = lax.all_to_all(send, 'col', split_axis=0, concat_axis=0, tiled=True)  8.23 us
    all_to_all x1, starting transfers between devices, body(): came = lax.all_to_all(send, 'col', split_axis=0, concat_axis=0, tiled=True)  4.17 us
    pallas_call x1, Pallas kernels, close(): pl.pallas_call(functools.partial(close_kernel, rows), out_shape=jax.Shape...  3.87 us
  transfers between devices with their start and end apart: 18, of which 7 were waited for; matrix products, arithmetic and copies ran while one was open for 1% of the time, Pallas kernels for 27%

profile of v5, /device:TPU:0, one launch (start us, length us, event | category | flops | bytes accessed | tf_op | source)
XLA Modules:
  0.0 113.4 jit_solution(5531659370001056157)
XLA Ops:
  0.0 1.0 copy-done
  1.0 1.6 %fusion.4 = bf16[256,1024]{1,0:T(8,128)(2,1)S(1)} fusion(bf16[256,1024]{1,0:T(8,128)(2,1)S(1)} %bitcast.34, s32[1024]{0:T(1024)} %constant.93.clone), kind=kOutput, calls=%fused_computation.6 | convolution fusion | flops 538181632 | bytes 1052672 | tf_op jit(solution)/shard_map/dot_general | solution.py:369
  2.7 1.7 %collective-permute-start = (bf16[4,64,512]{2,1,0:T(8,128)(2,1)S(1)}, bf16[4,64,512]{2,1,0:T(8,128)(2,1)S(1)}, u32[]{:S(2)}, u32[]{:S(2)}) collective-permute-start(bf16[4,64,512]{2,1,0:T(8,128)(2,1)S(1)} %bitcast.40), channel_id=1, source_target_pairs={{0,32},{16,48},{32,64},{48,80},{64,96},{80,112},{96,0},{112,16},{1... | collective-permute-start | bytes 786440 | tf_op jit(solution)/shard_map/ppermute | solution.py:348
  4.4 2.9 %collective-permute-start.1 = (bf16[4,64,512]{2,1,0:T(8,128)(2,1)S(1)}, bf16[4,64,512]{2,1,0:T(8,128)(2,1)S(1)}, u32[]{:S(2)}, u32[]{:S(2)}) collective-permute-start(bf16[4,64,512]{2,1,0:T(8,128)(2,1)S(1)} %bitcast.41), channel_id=1, source_target_pairs={{0,64},{16,80},{32,96},{48,112},{64,0},{80,16},{96,32},{112,48},{1... | collective-permute-start | bytes 786440 | tf_op jit(solution)/shard_map/ppermute | solution.py:348
  7.3 1.3 %collective-permute-start.2 = (bf16[4,64,512]{2,1,0:T(8,128)(2,1)S(1)}, bf16[4,64,512]{2,1,0:T(8,128)(2,1)S(1)}, u32[]{:S(2)}, u32[]{:S(2)}) collective-permute-start(bf16[4,64,512]{2,1,0:T(8,128)(2,1)S(1)} %bitcast.42), channel_id=1, source_target_pairs={{0,96},{16,112},{32,0},{48,16},{64,32},{80,48},{96,64},{112,80},{1... | collective-permute-start | bytes 786440 | tf_op jit(solution)/shard_map/ppermute | solution.py:348
  8.7 0.3 convert_reduce_fusion.1
  9.0 15.3 %all_to_all.20 = s32[16,1,512]{2,1,0:T(1,128)S(1)} all-to-all(s32[16,1,512]{2,1,0:T(1,128)S(1)} %broadcast_in_dim.14), channel_id=1, replica_groups=mesh['row'=8,'col'=16] {'col'}, dimensions={0} | all-to-all | bytes 65536 | tf_op jit(solution)/shard_map/all_to_all | solution.py:381
  24.3 0.0 collective-permute-done
  24.3 0.0 collective-permute-done.1
  24.3 0.1 pad_maximum_fusion.rest_4_
  24.4 0.1 collective-permute-start.3
  24.5 0.7 collective-permute-start.4
  25.3 0.8 collective-permute-start.5
  26.1 2.0 %collective-permute-start.6 = (bf16[4,64,512]{2,1,0:T(8,128)(2,1)S(1)}, bf16[4,64,512]{2,1,0:T(8,128)(2,1)}, u32[]{:S(2)}, u32[]{:S(2)}) collective-permute-start(bf16[4,64,512]{2,1,0:T(8,128)(2,1)S(1)} %bitcast.38), channel_id=1, source_target_pairs={{0,96},{16,112},{32,0},{48,16},{64,32},{80,48},{96,64},{112,80},{1... | collective-permute-start | bytes 786440 | tf_op jit(solution)/shard_map/ppermute | solution.py:348
  28.7 0.1 pad_add_fusion.3.place_ref
  28.8 0.1 select_reduce_fusion.rest_0_
  28.9 16.5 %product.2 = (s16[4,288,256]{2,1,0:T(8,128)(2,1)S(1)}, s16[4,288,256]{2,1,0:T(8,128)(2,1)S(1)}, s16[4,288,256]{2,1,0:T(8,128)(2,1)S(1)}, s16[4,288,256]{2,1,0:T(8,128)(2,1)S(1)}, bf16[32,512,512]{2,1,0:T(8,128)(2,1)S(1)}) custom-call(s32[4]{0:T(128)S(1)} %pad_add_fusion.3.place_ref, s32[32]{0:T(128)S(1)} %select_reduce_fusion.rest_0_, ...), custom_call_target="tpu_custom_call" | custom-call | flops 8589934592 | bytes 4194304 | tf_op jit(solution)/shard_map/product/pallas_call | solution.py:223
  45.5 1.1 pad_maximum_fusion.1.rest_2_
  46.5 0.1 collective-permute-start.7
  46.6 1.0 collective-permute-start.10
  47.6 1.5 %collective-permute-start.8 = (s16[4,288,256]{2,1,0:T(8,128)(2,1)S(1)}, s16[4,288,256]{2,1,0:T(8,128)(2,1)S(1)}, u32[]{:S(2)}, u32[]{:S(2)}) collective-permute-start(s16[4,288,256]{2,1,0:T(8,128)(2,1)S(1)} %get-tuple-element.60), channel_id=1, source_target_pairs={{0,2},{1,3},{2,0},{3,1},{4,6},{5,7},{6,4},{7,5},{8,10},{9,11},{10,... | collective-permute-start | bytes 1769480 | tf_op jit(solution)/shard_map/ppermute | solution.py:339
  49.1 0.0 collective-permute-start.9
  49.1 0.2 collective-permute-done.7.rest_3_
  49.3 14.5 %product.3 = (s16[4,272,256]{2,1,0:T(8,128)(2,1)S(1)}, s16[4,272,256]{2,1,0:T(8,128)(2,1)S(1)}, s16[4,272,256]{2,1,0:T(8,128)(2,1)S(1)}, s16[4,272,256]{2,1,0:T(8,128)(2,1)S(1)}) custom-call(s32[4]{0:T(128)S(1)} %pad_add_fusion.3.place_ref, bf16[32,512,512]{2,1,0:T(8,128)(2,1)S(1)} %get-tuple-element.46.rest_0_, ...), custom_call_target="tpu_custom_call" | custom-call | flops 8589934592 | bytes 4194304 | tf_op jit(solution)/shard_map/product/pallas_call | solution.py:223
  63.8 0.0 copy-start.2
  63.8 0.0 copy-start.3
  63.8 0.0 copy-start.1
  63.8 1.5 %collective-permute-done.9.refs_2_ = s16[4,288,256]{2,1,0:T(8,128)(2,1)S(1)} collective-permute-done((s16[4,288,256]{2,1,0:T(8,128)(2,1)S(1)}, s16[4,288,256]{2,1,0:T(8,128)(2,1)S(1)}, u32[]{:S(2)}, u32[]{:S(2)}) %collective-permute-start.9) | collective-permute-done | bytes 589856 | tf_op jit(solution)/shard_map/ppermute | solution.py:339
  65.3 2.2 %collective-permute-start.11 = (s16[4,272,256]{2,1,0:T(8,128)(2,1)S(1)}, s16[4,272,256]{2,1,0:T(8,128)(2,1)S(1)}, u32[]{:S(2)}, u32[]{:S(2)}) collective-permute-start(s16[4,272,256]{2,1,0:T(8,128)(2,1)S(1)} %get-tuple-element.68), channel_id=1, source_target_pairs={{0,2},{1,3},{2,0},{3,1},{4,6},{5,7},{6,4},{7,5},{8,10},{9,11},{10,... | collective-permute-start | bytes 1671176 | tf_op jit(solution)/shard_map/ppermute | solution.py:339
  67.5 0.3 collective-permute-start.12
  67.8 2.9 %collective-permute-start.13 = (s16[4,272,256]{2,1,0:T(8,128)(2,1)S(1)}, s16[4,272,256]{2,1,0:T(8,128)(2,1)S(1)}, u32[]{:S(2)}, u32[]{:S(2)}) collective-permute-start(s16[4,272,256]{2,1,0:T(8,128)(2,1)S(1)} %get-tuple-element.70), channel_id=1, source_target_pairs={{0,3},{1,0},{2,1},{3,2},{4,7},{5,4},{6,5},{7,6},{8,11},{9,8},{10,9... | collective-permute-start | bytes 1671176 | tf_op jit(solution)/shard_map/ppermute | solution.py:339
  70.7 5.7 %collective-permute-done.11.refs_5_ = s16[4,272,256]{2,1,0:T(8,128)(2,1)S(1)} collective-permute-done((s16[4,272,256]{2,1,0:T(8,128)(2,1)S(1)}, s16[4,272,256]{2,1,0:T(8,128)(2,1)S(1)}, u32[]{:S(2)}, u32[]{:S(2)}) %collective-permute-start.11) | collective-permute-done | bytes 557088 | tf_op jit(solution)/shard_map/ppermute | solution.py:339
  76.5 5.9 %collective-permute-done.12.refs_6_ = s16[4,272,256]{2,1,0:T(8,128)(2,1)S(1)} collective-permute-done((s16[4,272,256]{2,1,0:T(8,128)(2,1)S(1)}, s16[4,272,256]{2,1,0:T(8,128)(2,1)S(1)}, u32[]{:S(2)}, u32[]{:S(2)}) %collective-permute-start.12) | collective-permute-done | bytes 557088 | tf_op jit(solution)/shard_map/ppermute | solution.py:339
  82.3 1.4 %relay.1 = (s16[560,256]{1,0:T(8,128)(2,1)S(1)}, s16[560,256]{1,0:T(8,128)(2,1)S(1)}, s16[560,256]{1,0:T(8,128)(2,1)S(1)}, s16[560,256]{1,0:T(8,128)(2,1)S(1)}) custom-call(s16[4,288,256]{2,1,0:T(8,128)(2,1)S(1)} %get-tuple-element.63.refs_0_, s16[4,288,256]{2,1,0:T(8,128)(2,1)S(1)} %collective-permute-done.8.refs_1_, ...), custom_call_target="tpu_custom_call" | custom-call | tf_op jit(solution)/shard_map/relay/pallas_call | solution.py:254
  83.7 2.2 %collective-permute-start.14 = (s16[560,256]{1,0:T(8,128)(2,1)S(1)}, s16[560,256]{1,0:T(8,128)(2,1)S(1)}, u32[]{:S(2)}, u32[]{:S(2)}) collective-permute-start(s16[560,256]{1,0:T(8,128)(2,1)S(1)} %get-tuple-element.72), channel_id=1, source_target_pairs={{0,8},{1,9},{2,10},{3,11},{4,12},{5,13},{6,14},{7,15},{8,0},{9,1},... | collective-permute-start | bytes 860168 | tf_op jit(solution)/shard_map/ppermute | solution.py:339
  85.9 0.9 collective-permute-start.15
  86.8 2.4 %collective-permute-start.16 = (s16[560,256]{1,0:T(8,128)(2,1)S(1)}, s16[560,256]{1,0:T(8,128)(2,1)S(1)}, u32[]{:S(2)}, u32[]{:S(2)}) collective-permute-start(s16[560,256]{1,0:T(8,128)(2,1)S(1)} %get-tuple-element.74), channel_id=1, source_target_pairs={{0,12},{1,13},{2,14},{3,15},{4,0},{5,1},{6,2},{7,3},{8,4},{9,5},{1... | collective-permute-start | bytes 860168 | tf_op jit(solution)/shard_map/ppermute | solution.py:339
  89.1 0.1 broadcast_add_fusion
  89.2 2.9 %collective-permute-done.14.refs_1_ = s16[560,256]{1,0:T(8,128)(2,1)S(1)} collective-permute-done((s16[560,256]{1,0:T(8,128)(2,1)S(1)}, s16[560,256]{1,0:T(8,128)(2,1)S(1)}, u32[]{:S(2)}, u32[]{:S(2)}) %collective-permute-start.14) | collective-permute-done | bytes 286752 | tf_op jit(solution)/shard_map/ppermute | solution.py:339
  92.1 3.0 %collective-permute-done.15.refs_2_ = s16[560,256]{1,0:T(8,128)(2,1)S(1)} collective-permute-done((s16[560,256]{1,0:T(8,128)(2,1)S(1)}, s16[560,256]{1,0:T(8,128)(2,1)S(1)}, u32[]{:S(2)}, u32[]{:S(2)}) %collective-permute-start.15) | collective-permute-done | bytes 286752 | tf_op jit(solution)/shard_map/ppermute | solution.py:339
  95.0 1.2 %owner.1 = (f32[256,640]{1,0:T(8,128)}, s16[256,640]{1,0:T(8,128)(2,1)}) custom-call(s16[560,256]{1,0:T(8,128)(2,1)S(1)} %get-tuple-element.71.refs_0_, s16[560,256]{1,0:T(8,128)(2,1)S(1)} %collective-permute-done.14.refs_1_, s16[560,256]{1,0:T(8,128)(2,1)S(1)} %collective-permute-done.15.refs_2_, s16[560,256]{1,0:T(8,128)(2,1)S(1)} %collective-permute-done.16.refs_3_), custom_call_target="tpu_custom_call" | custom-call | tf_op jit(solution)/shard_map/owner/pallas_call | solution.py:285
  96.3 4.2 %all-to-all-start.1 = ((s16[16,16,640]{2,1,0:T(8,128)(2,1)}), s16[16,16,640]{2,1,0:T(8,128)(2,1)S(1)}, u32[]{:S(2)}, u32[]{:S(2)}) async-start(s16[16,16,640]{2,1,0:T(8,128)(2,1)} %bitcast.21), calls=%async_computation.1 | async-start | bytes 655360 | tf_op jit(solution)/shard_map/all_to_all | solution.py:410
  100.5 0.1 copy.15.ranks
  100.6 0.1 copy.16.energy
  100.8 0.1 add.58.pair_sum
  100.8 0.4 fusion.1.spread
  101.3 8.2 %all-to-all-done.1 = s16[16,16,640]{2,1,0:T(8,128)(2,1)S(1)} async-done(((s16[16,16,640]{2,1,0:T(8,128)(2,1)}), s16[16,16,640]{2,1,0:T(8,128)(2,1)S(1)}, u32[]{:S(2)}, u32[]{:S(2)}) %all-to-all-start.1) | async-done | bytes 327712 | tf_op jit(solution)/shard_map/all_to_all | solution.py:410
  109.5 3.9 %close.1 = f32[256,1024]{1,0:T(8,128)} custom-call(f32[256,640]{1,0:T(8,128)} %get-tuple-element.75.own, s16[256,640]{1,0:T(8,128)(2,1)S(1)} %bitcast.35, s32[256,2]{1,0:T(8,128)S(1)} %copy.15.ranks, f32[256,1]{1,0:T(8,128)S(1)} %copy.16.energy, f32[1,1024]{1,0:T(1,128)S(1)} %add.58.pair_sum, bf16[1024,1024]{1,0:T(8,128)(2,1)S(1)} %fusion.1.spread), custom_call_target="tpu_custom_call" | custom-call | tf_op jit(solution)/shard_map/close/pallas_call | solution.py:319
  (27 shorter events, 0.2 us)
Async XLA Ops:
  0.0 1.0 copy-start
  0.0 8.7 %copy-start.4 = (s32[256]{0:T(256)S(1)}, s32[256]{0:T(256)}, u32[]{:S(2)}) copy-start(s32[256]{0:T(256)} %param.15) | copy-start | bytes 3076
  0.0 28.8 %copy-start.5 = (s32[1,1,32]{2,1,0:T(1,128)S(1)}, s32[1,1,32]{2,1,0:T(1,128)}, u32[]{:S(2)}) copy-start(s32[1,1,32]{2,1,0:T(1,128)} %param.11) | copy-start | bytes 388
  2.7 21.6 %collective-permute-start = (bf16[4,64,512]{2,1,0:T(8,128)(2,1)S(1)}, bf16[4,64,512]{2,1,0:T(8,128)(2,1)S(1)}, u32[]{:S(2)}, u32[]{:S(2)}) collective-permute-start(bf16[4,64,512]{2,1,0:T(8,128)(2,1)S(1)} %bitcast.40), channel_id=1, source_target_pairs={{0,32},{16,48},{32,64},{48,80},{64,96},{80,112},{96,0},{112,16},{1... | collective-permute-start | bytes 786440 | tf_op jit(solution)/shard_map/ppermute | solution.py:348
  4.4 19.9 %collective-permute-start.1 = (bf16[4,64,512]{2,1,0:T(8,128)(2,1)S(1)}, bf16[4,64,512]{2,1,0:T(8,128)(2,1)S(1)}, u32[]{:S(2)}, u32[]{:S(2)}) collective-permute-start(bf16[4,64,512]{2,1,0:T(8,128)(2,1)S(1)} %bitcast.41), channel_id=1, source_target_pairs={{0,64},{16,80},{32,96},{48,112},{64,0},{80,16},{96,32},{112,48},{1... | collective-permute-start | bytes 786440 | tf_op jit(solution)/shard_map/ppermute | solution.py:348
  7.3 17.0 %collective-permute-start.2 = (bf16[4,64,512]{2,1,0:T(8,128)(2,1)S(1)}, bf16[4,64,512]{2,1,0:T(8,128)(2,1)S(1)}, u32[]{:S(2)}, u32[]{:S(2)}) collective-permute-start(bf16[4,64,512]{2,1,0:T(8,128)(2,1)S(1)} %bitcast.42), channel_id=1, source_target_pairs={{0,96},{16,112},{32,0},{48,16},{64,32},{80,48},{96,64},{112,80},{1... | collective-permute-start | bytes 786440 | tf_op jit(solution)/shard_map/ppermute | solution.py:348
  24.4 4.5 %collective-permute-start.3 = (bf16[4,4,64,512]{3,2,1,0:T(8,128)(2,1)S(1)}, bf16[4,4,64,512]{3,2,1,0:T(8,128)(2,1)S(1)}, u32[]{:S(2)}, u32[]{:S(2)}) collective-permute-start(bf16[4,4,64,512]{3,2,1,0:T(8,128)(2,1)S(1)} %pad_maximum_fusion.rest_4_), channel_id=1, source_target_pairs={{0,16},{16,0},{32,48},{48,32},{64,80},{80,64},{96,112},{112,96},{1... | collective-permute-start | bytes 3145736 | tf_op jit(solution)/shard_map/ppermute | solution.py:353
  24.5 20.9 %collective-permute-start.4 = (bf16[4,64,512]{2,1,0:T(8,128)(2,1)S(1)}, bf16[4,64,512]{2,1,0:T(8,128)(2,1)S(1)}, u32[]{:S(2)}, u32[]{:S(2)}) collective-permute-start(bf16[4,64,512]{2,1,0:T(8,128)(2,1)S(1)} %bitcast.36), channel_id=1, source_target_pairs={{0,32},{16,48},{32,64},{48,80},{64,96},{80,112},{96,0},{112,16},{1... | collective-permute-start | bytes 786440 | tf_op jit(solution)/shard_map/ppermute | solution.py:348
  25.3 20.2 %collective-permute-start.5 = (bf16[4,64,512]{2,1,0:T(8,128)(2,1)S(1)}, bf16[4,64,512]{2,1,0:T(8,128)(2,1)S(1)}, u32[]{:S(2)}, u32[]{:S(2)}) collective-permute-start(bf16[4,64,512]{2,1,0:T(8,128)(2,1)S(1)} %bitcast.37), channel_id=1, source_target_pairs={{0,64},{16,80},{32,96},{48,112},{64,0},{80,16},{96,32},{112,48},{1... | collective-permute-start | bytes 786440 | tf_op jit(solution)/shard_map/ppermute | solution.py:348
  26.1 19.4 %collective-permute-start.6 = (bf16[4,64,512]{2,1,0:T(8,128)(2,1)S(1)}, bf16[4,64,512]{2,1,0:T(8,128)(2,1)}, u32[]{:S(2)}, u32[]{:S(2)}) collective-permute-start(bf16[4,64,512]{2,1,0:T(8,128)(2,1)S(1)} %bitcast.38), channel_id=1, source_target_pairs={{0,96},{16,112},{32,0},{48,16},{64,32},{80,48},{96,64},{112,80},{1... | collective-permute-start | bytes 786440 | tf_op jit(solution)/shard_map/ppermute | solution.py:348
  46.5 2.7 %collective-permute-start.7 = (bf16[4,4,64,512]{3,2,1,0:T(8,128)(2,1)S(1)}, bf16[4,4,64,512]{3,2,1,0:T(8,128)(2,1)S(1)}, u32[]{:S(2)}, u32[]{:S(2)}) collective-permute-start(bf16[4,4,64,512]{3,2,1,0:T(8,128)(2,1)S(1)} %pad_maximum_fusion.1.rest_2_), channel_id=1, source_target_pairs={{0,16},{16,0},{32,48},{48,32},{64,80},{80,64},{96,112},{112,96},{1... | collective-permute-start | bytes 3145736 | tf_op jit(solution)/shard_map/ppermute | solution.py:353
  46.6 17.2 %collective-permute-start.10 = (s16[4,288,256]{2,1,0:T(8,128)(2,1)S(1)}, s16[4,288,256]{2,1,0:T(8,128)(2,1)S(1)}, u32[]{:S(2)}, u32[]{:S(2)}) collective-permute-start(s16[4,288,256]{2,1,0:T(8,128)(2,1)S(1)} %get-tuple-element.62), channel_id=1, source_target_pairs={{0,3},{1,0},{2,1},{3,2},{4,7},{5,4},{6,5},{7,6},{8,11},{9,8},{10,9... | collective-permute-start | bytes 1769480 | tf_op jit(solution)/shard_map/ppermute | solution.py:339
  47.6 16.2 %collective-permute-start.8 = (s16[4,288,256]{2,1,0:T(8,128)(2,1)S(1)}, s16[4,288,256]{2,1,0:T(8,128)(2,1)S(1)}, u32[]{:S(2)}, u32[]{:S(2)}) collective-permute-start(s16[4,288,256]{2,1,0:T(8,128)(2,1)S(1)} %get-tuple-element.60), channel_id=1, source_target_pairs={{0,2},{1,3},{2,0},{3,1},{4,6},{5,7},{6,4},{7,5},{8,10},{9,11},{10,... | collective-permute-start | bytes 1769480 | tf_op jit(solution)/shard_map/ppermute | solution.py:339
  49.1 16.2 %collective-permute-start.9 = (s16[4,288,256]{2,1,0:T(8,128)(2,1)S(1)}, s16[4,288,256]{2,1,0:T(8,128)(2,1)S(1)}, u32[]{:S(2)}, u32[]{:S(2)}) collective-permute-start(s16[4,288,256]{2,1,0:T(8,128)(2,1)S(1)} %get-tuple-element.61), channel_id=1, source_target_pairs={{0,1},{1,2},{2,3},{3,0},{4,5},{5,6},{6,7},{7,4},{8,9},{9,10},{10,1... | collective-permute-start | bytes 1769480 | tf_op jit(solution)/shard_map/ppermute | solution.py:339
  63.8 25.4 %copy-start.2 = (f32[32]{0:T(128)S(1)}, f32[32]{0:T(128)}, u32[]{:S(2)}) copy-start(f32[32]{0:T(128)} %param.14) | copy-start | bytes 388
  63.8 36.8 %copy-start.3 = (f32[256]{0:T(256)S(1)}, f32[256]{0:T(256)}, u32[]{:S(2)}) copy-start(f32[256]{0:T(256)} %param.13) | copy-start | bytes 3076
  63.8 37.1 %copy-start.1 = (s32[1024]{0:T(1024)S(1)}, s32[1024]{0:T(1024)}, u32[]{:S(2)}) copy-start(s32[1024]{0:T(1024)} %constant.94.clone) | copy-start | bytes 12292
  65.3 11.1 %collective-permute-start.11 = (s16[4,272,256]{2,1,0:T(8,128)(2,1)S(1)}, s16[4,272,256]{2,1,0:T(8,128)(2,1)S(1)}, u32[]{:S(2)}, u32[]{:S(2)}) collective-permute-start(s16[4,272,256]{2,1,0:T(8,128)(2,1)S(1)} %get-tuple-element.68), channel_id=1, source_target_pairs={{0,2},{1,3},{2,0},{3,1},{4,6},{5,7},{6,4},{7,5},{8,10},{9,11},{10,... | collective-permute-start | bytes 1671176 | tf_op jit(solution)/shard_map/ppermute | solution.py:339
  67.5 14.8 %collective-permute-start.12 = (s16[4,272,256]{2,1,0:T(8,128)(2,1)S(1)}, s16[4,272,256]{2,1,0:T(8,128)(2,1)S(1)}, u32[]{:S(2)}, u32[]{:S(2)}) collective-permute-start(s16[4,272,256]{2,1,0:T(8,128)(2,1)S(1)} %get-tuple-element.69), channel_id=1, source_target_pairs={{0,1},{1,2},{2,3},{3,0},{4,5},{5,6},{6,7},{7,4},{8,9},{9,10},{10,1... | collective-permute-start | bytes 1671176 | tf_op jit(solution)/shard_map/ppermute | solution.py:339
  67.8 14.5 %collective-permute-start.13 = (s16[4,272,256]{2,1,0:T(8,128)(2,1)S(1)}, s16[4,272,256]{2,1,0:T(8,128)(2,1)S(1)}, u32[]{:S(2)}, u32[]{:S(2)}) collective-permute-start(s16[4,272,256]{2,1,0:T(8,128)(2,1)S(1)} %get-tuple-element.70), channel_id=1, source_target_pairs={{0,3},{1,0},{2,1},{3,2},{4,7},{5,4},{6,5},{7,6},{8,11},{9,8},{10,9... | collective-permute-start | bytes 1671176 | tf_op jit(solution)/shard_map/ppermute | solution.py:339
  83.7 8.3 %collective-permute-start.14 = (s16[560,256]{1,0:T(8,128)(2,1)S(1)}, s16[560,256]{1,0:T(8,128)(2,1)S(1)}, u32[]{:S(2)}, u32[]{:S(2)}) collective-permute-start(s16[560,256]{1,0:T(8,128)(2,1)S(1)} %get-tuple-element.72), channel_id=1, source_target_pairs={{0,8},{1,9},{2,10},{3,11},{4,12},{5,13},{6,14},{7,15},{8,0},{9,1},... | collective-permute-start | bytes 860168 | tf_op jit(solution)/shard_map/ppermute | solution.py:339
  85.9 9.1 %collective-permute-start.15 = (s16[560,256]{1,0:T(8,128)(2,1)S(1)}, s16[560,256]{1,0:T(8,128)(2,1)S(1)}, u32[]{:S(2)}, u32[]{:S(2)}) collective-permute-start(s16[560,256]{1,0:T(8,128)(2,1)S(1)} %get-tuple-element.73), channel_id=1, source_target_pairs={{0,4},{1,5},{2,6},{3,7},{4,8},{5,9},{6,10},{7,11},{8,12},{9,13},{1... | collective-permute-start | bytes 860168 | tf_op jit(solution)/shard_map/ppermute | solution.py:339
  86.8 8.3 %collective-permute-start.16 = (s16[560,256]{1,0:T(8,128)(2,1)S(1)}, s16[560,256]{1,0:T(8,128)(2,1)S(1)}, u32[]{:S(2)}, u32[]{:S(2)}) collective-permute-start(s16[560,256]{1,0:T(8,128)(2,1)S(1)} %get-tuple-element.74), channel_id=1, source_target_pairs={{0,12},{1,13},{2,14},{3,15},{4,0},{5,1},{6,2},{7,3},{8,4},{9,5},{1... | collective-permute-start | bytes 860168 | tf_op jit(solution)/shard_map/ppermute | solution.py:339
  96.3 13.2 %all-to-all-start.1 = ((s16[16,16,640]{2,1,0:T(8,128)(2,1)}), s16[16,16,640]{2,1,0:T(8,128)(2,1)S(1)}, u32[]{:S(2)}, u32[]{:S(2)}) async-start(s16[16,16,640]{2,1,0:T(8,128)(2,1)} %bitcast.21), calls=%async_computation.1 | async-start | bytes 655360 | tf_op jit(solution)/shard_map/all_to_all | solution.py:410

commit v6 on v5

--- a/solution.py
+++ b/solution.py
@@ -20,7 +20,7 @@
 LOG_GRID = 200.0
 FULL = 32760.0
 TINY = 1e-37
-VMEM = 20 * 1024 * 1024
+VMEM = 16 * 1024 * 1024
 SMALL = 16 * 1024 * 1024
 
 
@@ -102,6 +102,13 @@
     def copy(p):
         return pltpu.make_async_copy(tiles_ref.at[order_ref[p]], v_ref.at[p], arrived.at[p])
 
+    def request_tiles(step):
+        for j in range(4):
+
+            @pl.when(live_ref[step * 4 + j] > 0)
+            def _():
+                copy(step * 4 + j).start()
+
     def await_tiles(step):
         for j in range(4):
 
@@ -110,11 +117,7 @@
                 copy(step * 4 + j).wait()
 
     if fetch:
-        for p in range(tiles):
-
-            @pl.when(live_ref[p] > 0)
-            def _():
-                copy(p).start()
+        request_tiles(0)
 
         def clear(p, carry):
             @pl.when(live_ref[p] <= 0)
@@ -158,12 +161,18 @@
         return pl.ds(part * half, half)
 
     if fetch:
+        request_tiles(1)
         await_tiles(0)
     for part in range(2):
         raw[pl.ds(0, tile), columns(part)] = multiply(0, part)
 
     def turn(step, carry):
         if fetch:
+
+            @pl.when(step + 1 < steps)
+            def _():
+                request_tiles(step + 1)
+
             await_tiles(step)
         before = pl.multiple_of(lax.rem(step + 1, 2) * tile, tile)
         now = pl.multiple_of(lax.rem(step, 2) * tile, tile)
@@ -292,39 +301,51 @@
     )(*came)
 
 
-def close_kernel(rows, own, came, ranks, energy, pair_sum, spread, out, joined):
+def back_to_place(ranks, values):
+    rows = values.shape[0]
+    matrix = (lax.broadcasted_iota(S32, (rows, rows), 1) == ranks).astype(F32).astype(BF16)
+    return sort_rows(matrix, values)
+
+
+def place_columns(values, spread):
+    high, low = halves(values)
+    return jnp.dot(high, spread, preferred_element_type=F32) + jnp.dot(low, spread, preferred_element_type=F32)
+
+
+def mine_kernel(own, ranks, spread, out):
+    mine = back_to_place(ranks[:, 0:1], own[...])
+    at = HALF + CW // 2 - LANES
+    out[...] = place_columns(mine[:, :HALF], spread[pl.ds(0, HALF), :]) + place_columns(
+        mine[:, HALF:], spread[pl.ds(at, LANES), :]
+    )
+
+
+def close_kernel(mine, came, ranks, energy, pair_sum, spread, out):
     heads = came[:, pl.ds(HALF, LANES)].astype(S32).astype(F32)
     scale = jnp.exp2(heads[:, 0:1] * (1.0 / LOG_GRID)) * (1.0 / FULL)
-    plain = came[...].astype(S32).astype(F32) * scale
-    slot = lax.broadcasted_iota(S32, (rows, rows), 1)
-    back = [(slot == ranks[:, k : k + 1]).astype(F32).astype(BF16) for k in range(2)]
-    mine = sort_rows(back[0], own[...])
-    other = sort_rows(back[1], plain)
-    joined[:, pl.ds(0, HALF)] = mine[:, :HALF]
-    joined[:, pl.ds(HALF, HALF)] = other[:, :HALF]
-    off_diagonal = lax.broadcasted_iota(S32, (rows, LANES), 1) < LANES - NO // 2
+    other = back_to_place(ranks[:, 1:2], came[...].astype(S32).astype(F32) * scale)
     edge = CW // 2 - LANES
-    last_mine, last_other = mine[:, edge : edge + LANES], other[:, edge : edge + LANES]
-    joined[:, pl.ds(edge, LANES)] = last_mine + jnp.where(off_diagonal, 0.0, last_other)
-    joined[:, pl.ds(HALF + edge, LANES)] = jnp.where(off_diagonal, last_other, mine[:, HALF:] + other[:, HALF:])
-    total = None
-    for part in halves(joined[...]):
-        add = jnp.dot(part, spread[...], preferred_element_type=F32)
-        total = add if total is None else total + add
-    out[...] = total / (energy[...] - pair_sum[...])
-
-
-def close(own, came, ranks, energy, pair_sum, spread, rows):
+    last = other[:, edge : edge + LANES]
+    off_diagonal = lax.broadcasted_iota(S32, last.shape, 1) < LANES - NO // 2
+    mates = jnp.concatenate(
+        [other[:, :edge], jnp.where(off_diagonal, last, other[:, HALF:]), other[:, edge + LANES : HALF]], axis=1
+    )
+    total = place_columns(mates, spread[pl.ds(HALF, HALF), :])
+    total = total + place_columns(jnp.where(off_diagonal, 0.0, last), spread[pl.ds(edge, LANES), :])
+    out[...] = (mine[...] + total) / (energy[...] - pair_sum[...])
+
+
+def last_call(kernel, name, args, result):
     vmem = pl.BlockSpec(memory_space=pltpu.VMEM)
     return pl.pallas_call(
-        functools.partial(close_kernel, rows),
-        out_shape=jax.ShapeDtypeStruct((rows, OCC), F32),
-        in_specs=[vmem] * 6,
+        kernel,
+        out_shape=result,
+        in_specs=[vmem] * len(args),
         out_specs=vmem,
-        scratch_shapes=[pltpu.VMEM((rows, OCC), F32)],
         compiler_params=pltpu.CompilerParams(vmem_limit_bytes=SMALL),
-        name="close",
-    )(own, came, ranks, energy, pair_sum, spread)
+        cost_estimate=pl.CostEstimate(flops=4 * OCC**3 // 4, bytes_accessed=2 * OCC * OCC, transcendentals=0),
+        name=name,
+    )(*args)
 
 
 def trade(pieces, x_core):
@@ -345,7 +366,8 @@
 
 
 def fetch_along(part):
-    return [part] + [lax.ppermute(part, "row", shifted_rows(k, 0)) for k in range(1, SIDE)]
+    far, next_to, last = (lax.ppermute(part, "row", shifted_rows(k, 0)) for k in (2, 1, 3))
+    return [part, next_to, far, last]
 
 
 def share(along):
@@ -406,11 +428,14 @@
             sent, along[c + 1] = lax.optimization_barrier((sent, along[c + 1]))
         landed += trade(sent, 0)
     own, send = owner(trade(relay(landed, rows, far_flags), 1), rows, far_flags)
-    own = pltpu.with_memory_space_constraint(own, pltpu.HBM)
     came = lax.all_to_all(send, "col", split_axis=0, concat_axis=0, tiled=True)
     pair_sum = (occ_energy[:, None] + occ_energy[None, :]).reshape(1, OCC)
     back = jnp.stack([own_rank, mate_rank], axis=1).astype(S32)
-    return close(own, came, back, pair_energy[:, None], pair_sum, spread, rows)
+    own = pltpu.with_memory_space_constraint(own, pltpu.HBM)
+    mine = last_call(mine_kernel, "mine", (own, back, spread), pltpu.HBM((rows, OCC), F32))
+    mine = pltpu.with_memory_space_constraint(mine, pltpu.HBM)
+    args = (mine, came, back, pair_energy[:, None], pair_sum, spread)
+    return last_call(close_kernel, "close", args, jax.ShapeDtypeStruct((rows, OCC), F32))
 
 
 def solution(mesh):

time: 114 us -> 114 us (level)
  Pallas kernels: 37.5 us -> 40.6 us
  waiting for transfers between devices: 27.4 us -> 25.1 us
    pallas_call x1 -> x2, Pallas kernels: 3.87 us -> 6.99 us  [last_call(): pl.pallas_call(kernel, out_shape=result, in_specs=[vmem] * len(args), out...]
    all_to_all x1, waiting for transfers between devices: 8.23 us -> 5.23 us  [body(): came = lax.all_to_all(send, 'col', split_axis=0, concat_axis=0, tiled=True)]
  transfers between devices with their start and end apart: 18 -> 18, of which waited for: 7 -> 6; matrix products, arithmetic and copies ran while one was open for 1% -> 1% of each run, Pallas kernels for 27% -> 30%
where the time goes in v6:
time: 114 us; the launch traced here: 113 us
  Pallas kernels  40.6 us (36%)
  starting transfers between devices  26.1 us (23%)
  waiting for transfers between devices  25.1 us (22%)
  blocking collectives  15.3 us (13%)
  other arithmetic  2.19 us (2%)
  matrix products  1.58 us (1%)
  local copies, waits for them, and re-layouts  1.48 us (1%)
    pallas_call x2, Pallas kernels, product(): pl.pallas_call(functools.partial(product_kernel, has_far, rows, fetch), o...  31 us
    ppermute x9, waiting for transfers between devices, trade(): got.append(lax.ppermute(pieces[k], ('row', 'col'), perm))  19.9 us
    all_to_all x1, blocking collectives, body(): lax.all_to_all(spoken, 'col', split_axis=0, concat_axis=0, tiled=True)  15.3 us
    ppermute x9, starting transfers between devices, trade(): got.append(lax.ppermute(pieces[k], ('row', 'col'), perm))  12.6 us
    ppermute x6, starting transfers between devices, fetch_along(): lax.ppermute(part, 'row', shifted_rows(k, 0))  9.49 us
    pallas_call x2, Pallas kernels, last_call(): pl.pallas_call(kernel, out_shape=result, in_specs=[vmem] * len(args), out...  6.99 us
    all_to_all x1, waiting for transfers between devices, body(): came = lax.all_to_all(send, 'col', split_axis=0, concat_axis=0, tiled=True)  5.23 us
    all_to_all x1, starting transfers between devices, body(): came = lax.all_to_all(send, 'col', split_axis=0, concat_axis=0, tiled=True)  3.84 us
  transfers between devices with their start and end apart: 18, of which 6 were waited for; matrix products, arithmetic and copies ran while one was open for 1% of the time, Pallas kernels for 30%

profile of v6, /device:TPU:0, one launch (start us, length us, event | category | flops | bytes accessed | tf_op | source)
XLA Modules:
  0.0 113.3 jit_solution(9870626098421367905)
XLA Ops:
  0.0 1.0 copy-done
  1.0 1.6 %fusion.4 = bf16[256,1024]{1,0:T(8,128)(2,1)S(1)} fusion(bf16[256,1024]{1,0:T(8,128)(2,1)S(1)} %bitcast.34, s32[1024]{0:T(1024)} %constant.93.clone), kind=kOutput, calls=%fused_computation.6 | convolution fusion | flops 538181632 | bytes 1052672 | tf_op jit(solution)/shard_map/dot_general | solution.py:391
  2.7 1.7 %collective-permute-start = (bf16[4,64,512]{2,1,0:T(8,128)(2,1)S(1)}, bf16[4,64,512]{2,1,0:T(8,128)(2,1)S(1)}, u32[]{:S(2)}, u32[]{:S(2)}) collective-permute-start(bf16[4,64,512]{2,1,0:T(8,128)(2,1)S(1)} %bitcast.40), channel_id=1, source_target_pairs={{0,32},{16,48},{32,64},{48,80},{64,96},{80,112},{96,0},{112,16},{1... | collective-permute-start | bytes 786440 | tf_op jit(solution)/shard_map/ppermute | solution.py:369
  4.4 2.9 %collective-permute-start.1 = (bf16[4,64,512]{2,1,0:T(8,128)(2,1)S(1)}, bf16[4,64,512]{2,1,0:T(8,128)(2,1)S(1)}, u32[]{:S(2)}, u32[]{:S(2)}) collective-permute-start(bf16[4,64,512]{2,1,0:T(8,128)(2,1)S(1)} %bitcast.41), channel_id=1, source_target_pairs={{0,64},{16,80},{32,96},{48,112},{64,0},{80,16},{96,32},{112,48},{1... | collective-permute-start | bytes 786440 | tf_op jit(solution)/shard_map/ppermute | solution.py:369
  7.3 1.3 %collective-permute-start.2 = (bf16[4,64,512]{2,1,0:T(8,128)(2,1)S(1)}, bf16[4,64,512]{2,1,0:T(8,128)(2,1)S(1)}, u32[]{:S(2)}, u32[]{:S(2)}) collective-permute-start(bf16[4,64,512]{2,1,0:T(8,128)(2,1)S(1)} %bitcast.42), channel_id=1, source_target_pairs={{0,96},{16,112},{32,0},{48,16},{64,32},{80,48},{96,64},{112,80},{1... | collective-permute-start | bytes 786440 | tf_op jit(solution)/shard_map/ppermute | solution.py:369
  8.7 0.3 convert_reduce_fusion.1
  9.0 15.3 %all_to_all.20 = s32[16,1,512]{2,1,0:T(1,128)S(1)} all-to-all(s32[16,1,512]{2,1,0:T(1,128)S(1)} %broadcast_in_dim.14), channel_id=1, replica_groups=mesh['row'=8,'col'=16] {'col'}, dimensions={0} | all-to-all | bytes 65536 | tf_op jit(solution)/shard_map/all_to_all | solution.py:403
  24.3 0.1 pad_maximum_fusion.rest_4_
  24.4 0.1 collective-permute-start.3
  24.5 0.7 collective-permute-start.4
  25.3 0.8 collective-permute-start.5
  26.1 2.0 %collective-permute-start.6 = (bf16[4,64,512]{2,1,0:T(8,128)(2,1)S(1)}, bf16[4,64,512]{2,1,0:T(8,128)(2,1)}, u32[]{:S(2)}, u32[]{:S(2)}) collective-permute-start(bf16[4,64,512]{2,1,0:T(8,128)(2,1)S(1)} %bitcast.38), channel_id=1, source_target_pairs={{0,96},{16,112},{32,0},{48,16},{64,32},{80,48},{96,64},{112,80},{1... | collective-permute-start | bytes 786440 | tf_op jit(solution)/shard_map/ppermute | solution.py:369
  28.7 0.1 pad_add_fusion.3.place_ref
  28.8 0.1 select_reduce_fusion.rest_0_
  28.9 16.5 %product.2 = (s16[4,288,256]{2,1,0:T(8,128)(2,1)S(1)}, s16[4,288,256]{2,1,0:T(8,128)(2,1)S(1)}, s16[4,288,256]{2,1,0:T(8,128)(2,1)S(1)}, s16[4,288,256]{2,1,0:T(8,128)(2,1)S(1)}, bf16[32,512,512]{2,1,0:T(8,128)(2,1)S(1)}) custom-call(s32[4]{0:T(128)S(1)} %pad_add_fusion.3.place_ref, s32[32]{0:T(128)S(1)} %select_reduce_fusion.rest_0_, ...), custom_call_target="tpu_custom_call" | custom-call | flops 8589934592 | bytes 4194304 | tf_op jit(solution)/shard_map/product/pallas_call | solution.py:232
  45.5 0.0 collective-permute-done.6
  45.5 1.1 pad_maximum_fusion.1.rest_2_
  46.6 0.1 collective-permute-start.7
  46.7 1.5 %collective-permute-start.10 = (s16[4,288,256]{2,1,0:T(8,128)(2,1)S(1)}, s16[4,288,256]{2,1,0:T(8,128)(2,1)S(1)}, u32[]{:S(2)}, u32[]{:S(2)}) collective-permute-start(s16[4,288,256]{2,1,0:T(8,128)(2,1)S(1)} %get-tuple-element.62), channel_id=1, source_target_pairs={{0,3},{1,0},{2,1},{3,2},{4,7},{5,4},{6,5},{7,6},{8,11},{9,8},{10,9... | collective-permute-start | bytes 1769480 | tf_op jit(solution)/shard_map/ppermute | solution.py:360
  48.1 1.2 %collective-permute-start.8 = (s16[4,288,256]{2,1,0:T(8,128)(2,1)S(1)}, s16[4,288,256]{2,1,0:T(8,128)(2,1)S(1)}, u32[]{:S(2)}, u32[]{:S(2)}) collective-permute-start(s16[4,288,256]{2,1,0:T(8,128)(2,1)S(1)} %get-tuple-element.60), channel_id=1, source_target_pairs={{0,2},{1,3},{2,0},{3,1},{4,6},{5,7},{6,4},{7,5},{8,10},{9,11},{10,... | collective-permute-start | bytes 1769480 | tf_op jit(solution)/shard_map/ppermute | solution.py:360
  49.4 0.0 collective-permute-start.9
  49.4 0.0 collective-permute-done.7.rest_3_
  49.4 14.5 %product.3 = (s16[4,272,256]{2,1,0:T(8,128)(2,1)S(1)}, s16[4,272,256]{2,1,0:T(8,128)(2,1)S(1)}, s16[4,272,256]{2,1,0:T(8,128)(2,1)S(1)}, s16[4,272,256]{2,1,0:T(8,128)(2,1)S(1)}) custom-call(s32[4]{0:T(128)S(1)} %pad_add_fusion.3.place_ref, bf16[32,512,512]{2,1,0:T(8,128)(2,1)S(1)} %get-tuple-element.46.rest_0_, ...), custom_call_target="tpu_custom_call" | custom-call | flops 8589934592 | bytes 4194304 | tf_op jit(solution)/shard_map/product/pallas_call | solution.py:232
  63.9 0.0 copy-start.3
  63.9 0.0 copy-start.2
  63.9 0.0 copy-start.1
  63.9 1.9 %collective-permute-done.9.refs_2_ = s16[4,288,256]{2,1,0:T(8,128)(2,1)S(1)} collective-permute-done((s16[4,288,256]{2,1,0:T(8,128)(2,1)S(1)}, s16[4,288,256]{2,1,0:T(8,128)(2,1)S(1)}, u32[]{:S(2)}, u32[]{:S(2)}) %collective-permute-start.9) | collective-permute-done | bytes 589856 | tf_op jit(solution)/shard_map/ppermute | solution.py:360
  65.8 1.7 %collective-permute-start.11 = (s16[4,272,256]{2,1,0:T(8,128)(2,1)S(1)}, s16[4,272,256]{2,1,0:T(8,128)(2,1)S(1)}, u32[]{:S(2)}, u32[]{:S(2)}) collective-permute-start(s16[4,272,256]{2,1,0:T(8,128)(2,1)S(1)} %get-tuple-element.68), channel_id=1, source_target_pairs={{0,2},{1,3},{2,0},{3,1},{4,6},{5,7},{6,4},{7,5},{8,10},{9,11},{10,... | collective-permute-start | bytes 1671176 | tf_op jit(solution)/shard_map/ppermute | solution.py:360
  67.5 0.6 collective-permute-start.12
  68.1 2.7 %collective-permute-start.13 = (s16[4,272,256]{2,1,0:T(8,128)(2,1)S(1)}, s16[4,272,256]{2,1,0:T(8,128)(2,1)S(1)}, u32[]{:S(2)}, u32[]{:S(2)}) collective-permute-start(s16[4,272,256]{2,1,0:T(8,128)(2,1)S(1)} %get-tuple-element.70), channel_id=1, source_target_pairs={{0,3},{1,0},{2,1},{3,2},{4,7},{5,4},{6,5},{7,6},{8,11},{9,8},{10,9... | collective-permute-start | bytes 1671176 | tf_op jit(solution)/shard_map/ppermute | solution.py:360
  70.8 6.2 %collective-permute-done.11.refs_5_ = s16[4,272,256]{2,1,0:T(8,128)(2,1)S(1)} collective-permute-done((s16[4,272,256]{2,1,0:T(8,128)(2,1)S(1)}, s16[4,272,256]{2,1,0:T(8,128)(2,1)S(1)}, u32[]{:S(2)}, u32[]{:S(2)}) %collective-permute-start.11) | collective-permute-done | bytes 557088 | tf_op jit(solution)/shard_map/ppermute | solution.py:360
  77.0 5.9 %collective-permute-done.12.refs_6_ = s16[4,272,256]{2,1,0:T(8,128)(2,1)S(1)} collective-permute-done((s16[4,272,256]{2,1,0:T(8,128)(2,1)S(1)}, s16[4,272,256]{2,1,0:T(8,128)(2,1)S(1)}, u32[]{:S(2)}, u32[]{:S(2)}) %collective-permute-start.12) | collective-permute-done | bytes 557088 | tf_op jit(solution)/shard_map/ppermute | solution.py:360
  82.9 1.4 %relay.1 = (s16[560,256]{1,0:T(8,128)(2,1)S(1)}, s16[560,256]{1,0:T(8,128)(2,1)S(1)}, s16[560,256]{1,0:T(8,128)(2,1)S(1)}, s16[560,256]{1,0:T(8,128)(2,1)S(1)}) custom-call(s16[4,288,256]{2,1,0:T(8,128)(2,1)S(1)} %get-tuple-element.63.refs_0_, s16[4,288,256]{2,1,0:T(8,128)(2,1)S(1)} %collective-permute-done.8.refs_1_, ...), custom_call_target="tpu_custom_call" | custom-call | tf_op jit(solution)/shard_map/relay/pallas_call | solution.py:263
  84.3 1.7 %collective-permute-start.14 = (s16[560,256]{1,0:T(8,128)(2,1)S(1)}, s16[560,256]{1,0:T(8,128)(2,1)S(1)}, u32[]{:S(2)}, u32[]{:S(2)}) collective-permute-start(s16[560,256]{1,0:T(8,128)(2,1)S(1)} %get-tuple-element.72), channel_id=1, source_target_pairs={{0,8},{1,9},{2,10},{3,11},{4,12},{5,13},{6,14},{7,15},{8,0},{9,1},... | collective-permute-start | bytes 860168 | tf_op jit(solution)/shard_map/ppermute | solution.py:360
  86.0 1.2 %collective-permute-start.15 = (s16[560,256]{1,0:T(8,128)(2,1)S(1)}, s16[560,256]{1,0:T(8,128)(2,1)S(1)}, u32[]{:S(2)}, u32[]{:S(2)}) collective-permute-start(s16[560,256]{1,0:T(8,128)(2,1)S(1)} %get-tuple-element.73), channel_id=1, source_target_pairs={{0,4},{1,5},{2,6},{3,7},{4,8},{5,9},{6,10},{7,11},{8,12},{9,13},{1... | collective-permute-start | bytes 860168 | tf_op jit(solution)/shard_map/ppermute | solution.py:360
  87.2 2.1 %collective-permute-start.16 = (s16[560,256]{1,0:T(8,128)(2,1)S(1)}, s16[560,256]{1,0:T(8,128)(2,1)S(1)}, u32[]{:S(2)}, u32[]{:S(2)}) collective-permute-start(s16[560,256]{1,0:T(8,128)(2,1)S(1)} %get-tuple-element.74), channel_id=1, source_target_pairs={{0,12},{1,13},{2,14},{3,15},{4,0},{5,1},{6,2},{7,3},{8,4},{9,5},{1... | collective-permute-start | bytes 860168 | tf_op jit(solution)/shard_map/ppermute | solution.py:360
  89.3 0.1 copy.16.ranks
  89.4 0.1 copy.18.energy
  89.6 0.1 broadcast_add_fusion
  89.6 0.1 add.58.pair_sum
  89.7 2.9 %collective-permute-done.14.refs_1_ = s16[560,256]{1,0:T(8,128)(2,1)S(1)} collective-permute-done((s16[560,256]{1,0:T(8,128)(2,1)S(1)}, s16[560,256]{1,0:T(8,128)(2,1)S(1)}, u32[]{:S(2)}, u32[]{:S(2)}) %collective-permute-start.14) | collective-permute-done | bytes 286752 | tf_op jit(solution)/shard_map/ppermute | solution.py:360
  92.6 3.0 %collective-permute-done.15.refs_2_ = s16[560,256]{1,0:T(8,128)(2,1)S(1)} collective-permute-done((s16[560,256]{1,0:T(8,128)(2,1)S(1)}, s16[560,256]{1,0:T(8,128)(2,1)S(1)}, u32[]{:S(2)}, u32[]{:S(2)}) %collective-permute-start.15) | collective-permute-done | bytes 286752 | tf_op jit(solution)/shard_map/ppermute | solution.py:360
  95.6 1.2 %owner.1 = (f32[256,640]{1,0:T(8,128)}, s16[256,640]{1,0:T(8,128)(2,1)}) custom-call(s16[560,256]{1,0:T(8,128)(2,1)S(1)} %get-tuple-element.71.refs_0_, s16[560,256]{1,0:T(8,128)(2,1)S(1)} %collective-permute-done.14.refs_1_, s16[560,256]{1,0:T(8,128)(2,1)S(1)} %collective-permute-done.15.refs_2_, s16[560,256]{1,0:T(8,128)(2,1)S(1)} %collective-permute-done.16.refs_3_), custom_call_target="tpu_custom_call" | custom-call | tf_op jit(solution)/shard_map/owner/pallas_call | solution.py:294
  96.8 3.8 %all-to-all-start.1 = ((s16[16,16,640]{2,1,0:T(8,128)(2,1)}), s16[16,16,640]{2,1,0:T(8,128)(2,1)S(1)}, u32[]{:S(2)}, u32[]{:S(2)}) async-start(s16[16,16,640]{2,1,0:T(8,128)(2,1)} %bitcast.23), calls=%async_computation.1 | async-start | bytes 655360 | tf_op jit(solution)/shard_map/all_to_all | solution.py:431
  100.7 0.4 fusion.1.spread
  101.1 3.4 %mine.1 = f32[256,1024]{1,0:T(8,128)} custom-call(f32[256,640]{1,0:T(8,128)} %get-tuple-element.75.own, s32[256,2]{1,0:T(8,128)S(1)} %copy.16.ranks, bf16[1024,1024]{1,0:T(8,128)(2,1)S(1)} %fusion.1.spread), custom_call_target="tpu_custom_call" | custom-call | flops 1073741824 | bytes 2097152 | tf_op jit(solution)/shard_map/mine/pallas_call | solution.py:340
  104.5 5.2 %all-to-all-done.1 = s16[16,16,640]{2,1,0:T(8,128)(2,1)S(1)} async-done(((s16[16,16,640]{2,1,0:T(8,128)(2,1)}), s16[16,16,640]{2,1,0:T(8,128)(2,1)S(1)}, u32[]{:S(2)}, u32[]{:S(2)}) %all-to-all-start.1) | async-done | bytes 327712 | tf_op jit(solution)/shard_map/all_to_all | solution.py:431
  109.7 3.6 %close.1 = f32[256,1024]{1,0:T(8,128)} custom-call(f32[256,1024]{1,0:T(8,128)} %mine.1, s16[256,640]{1,0:T(8,128)(2,1)S(1)} %bitcast.35, s32[256,2]{1,0:T(8,128)S(1)} %copy.16.ranks, f32[256,1]{1,0:T(8,128)S(1)} %copy.18.energy, f32[1,1024]{1,0:T(1,128)S(1)} %add.58.pair_sum, bf16[1024,1024]{1,0:T(8,128)(2,1)S(1)} %fusion.1.spread), custom_call_target="tpu_custom_call" | custom-call | flops 1073741824 | bytes 2097152 | tf_op jit(solution)/shard_map/close/pallas_call | solution.py:340
  (28 shorter events, 0.2 us)
Async XLA Ops:
  0.0 1.0 copy-start
  0.0 8.7 %copy-start.4 = (s32[256]{0:T(256)S(1)}, s32[256]{0:T(256)}, u32[]{:S(2)}) copy-start(s32[256]{0:T(256)} %param.15) | copy-start | bytes 3076
  0.0 28.8 %copy-start.5 = (s32[1,1,32]{2,1,0:T(1,128)S(1)}, s32[1,1,32]{2,1,0:T(1,128)}, u32[]{:S(2)}) copy-start(s32[1,1,32]{2,1,0:T(1,128)} %param.11) | copy-start | bytes 388
  2.7 21.6 %collective-permute-start = (bf16[4,64,512]{2,1,0:T(8,128)(2,1)S(1)}, bf16[4,64,512]{2,1,0:T(8,128)(2,1)S(1)}, u32[]{:S(2)}, u32[]{:S(2)}) collective-permute-start(bf16[4,64,512]{2,1,0:T(8,128)(2,1)S(1)} %bitcast.40), channel_id=1, source_target_pairs={{0,32},{16,48},{32,64},{48,80},{64,96},{80,112},{96,0},{112,16},{1... | collective-permute-start | bytes 786440 | tf_op jit(solution)/shard_map/ppermute | solution.py:369
  4.4 19.9 %collective-permute-start.1 = (bf16[4,64,512]{2,1,0:T(8,128)(2,1)S(1)}, bf16[4,64,512]{2,1,0:T(8,128)(2,1)S(1)}, u32[]{:S(2)}, u32[]{:S(2)}) collective-permute-start(bf16[4,64,512]{2,1,0:T(8,128)(2,1)S(1)} %bitcast.41), channel_id=1, source_target_pairs={{0,64},{16,80},{32,96},{48,112},{64,0},{80,16},{96,32},{112,48},{1... | collective-permute-start | bytes 786440 | tf_op jit(solution)/shard_map/ppermute | solution.py:369
  7.3 17.0 %collective-permute-start.2 = (bf16[4,64,512]{2,1,0:T(8,128)(2,1)S(1)}, bf16[4,64,512]{2,1,0:T(8,128)(2,1)S(1)}, u32[]{:S(2)}, u32[]{:S(2)}) collective-permute-start(bf16[4,64,512]{2,1,0:T(8,128)(2,1)S(1)} %bitcast.42), channel_id=1, source_target_pairs={{0,96},{16,112},{32,0},{48,16},{64,32},{80,48},{96,64},{112,80},{1... | collective-permute-start | bytes 786440 | tf_op jit(solution)/shard_map/ppermute | solution.py:369
  24.4 4.5 %collective-permute-start.3 = (bf16[4,4,64,512]{3,2,1,0:T(8,128)(2,1)S(1)}, bf16[4,4,64,512]{3,2,1,0:T(8,128)(2,1)S(1)}, u32[]{:S(2)}, u32[]{:S(2)}) collective-permute-start(bf16[4,4,64,512]{3,2,1,0:T(8,128)(2,1)S(1)} %pad_maximum_fusion.rest_4_), channel_id=1, source_target_pairs={{0,16},{16,0},{32,48},{48,32},{64,80},{80,64},{96,112},{112,96},{1... | collective-permute-start | bytes 3145736 | tf_op jit(solution)/shard_map/ppermute | solution.py:375
  24.5 20.9 %collective-permute-start.4 = (bf16[4,64,512]{2,1,0:T(8,128)(2,1)S(1)}, bf16[4,64,512]{2,1,0:T(8,128)(2,1)S(1)}, u32[]{:S(2)}, u32[]{:S(2)}) collective-permute-start(bf16[4,64,512]{2,1,0:T(8,128)(2,1)S(1)} %bitcast.36), channel_id=1, source_target_pairs={{0,32},{16,48},{32,64},{48,80},{64,96},{80,112},{96,0},{112,16},{1... | collective-permute-start | bytes 786440 | tf_op jit(solution)/shard_map/ppermute | solution.py:369
  25.3 20.2 %collective-permute-start.5 = (bf16[4,64,512]{2,1,0:T(8,128)(2,1)S(1)}, bf16[4,64,512]{2,1,0:T(8,128)(2,1)S(1)}, u32[]{:S(2)}, u32[]{:S(2)}) collective-permute-start(bf16[4,64,512]{2,1,0:T(8,128)(2,1)S(1)} %bitcast.37), channel_id=1, source_target_pairs={{0,64},{16,80},{32,96},{48,112},{64,0},{80,16},{96,32},{112,48},{1... | collective-permute-start | bytes 786440 | tf_op jit(solution)/shard_map/ppermute | solution.py:369
  26.1 19.4 %collective-permute-start.6 = (bf16[4,64,512]{2,1,0:T(8,128)(2,1)S(1)}, bf16[4,64,512]{2,1,0:T(8,128)(2,1)}, u32[]{:S(2)}, u32[]{:S(2)}) collective-permute-start(bf16[4,64,512]{2,1,0:T(8,128)(2,1)S(1)} %bitcast.38), channel_id=1, source_target_pairs={{0,96},{16,112},{32,0},{48,16},{64,32},{80,48},{96,64},{112,80},{1... | collective-permute-start | bytes 786440 | tf_op jit(solution)/shard_map/ppermute | solution.py:369
  46.6 2.8 %collective-permute-start.7 = (bf16[4,4,64,512]{3,2,1,0:T(8,128)(2,1)S(1)}, bf16[4,4,64,512]{3,2,1,0:T(8,128)(2,1)S(1)}, u32[]{:S(2)}, u32[]{:S(2)}) collective-permute-start(bf16[4,4,64,512]{3,2,1,0:T(8,128)(2,1)S(1)} %pad_maximum_fusion.1.rest_2_), channel_id=1, source_target_pairs={{0,16},{16,0},{32,48},{48,32},{64,80},{80,64},{96,112},{112,96},{1... | collective-permute-start | bytes 3145736 | tf_op jit(solution)/shard_map/ppermute | solution.py:375
  46.7 17.2 %collective-permute-start.10 = (s16[4,288,256]{2,1,0:T(8,128)(2,1)S(1)}, s16[4,288,256]{2,1,0:T(8,128)(2,1)S(1)}, u32[]{:S(2)}, u32[]{:S(2)}) collective-permute-start(s16[4,288,256]{2,1,0:T(8,128)(2,1)S(1)} %get-tuple-element.62), channel_id=1, source_target_pairs={{0,3},{1,0},{2,1},{3,2},{4,7},{5,4},{6,5},{7,6},{8,11},{9,8},{10,9... | collective-permute-start | bytes 1769480 | tf_op jit(solution)/shard_map/ppermute | solution.py:360
  48.1 15.8 %collective-permute-start.8 = (s16[4,288,256]{2,1,0:T(8,128)(2,1)S(1)}, s16[4,288,256]{2,1,0:T(8,128)(2,1)S(1)}, u32[]{:S(2)}, u32[]{:S(2)}) collective-permute-start(s16[4,288,256]{2,1,0:T(8,128)(2,1)S(1)} %get-tuple-element.60), channel_id=1, source_target_pairs={{0,2},{1,3},{2,0},{3,1},{4,6},{5,7},{6,4},{7,5},{8,10},{9,11},{10,... | collective-permute-start | bytes 1769480 | tf_op jit(solution)/shard_map/ppermute | solution.py:360
  49.4 16.5 %collective-permute-start.9 = (s16[4,288,256]{2,1,0:T(8,128)(2,1)S(1)}, s16[4,288,256]{2,1,0:T(8,128)(2,1)S(1)}, u32[]{:S(2)}, u32[]{:S(2)}) collective-permute-start(s16[4,288,256]{2,1,0:T(8,128)(2,1)S(1)} %get-tuple-element.61), channel_id=1, source_target_pairs={{0,1},{1,2},{2,3},{3,0},{4,5},{5,6},{6,7},{7,4},{8,9},{9,10},{10,1... | collective-permute-start | bytes 1769480 | tf_op jit(solution)/shard_map/ppermute | solution.py:360
  63.9 25.5 %copy-start.3 = (f32[256]{0:T(256)S(1)}, f32[256]{0:T(256)}, u32[]{:S(2)}) copy-start(f32[256]{0:T(256)} %param.13) | copy-start | bytes 3076
  63.9 25.7 %copy-start.2 = (f32[32]{0:T(128)S(1)}, f32[32]{0:T(128)}, u32[]{:S(2)}) copy-start(f32[32]{0:T(128)} %param.14) | copy-start | bytes 388
  63.9 36.8 %copy-start.1 = (s32[1024]{0:T(1024)S(1)}, s32[1024]{0:T(1024)}, u32[]{:S(2)}) copy-start(s32[1024]{0:T(1024)} %constant.94.clone) | copy-start | bytes 12292
  65.8 11.1 %collective-permute-start.11 = (s16[4,272,256]{2,1,0:T(8,128)(2,1)S(1)}, s16[4,272,256]{2,1,0:T(8,128)(2,1)S(1)}, u32[]{:S(2)}, u32[]{:S(2)}) collective-permute-start(s16[4,272,256]{2,1,0:T(8,128)(2,1)S(1)} %get-tuple-element.68), channel_id=1, source_target_pairs={{0,2},{1,3},{2,0},{3,1},{4,6},{5,7},{6,4},{7,5},{8,10},{9,11},{10,... | collective-permute-start | bytes 1671176 | tf_op jit(solution)/shard_map/ppermute | solution.py:360
  67.5 15.3 %collective-permute-start.12 = (s16[4,272,256]{2,1,0:T(8,128)(2,1)S(1)}, s16[4,272,256]{2,1,0:T(8,128)(2,1)S(1)}, u32[]{:S(2)}, u32[]{:S(2)}) collective-permute-start(s16[4,272,256]{2,1,0:T(8,128)(2,1)S(1)} %get-tuple-element.69), channel_id=1, source_target_pairs={{0,1},{1,2},{2,3},{3,0},{4,5},{5,6},{6,7},{7,4},{8,9},{9,10},{10,1... | collective-permute-start | bytes 1671176 | tf_op jit(solution)/shard_map/ppermute | solution.py:360
  68.1 14.8 %collective-permute-start.13 = (s16[4,272,256]{2,1,0:T(8,128)(2,1)S(1)}, s16[4,272,256]{2,1,0:T(8,128)(2,1)S(1)}, u32[]{:S(2)}, u32[]{:S(2)}) collective-permute-start(s16[4,272,256]{2,1,0:T(8,128)(2,1)S(1)} %get-tuple-element.70), channel_id=1, source_target_pairs={{0,3},{1,0},{2,1},{3,2},{4,7},{5,4},{6,5},{7,6},{8,11},{9,8},{10,9... | collective-permute-start | bytes 1671176 | tf_op jit(solution)/shard_map/ppermute | solution.py:360
  84.3 8.3 %collective-permute-start.14 = (s16[560,256]{1,0:T(8,128)(2,1)S(1)}, s16[560,256]{1,0:T(8,128)(2,1)S(1)}, u32[]{:S(2)}, u32[]{:S(2)}) collective-permute-start(s16[560,256]{1,0:T(8,128)(2,1)S(1)} %get-tuple-element.72), channel_id=1, source_target_pairs={{0,8},{1,9},{2,10},{3,11},{4,12},{5,13},{6,14},{7,15},{8,0},{9,1},... | collective-permute-start | bytes 860168 | tf_op jit(solution)/shard_map/ppermute | solution.py:360
  86.0 9.6 %collective-permute-start.15 = (s16[560,256]{1,0:T(8,128)(2,1)S(1)}, s16[560,256]{1,0:T(8,128)(2,1)S(1)}, u32[]{:S(2)}, u32[]{:S(2)}) collective-permute-start(s16[560,256]{1,0:T(8,128)(2,1)S(1)} %get-tuple-element.73), channel_id=1, source_target_pairs={{0,4},{1,5},{2,6},{3,7},{4,8},{5,9},{6,10},{7,11},{8,12},{9,13},{1... | collective-permute-start | bytes 860168 | tf_op jit(solution)/shard_map/ppermute | solution.py:360
  87.2 8.4 %collective-permute-start.16 = (s16[560,256]{1,0:T(8,128)(2,1)S(1)}, s16[560,256]{1,0:T(8,128)(2,1)S(1)}, u32[]{:S(2)}, u32[]{:S(2)}) collective-permute-start(s16[560,256]{1,0:T(8,128)(2,1)S(1)} %get-tuple-element.74), channel_id=1, source_target_pairs={{0,12},{1,13},{2,14},{3,15},{4,0},{5,1},{6,2},{7,3},{8,4},{9,5},{1... | collective-permute-start | bytes 860168 | tf_op jit(solution)/shard_map/ppermute | solution.py:360
  96.8 12.9 %all-to-all-start.1 = ((s16[16,16,640]{2,1,0:T(8,128)(2,1)}), s16[16,16,640]{2,1,0:T(8,128)(2,1)S(1)}, u32[]{:S(2)}, u32[]{:S(2)}) async-start(s16[16,16,640]{2,1,0:T(8,128)(2,1)} %bitcast.23), calls=%async_computation.1 | async-start | bytes 655360 | tf_op jit(solution)/shard_map/all_to_all | solution.py:431

commit v7 on v6

--- a/solution.py
+++ b/solution.py
@@ -402,17 +402,15 @@
     spoken = jnp.broadcast_to(both[None, :], (groups, 2 * rows))
     ranks = lax.all_to_all(spoken, "col", split_axis=0, concat_axis=0, tiled=True)
     along = [fetch_along(part) for part in parts]
-    ranks, along[0] = lax.optimization_barrier((ranks, along[0]))
     ranks = jnp.stack([ranks[:, :rows], ranks[:, rows:]])
-
-    row = lax.axis_index("row")
-    col = lax.axis_index("col")
+    row, col = lax.axis_index("row"), lax.axis_index("col")
     z, x, core = col // SIDE, col % SIDE, row % 2
     place = jnp.stack([row // 2, core, jnp.where(core == 0, x, z), jnp.where(core == 0, z, x)]).astype(S32)
     slots = tile_list[0, 0]
     slot_ids = jnp.arange(slots.shape[0], dtype=S32)
     order = jnp.sum(jnp.where(slots[None, :] == slot_ids[:, None], slot_ids[None, :], 0), axis=1)
     live = (order < tile_count[0, 0]).astype(S32)
+    ranks, order, live, place, along[0] = lax.optimization_barrier((ranks, order, live, place, along[0]))
 
     tiles = integrals[0, 0]
     far_flags = tuple(c == 0 for c in range(CHUNKS))

time: 114 us -> 113 us (level)
  blocking collectives: 15.3 us -> 0 us
  starting transfers between devices: 26.1 us -> 34.6 us
  waiting for transfers between devices: 25.1 us -> 31.4 us
    all_to_all x1 -> x0, blocking collectives: 15.3 us -> none  [body(): lax.all_to_all(spoken, 'col', split_axis=0, concat_axis=0, tiled=True)]
    all_to_all x0 -> x1, starting transfers between devices: none -> 7.88 us  [body(): lax.all_to_all(spoken, 'col', split_axis=0, concat_axis=0, tiled=True)]
    all_to_all x0 -> x1, waiting for transfers between devices: none -> 6.67 us  [body(): lax.all_to_all(spoken, 'col', split_axis=0, concat_axis=0, tiled=True)]
  transfers between devices with their start and end apart: 18 -> 19, of which waited for: 6 -> 7; matrix products, arithmetic and copies ran while one was open for 1% -> 2% of each run, Pallas kernels for 30% -> 31%
where the time goes in v7:
time: 113 us; the launch traced here: 112 us
  Pallas kernels  40.6 us (36%)
  starting transfers between devices  34.6 us (31%)
  waiting for transfers between devices  31.4 us (28%)
  local copies, waits for them, and re-layouts  2.09 us (2%)
  matrix products  1.58 us (1%)
  other arithmetic  1.24 us (1%)
    pallas_call x2, Pallas kernels, product(): pl.pallas_call(functools.partial(product_kernel, has_far, rows, fetch), o...  30.9 us
    ppermute x9, waiting for transfers between devices, trade(): got.append(lax.ppermute(pieces[k], ('row', 'col'), perm))  19.5 us
    ppermute x9, starting transfers between devices, trade(): got.append(lax.ppermute(pieces[k], ('row', 'col'), perm))  12.6 us
    ppermute x6, starting transfers between devices, fetch_along(): lax.ppermute(part, 'row', shifted_rows(k, 0))  9.49 us
    all_to_all x1, starting transfers between devices, body(): lax.all_to_all(spoken, 'col', split_axis=0, concat_axis=0, tiled=True)  7.88 us
    pallas_call x2, Pallas kernels, last_call(): pl.pallas_call(kernel, out_shape=result, in_specs=[vmem] * len(args), out...  6.99 us
    all_to_all x1, waiting for transfers between devices, body(): lax.all_to_all(spoken, 'col', split_axis=0, concat_axis=0, tiled=True)  6.67 us
    all_to_all x1, waiting for transfers between devices, body(): came = lax.all_to_all(send, 'col', split_axis=0, concat_axis=0, tiled=True)  5.22 us
  transfers between devices with their start and end apart: 19, of which 7 were waited for; matrix products, arithmetic and copies ran while one was open for 2% of the time, Pallas kernels for 31%

profile of v7, /device:TPU:0, one launch (start us, length us, event | category | flops | bytes accessed | tf_op | source)
XLA Modules:
  0.0 112.4 jit_solution(11233689915604743544)
XLA Ops:
  0.0 1.0 copy-done
  1.0 1.6 %fusion.4 = bf16[256,1024]{1,0:T(8,128)(2,1)S(1)} fusion(bf16[256,1024]{1,0:T(8,128)(2,1)S(1)} %bitcast.34, s32[1024]{0:T(1024)} %constant.93.clone), kind=kOutput, calls=%fused_computation.6 | convolution fusion | flops 538181632 | bytes 1052672 | tf_op jit(solution)/shard_map/dot_general | solution.py:391
  2.7 1.7 %collective-permute-start = (bf16[4,64,512]{2,1,0:T(8,128)(2,1)S(1)}, bf16[4,64,512]{2,1,0:T(8,128)(2,1)S(1)}, u32[]{:S(2)}, u32[]{:S(2)}) collective-permute-start(bf16[4,64,512]{2,1,0:T(8,128)(2,1)S(1)} %bitcast.40), channel_id=1, source_target_pairs={{0,32},{16,48},{32,64},{48,80},{64,96},{80,112},{96,0},{112,16},{1... | collective-permute-start | bytes 786440 | tf_op jit(solution)/shard_map/ppermute | solution.py:369
  4.4 2.9 %collective-permute-start.1 = (bf16[4,64,512]{2,1,0:T(8,128)(2,1)S(1)}, bf16[4,64,512]{2,1,0:T(8,128)(2,1)S(1)}, u32[]{:S(2)}, u32[]{:S(2)}) collective-permute-start(bf16[4,64,512]{2,1,0:T(8,128)(2,1)S(1)} %bitcast.41), channel_id=1, source_target_pairs={{0,64},{16,80},{32,96},{48,112},{64,0},{80,16},{96,32},{112,48},{1... | collective-permute-start | bytes 786440 | tf_op jit(solution)/shard_map/ppermute | solution.py:369
  7.3 1.3 %collective-permute-start.2 = (bf16[4,64,512]{2,1,0:T(8,128)(2,1)S(1)}, bf16[4,64,512]{2,1,0:T(8,128)(2,1)S(1)}, u32[]{:S(2)}, u32[]{:S(2)}) collective-permute-start(bf16[4,64,512]{2,1,0:T(8,128)(2,1)S(1)} %bitcast.42), channel_id=1, source_target_pairs={{0,96},{16,112},{32,0},{48,16},{64,32},{80,48},{96,64},{112,80},{1... | collective-permute-start | bytes 786440 | tf_op jit(solution)/shard_map/ppermute | solution.py:369
  8.7 0.3 convert_reduce_fusion.1
  9.0 0.6 broadcast_in_dim.12
  9.6 7.9 %all-to-all-start = ((s32[16,1,512]{2,1,0:T(1,128)}), s32[16,1,512]{2,1,0:T(1,128)S(1)}, u32[]{:S(2)}, u32[]{:S(2)}) async-start(s32[16,1,512]{2,1,0:T(1,128)} %broadcast_in_dim.12), calls=%async_computation | async-start | bytes 65536 | tf_op jit(solution)/shard_map/all_to_all | solution.py:403
  17.5 0.1 select_reduce_fusion.rest_0_
  18.3 0.1 pad_add_fusion.3.place_ref
  18.4 6.7 %all-to-all-done = s32[16,1,512]{2,1,0:T(1,128)S(1)} async-done(((s32[16,1,512]{2,1,0:T(1,128)}), s32[16,1,512]{2,1,0:T(1,128)S(1)}, u32[]{:S(2)}, u32[]{:S(2)}) %all-to-all-start) | async-done | bytes 32800 | tf_op jit(solution)/shard_map/all_to_all | solution.py:403
  25.1 0.1 pad_maximum_fusion.rest_4_
  25.3 0.1 collective-permute-start.3
  25.4 0.7 collective-permute-start.4
  26.1 0.8 collective-permute-start.5
  26.9 2.0 %collective-permute-start.6 = (bf16[4,64,512]{2,1,0:T(8,128)(2,1)S(1)}, bf16[4,64,512]{2,1,0:T(8,128)(2,1)S(1)}, u32[]{:S(2)}, u32[]{:S(2)}) collective-permute-start(bf16[4,64,512]{2,1,0:T(8,128)(2,1)S(1)} %bitcast.38), channel_id=1, source_target_pairs={{0,96},{16,112},{32,0},{48,16},{64,32},{80,48},{96,64},{112,80},{1... | collective-permute-start | bytes 786440 | tf_op jit(solution)/shard_map/ppermute | solution.py:369
  28.9 16.4 %product.2 = (s16[4,288,256]{2,1,0:T(8,128)(2,1)S(1)}, s16[4,288,256]{2,1,0:T(8,128)(2,1)S(1)}, s16[4,288,256]{2,1,0:T(8,128)(2,1)S(1)}, s16[4,288,256]{2,1,0:T(8,128)(2,1)S(1)}, bf16[32,512,512]{2,1,0:T(8,128)(2,1)S(1)}) custom-call(s32[4]{0:T(128)S(1)} %pad_add_fusion.3.place_ref, s32[32]{0:T(128)S(1)} %select_reduce_fusion.rest_0_, ...), custom_call_target="tpu_custom_call" | custom-call | flops 8589934592 | bytes 4194304 | tf_op jit(solution)/shard_map/product/pallas_call | solution.py:232
  45.3 0.1 pad_maximum_fusion.1.rest_2_
  45.4 0.4 collective-permute-start.7
  45.8 1.2 %collective-permute-start.10 = (s16[4,288,256]{2,1,0:T(8,128)(2,1)S(1)}, s16[4,288,256]{2,1,0:T(8,128)(2,1)S(1)}, u32[]{:S(2)}, u32[]{:S(2)}) collective-permute-start(s16[4,288,256]{2,1,0:T(8,128)(2,1)S(1)} %get-tuple-element.68), channel_id=1, source_target_pairs={{0,3},{1,0},{2,1},{3,2},{4,7},{5,4},{6,5},{7,6},{8,11},{9,8},{10,9... | collective-permute-start | bytes 1769480 | tf_op jit(solution)/shard_map/ppermute | solution.py:360
  47.0 1.4 %collective-permute-start.8 = (s16[4,288,256]{2,1,0:T(8,128)(2,1)S(1)}, s16[4,288,256]{2,1,0:T(8,128)(2,1)S(1)}, u32[]{:S(2)}, u32[]{:S(2)}) collective-permute-start(s16[4,288,256]{2,1,0:T(8,128)(2,1)S(1)} %get-tuple-element.66), channel_id=1, source_target_pairs={{0,2},{1,3},{2,0},{3,1},{4,6},{5,7},{6,4},{7,5},{8,10},{9,11},{10,... | collective-permute-start | bytes 1769480 | tf_op jit(solution)/shard_map/ppermute | solution.py:360
  48.4 0.0 collective-permute-start.9
  48.4 14.6 %product.3 = (s16[4,272,256]{2,1,0:T(8,128)(2,1)S(1)}, s16[4,272,256]{2,1,0:T(8,128)(2,1)S(1)}, s16[4,272,256]{2,1,0:T(8,128)(2,1)S(1)}, s16[4,272,256]{2,1,0:T(8,128)(2,1)S(1)}) custom-call(s32[4]{0:T(128)S(1)} %pad_add_fusion.3.place_ref, bf16[32,512,512]{2,1,0:T(8,128)(2,1)S(1)} %get-tuple-element.52.rest_0_, ...), custom_call_target="tpu_custom_call" | custom-call | flops 8589934592 | bytes 4194304 | tf_op jit(solution)/shard_map/product/pallas_call | solution.py:232
  63.0 0.0 copy-start.3
  63.1 0.0 copy-start.2
  63.1 0.0 copy-start.1
  63.1 1.6 %collective-permute-done.9.refs_2_ = s16[4,288,256]{2,1,0:T(8,128)(2,1)S(1)} collective-permute-done((s16[4,288,256]{2,1,0:T(8,128)(2,1)S(1)}, s16[4,288,256]{2,1,0:T(8,128)(2,1)S(1)}, u32[]{:S(2)}, u32[]{:S(2)}) %collective-permute-start.9) | collective-permute-done | bytes 589856 | tf_op jit(solution)/shard_map/ppermute | solution.py:360
  64.7 2.0 %collective-permute-start.11 = (s16[4,272,256]{2,1,0:T(8,128)(2,1)S(1)}, s16[4,272,256]{2,1,0:T(8,128)(2,1)S(1)}, u32[]{:S(2)}, u32[]{:S(2)}) collective-permute-start(s16[4,272,256]{2,1,0:T(8,128)(2,1)S(1)} %get-tuple-element.74), channel_id=1, source_target_pairs={{0,2},{1,3},{2,0},{3,1},{4,6},{5,7},{6,4},{7,5},{8,10},{9,11},{10,... | collective-permute-start | bytes 1671176 | tf_op jit(solution)/shard_map/ppermute | solution.py:360
  66.7 0.5 collective-permute-start.12
  67.2 2.7 %collective-permute-start.13 = (s16[4,272,256]{2,1,0:T(8,128)(2,1)S(1)}, s16[4,272,256]{2,1,0:T(8,128)(2,1)S(1)}, u32[]{:S(2)}, u32[]{:S(2)}) collective-permute-start(s16[4,272,256]{2,1,0:T(8,128)(2,1)S(1)} %get-tuple-element.76), channel_id=1, source_target_pairs={{0,3},{1,0},{2,1},{3,2},{4,7},{5,4},{6,5},{7,6},{8,11},{9,8},{10,9... | collective-permute-start | bytes 1671176 | tf_op jit(solution)/shard_map/ppermute | solution.py:360
  69.9 5.9 %collective-permute-done.11.refs_5_ = s16[4,272,256]{2,1,0:T(8,128)(2,1)S(1)} collective-permute-done((s16[4,272,256]{2,1,0:T(8,128)(2,1)S(1)}, s16[4,272,256]{2,1,0:T(8,128)(2,1)S(1)}, u32[]{:S(2)}, u32[]{:S(2)}) %collective-permute-start.11) | collective-permute-done | bytes 557088 | tf_op jit(solution)/shard_map/ppermute | solution.py:360
  75.8 5.9 %collective-permute-done.12.refs_6_ = s16[4,272,256]{2,1,0:T(8,128)(2,1)S(1)} collective-permute-done((s16[4,272,256]{2,1,0:T(8,128)(2,1)S(1)}, s16[4,272,256]{2,1,0:T(8,128)(2,1)S(1)}, u32[]{:S(2)}, u32[]{:S(2)}) %collective-permute-start.12) | collective-permute-done | bytes 557088 | tf_op jit(solution)/shard_map/ppermute | solution.py:360
  81.7 1.4 %relay.1 = (s16[560,256]{1,0:T(8,128)(2,1)S(1)}, s16[560,256]{1,0:T(8,128)(2,1)S(1)}, s16[560,256]{1,0:T(8,128)(2,1)S(1)}, s16[560,256]{1,0:T(8,128)(2,1)S(1)}) custom-call(s16[4,288,256]{2,1,0:T(8,128)(2,1)S(1)} %get-tuple-element.69.refs_0_, s16[4,288,256]{2,1,0:T(8,128)(2,1)S(1)} %collective-permute-done.8.refs_1_, ...), custom_call_target="tpu_custom_call" | custom-call | tf_op jit(solution)/shard_map/relay/pallas_call | solution.py:263
  83.1 1.5 %collective-permute-start.14 = (s16[560,256]{1,0:T(8,128)(2,1)S(1)}, s16[560,256]{1,0:T(8,128)(2,1)S(1)}, u32[]{:S(2)}, u32[]{:S(2)}) collective-permute-start(s16[560,256]{1,0:T(8,128)(2,1)S(1)} %get-tuple-element.78), channel_id=1, source_target_pairs={{0,8},{1,9},{2,10},{3,11},{4,12},{5,13},{6,14},{7,15},{8,0},{9,1},... | collective-permute-start | bytes 860168 | tf_op jit(solution)/shard_map/ppermute | solution.py:360
  84.6 0.8 collective-permute-start.15
  85.4 2.4 %collective-permute-start.16 = (s16[560,256]{1,0:T(8,128)(2,1)S(1)}, s16[560,256]{1,0:T(8,128)(2,1)S(1)}, u32[]{:S(2)}, u32[]{:S(2)}) collective-permute-start(s16[560,256]{1,0:T(8,128)(2,1)S(1)} %get-tuple-element.80), channel_id=1, source_target_pairs={{0,12},{1,13},{2,14},{3,15},{4,0},{5,1},{6,2},{7,3},{8,4},{9,5},{1... | collective-permute-start | bytes 860168 | tf_op jit(solution)/shard_map/ppermute | solution.py:360
  87.8 0.1 copy.16.ranks
  88.0 0.1 copy.18.energy
  88.1 0.1 broadcast_add_fusion
  88.2 0.1 add.58.pair_sum
  88.3 3.2 %collective-permute-done.14.refs_1_ = s16[560,256]{1,0:T(8,128)(2,1)S(1)} collective-permute-done((s16[560,256]{1,0:T(8,128)(2,1)S(1)}, s16[560,256]{1,0:T(8,128)(2,1)S(1)}, u32[]{:S(2)}, u32[]{:S(2)}) %collective-permute-start.14) | collective-permute-done | bytes 286752 | tf_op jit(solution)/shard_map/ppermute | solution.py:360
  91.4 3.0 %collective-permute-done.15.refs_2_ = s16[560,256]{1,0:T(8,128)(2,1)S(1)} collective-permute-done((s16[560,256]{1,0:T(8,128)(2,1)S(1)}, s16[560,256]{1,0:T(8,128)(2,1)S(1)}, u32[]{:S(2)}, u32[]{:S(2)}) %collective-permute-start.15) | collective-permute-done | bytes 286752 | tf_op jit(solution)/shard_map/ppermute | solution.py:360
  94.4 1.2 %owner.1 = (f32[256,640]{1,0:T(8,128)}, s16[256,640]{1,0:T(8,128)(2,1)}) custom-call(s16[560,256]{1,0:T(8,128)(2,1)S(1)} %get-tuple-element.77.refs_0_, s16[560,256]{1,0:T(8,128)(2,1)S(1)} %collective-permute-done.14.refs_1_, s16[560,256]{1,0:T(8,128)(2,1)S(1)} %collective-permute-done.15.refs_2_, s16[560,256]{1,0:T(8,128)(2,1)S(1)} %collective-permute-done.16.refs_3_), custom_call_target="tpu_custom_call" | custom-call | tf_op jit(solution)/shard_map/owner/pallas_call | solution.py:294
  95.6 4.1 %all-to-all-start.1 = ((s16[16,16,640]{2,1,0:T(8,128)(2,1)}), s16[16,16,640]{2,1,0:T(8,128)(2,1)S(1)}, u32[]{:S(2)}, u32[]{:S(2)}) async-start(s16[16,16,640]{2,1,0:T(8,128)(2,1)} %bitcast.23), calls=%async_computation.1 | async-start | bytes 655360 | tf_op jit(solution)/shard_map/all_to_all | solution.py:429
  99.8 0.4 fusion.1.spread
  100.2 3.4 %mine.1 = f32[256,1024]{1,0:T(8,128)} custom-call(f32[256,640]{1,0:T(8,128)} %get-tuple-element.81.own, s32[256,2]{1,0:T(8,128)S(1)} %copy.16.ranks, bf16[1024,1024]{1,0:T(8,128)(2,1)S(1)} %fusion.1.spread), custom_call_target="tpu_custom_call" | custom-call | flops 1073741824 | bytes 2097152 | tf_op jit(solution)/shard_map/mine/pallas_call | solution.py:340
  103.6 5.2 %all-to-all-done.1 = s16[16,16,640]{2,1,0:T(8,128)(2,1)S(1)} async-done(((s16[16,16,640]{2,1,0:T(8,128)(2,1)}), s16[16,16,640]{2,1,0:T(8,128)(2,1)S(1)}, u32[]{:S(2)}, u32[]{:S(2)}) %all-to-all-start.1) | async-done | bytes 327712 | tf_op jit(solution)/shard_map/all_to_all | solution.py:429
  108.8 3.6 %close.1 = f32[256,1024]{1,0:T(8,128)} custom-call(f32[256,1024]{1,0:T(8,128)} %mine.1, s16[256,640]{1,0:T(8,128)(2,1)S(1)} %bitcast.35, s32[256,2]{1,0:T(8,128)S(1)} %copy.16.ranks, f32[256,1]{1,0:T(8,128)S(1)} %copy.18.energy, f32[1,1024]{1,0:T(1,128)S(1)} %add.58.pair_sum, bf16[1024,1024]{1,0:T(8,128)(2,1)S(1)} %fusion.1.spread), custom_call_target="tpu_custom_call" | custom-call | flops 1073741824 | bytes 2097152 | tf_op jit(solution)/shard_map/close/pallas_call | solution.py:340
  (29 shorter events, 0.1 us)
Async XLA Ops:
  0.0 1.0 copy-start
  0.0 8.7 %copy-start.4 = (s32[256]{0:T(256)S(1)}, s32[256]{0:T(256)}, u32[]{:S(2)}) copy-start(s32[256]{0:T(256)} %param.15) | copy-start | bytes 3076
  0.0 17.5 %copy-start.5 = (s32[1,1,32]{2,1,0:T(1,128)S(1)}, s32[1,1,32]{2,1,0:T(1,128)}, u32[]{:S(2)}) copy-start(s32[1,1,32]{2,1,0:T(1,128)} %param.11) | copy-start | bytes 388
  2.7 22.4 %collective-permute-start = (bf16[4,64,512]{2,1,0:T(8,128)(2,1)S(1)}, bf16[4,64,512]{2,1,0:T(8,128)(2,1)S(1)}, u32[]{:S(2)}, u32[]{:S(2)}) collective-permute-start(bf16[4,64,512]{2,1,0:T(8,128)(2,1)S(1)} %bitcast.40), channel_id=1, source_target_pairs={{0,32},{16,48},{32,64},{48,80},{64,96},{80,112},{96,0},{112,16},{1... | collective-permute-start | bytes 786440 | tf_op jit(solution)/shard_map/ppermute | solution.py:369
  4.4 20.7 %collective-permute-start.1 = (bf16[4,64,512]{2,1,0:T(8,128)(2,1)S(1)}, bf16[4,64,512]{2,1,0:T(8,128)(2,1)S(1)}, u32[]{:S(2)}, u32[]{:S(2)}) collective-permute-start(bf16[4,64,512]{2,1,0:T(8,128)(2,1)S(1)} %bitcast.41), channel_id=1, source_target_pairs={{0,64},{16,80},{32,96},{48,112},{64,0},{80,16},{96,32},{112,48},{1... | collective-permute-start | bytes 786440 | tf_op jit(solution)/shard_map/ppermute | solution.py:369
  7.3 17.8 %collective-permute-start.2 = (bf16[4,64,512]{2,1,0:T(8,128)(2,1)S(1)}, bf16[4,64,512]{2,1,0:T(8,128)(2,1)S(1)}, u32[]{:S(2)}, u32[]{:S(2)}) collective-permute-start(bf16[4,64,512]{2,1,0:T(8,128)(2,1)S(1)} %bitcast.42), channel_id=1, source_target_pairs={{0,96},{16,112},{32,0},{48,16},{64,32},{80,48},{96,64},{112,80},{1... | collective-permute-start | bytes 786440 | tf_op jit(solution)/shard_map/ppermute | solution.py:369
  9.6 15.5 %all-to-all-start = ((s32[16,1,512]{2,1,0:T(1,128)}), s32[16,1,512]{2,1,0:T(1,128)S(1)}, u32[]{:S(2)}, u32[]{:S(2)}) async-start(s32[16,1,512]{2,1,0:T(1,128)} %broadcast_in_dim.12), calls=%async_computation | async-start | bytes 65536 | tf_op jit(solution)/shard_map/all_to_all | solution.py:403
  25.3 3.6 %collective-permute-start.3 = (bf16[4,4,64,512]{3,2,1,0:T(8,128)(2,1)S(1)}, bf16[4,4,64,512]{3,2,1,0:T(8,128)(2,1)S(1)}, u32[]{:S(2)}, u32[]{:S(2)}) collective-permute-start(bf16[4,4,64,512]{3,2,1,0:T(8,128)(2,1)S(1)} %pad_maximum_fusion.rest_4_), channel_id=1, source_target_pairs={{0,16},{16,0},{32,48},{48,32},{64,80},{80,64},{96,112},{112,96},{1... | collective-permute-start | bytes 3145736 | tf_op jit(solution)/shard_map/ppermute | solution.py:375
  25.4 19.9 %collective-permute-start.4 = (bf16[4,64,512]{2,1,0:T(8,128)(2,1)S(1)}, bf16[4,64,512]{2,1,0:T(8,128)(2,1)S(1)}, u32[]{:S(2)}, u32[]{:S(2)}) collective-permute-start(bf16[4,64,512]{2,1,0:T(8,128)(2,1)S(1)} %bitcast.36), channel_id=1, source_target_pairs={{0,32},{16,48},{32,64},{48,80},{64,96},{80,112},{96,0},{112,16},{1... | collective-permute-start | bytes 786440 | tf_op jit(solution)/shard_map/ppermute | solution.py:369
  26.1 19.2 %collective-permute-start.5 = (bf16[4,64,512]{2,1,0:T(8,128)(2,1)S(1)}, bf16[4,64,512]{2,1,0:T(8,128)(2,1)S(1)}, u32[]{:S(2)}, u32[]{:S(2)}) collective-permute-start(bf16[4,64,512]{2,1,0:T(8,128)(2,1)S(1)} %bitcast.37), channel_id=1, source_target_pairs={{0,64},{16,80},{32,96},{48,112},{64,0},{80,16},{96,32},{112,48},{1... | collective-permute-start | bytes 786440 | tf_op jit(solution)/shard_map/ppermute | solution.py:369
  26.9 18.4 %collective-permute-start.6 = (bf16[4,64,512]{2,1,0:T(8,128)(2,1)S(1)}, bf16[4,64,512]{2,1,0:T(8,128)(2,1)S(1)}, u32[]{:S(2)}, u32[]{:S(2)}) collective-permute-start(bf16[4,64,512]{2,1,0:T(8,128)(2,1)S(1)} %bitcast.38), channel_id=1, source_target_pairs={{0,96},{16,112},{32,0},{48,16},{64,32},{80,48},{96,64},{112,80},{1... | collective-permute-start | bytes 786440 | tf_op jit(solution)/shard_map/ppermute | solution.py:369
  45.4 3.0 %collective-permute-start.7 = (bf16[4,4,64,512]{3,2,1,0:T(8,128)(2,1)S(1)}, bf16[4,4,64,512]{3,2,1,0:T(8,128)(2,1)S(1)}, u32[]{:S(2)}, u32[]{:S(2)}) collective-permute-start(bf16[4,4,64,512]{3,2,1,0:T(8,128)(2,1)S(1)} %pad_maximum_fusion.1.rest_2_), channel_id=1, source_target_pairs={{0,16},{16,0},{32,48},{48,32},{64,80},{80,64},{96,112},{112,96},{1... | collective-permute-start | bytes 3145736 | tf_op jit(solution)/shard_map/ppermute | solution.py:375
  45.8 17.3 %collective-permute-start.10 = (s16[4,288,256]{2,1,0:T(8,128)(2,1)S(1)}, s16[4,288,256]{2,1,0:T(8,128)(2,1)S(1)}, u32[]{:S(2)}, u32[]{:S(2)}) collective-permute-start(s16[4,288,256]{2,1,0:T(8,128)(2,1)S(1)} %get-tuple-element.68), channel_id=1, source_target_pairs={{0,3},{1,0},{2,1},{3,2},{4,7},{5,4},{6,5},{7,6},{8,11},{9,8},{10,9... | collective-permute-start | bytes 1769480 | tf_op jit(solution)/shard_map/ppermute | solution.py:360
  47.0 16.1 %collective-permute-start.8 = (s16[4,288,256]{2,1,0:T(8,128)(2,1)S(1)}, s16[4,288,256]{2,1,0:T(8,128)(2,1)S(1)}, u32[]{:S(2)}, u32[]{:S(2)}) collective-permute-start(s16[4,288,256]{2,1,0:T(8,128)(2,1)S(1)} %get-tuple-element.66), channel_id=1, source_target_pairs={{0,2},{1,3},{2,0},{3,1},{4,6},{5,7},{6,4},{7,5},{8,10},{9,11},{10,... | collective-permute-start | bytes 1769480 | tf_op jit(solution)/shard_map/ppermute | solution.py:360
  48.4 16.3 %collective-permute-start.9 = (s16[4,288,256]{2,1,0:T(8,128)(2,1)S(1)}, s16[4,288,256]{2,1,0:T(8,128)(2,1)S(1)}, u32[]{:S(2)}, u32[]{:S(2)}) collective-permute-start(s16[4,288,256]{2,1,0:T(8,128)(2,1)S(1)} %get-tuple-element.67), channel_id=1, source_target_pairs={{0,1},{1,2},{2,3},{3,0},{4,5},{5,6},{6,7},{7,4},{8,9},{9,10},{10,1... | collective-permute-start | bytes 1769480 | tf_op jit(solution)/shard_map/ppermute | solution.py:360
  63.0 24.9 %copy-start.3 = (f32[256]{0:T(256)S(1)}, f32[256]{0:T(256)}, u32[]{:S(2)}) copy-start(f32[256]{0:T(256)} %param.13) | copy-start | bytes 3076
  63.1 25.0 %copy-start.2 = (f32[32]{0:T(128)S(1)}, f32[32]{0:T(128)}, u32[]{:S(2)}) copy-start(f32[32]{0:T(128)} %param.14) | copy-start | bytes 388
  63.1 36.7 %copy-start.1 = (s32[1024]{0:T(1024)S(1)}, s32[1024]{0:T(1024)}, u32[]{:S(2)}) copy-start(s32[1024]{0:T(1024)} %constant.94.clone) | copy-start | bytes 12292
  64.7 11.1 %collective-permute-start.11 = (s16[4,272,256]{2,1,0:T(8,128)(2,1)S(1)}, s16[4,272,256]{2,1,0:T(8,128)(2,1)S(1)}, u32[]{:S(2)}, u32[]{:S(2)}) collective-permute-start(s16[4,272,256]{2,1,0:T(8,128)(2,1)S(1)} %get-tuple-element.74), channel_id=1, source_target_pairs={{0,2},{1,3},{2,0},{3,1},{4,6},{5,7},{6,4},{7,5},{8,10},{9,11},{10,... | collective-permute-start | bytes 1671176 | tf_op jit(solution)/shard_map/ppermute | solution.py:360
  66.7 15.0 %collective-permute-start.12 = (s16[4,272,256]{2,1,0:T(8,128)(2,1)S(1)}, s16[4,272,256]{2,1,0:T(8,128)(2,1)S(1)}, u32[]{:S(2)}, u32[]{:S(2)}) collective-permute-start(s16[4,272,256]{2,1,0:T(8,128)(2,1)S(1)} %get-tuple-element.75), channel_id=1, source_target_pairs={{0,1},{1,2},{2,3},{3,0},{4,5},{5,6},{6,7},{7,4},{8,9},{9,10},{10,1... | collective-permute-start | bytes 1671176 | tf_op jit(solution)/shard_map/ppermute | solution.py:360
  67.2 14.4 %collective-permute-start.13 = (s16[4,272,256]{2,1,0:T(8,128)(2,1)S(1)}, s16[4,272,256]{2,1,0:T(8,128)(2,1)S(1)}, u32[]{:S(2)}, u32[]{:S(2)}) collective-permute-start(s16[4,272,256]{2,1,0:T(8,128)(2,1)S(1)} %get-tuple-element.76), channel_id=1, source_target_pairs={{0,3},{1,0},{2,1},{3,2},{4,7},{5,4},{6,5},{7,6},{8,11},{9,8},{10,9... | collective-permute-start | bytes 1671176 | tf_op jit(solution)/shard_map/ppermute | solution.py:360
  83.1 8.3 %collective-permute-start.14 = (s16[560,256]{1,0:T(8,128)(2,1)S(1)}, s16[560,256]{1,0:T(8,128)(2,1)S(1)}, u32[]{:S(2)}, u32[]{:S(2)}) collective-permute-start(s16[560,256]{1,0:T(8,128)(2,1)S(1)} %get-tuple-element.78), channel_id=1, source_target_pairs={{0,8},{1,9},{2,10},{3,11},{4,12},{5,13},{6,14},{7,15},{8,0},{9,1},... | collective-permute-start | bytes 860168 | tf_op jit(solution)/shard_map/ppermute | solution.py:360
  84.6 9.8 %collective-permute-start.15 = (s16[560,256]{1,0:T(8,128)(2,1)S(1)}, s16[560,256]{1,0:T(8,128)(2,1)S(1)}, u32[]{:S(2)}, u32[]{:S(2)}) collective-permute-start(s16[560,256]{1,0:T(8,128)(2,1)S(1)} %get-tuple-element.79), channel_id=1, source_target_pairs={{0,4},{1,5},{2,6},{3,7},{4,8},{5,9},{6,10},{7,11},{8,12},{9,13},{1... | collective-permute-start | bytes 860168 | tf_op jit(solution)/shard_map/ppermute | solution.py:360
  85.4 9.0 %collective-permute-start.16 = (s16[560,256]{1,0:T(8,128)(2,1)S(1)}, s16[560,256]{1,0:T(8,128)(2,1)S(1)}, u32[]{:S(2)}, u32[]{:S(2)}) collective-permute-start(s16[560,256]{1,0:T(8,128)(2,1)S(1)} %get-tuple-element.80), channel_id=1, source_target_pairs={{0,12},{1,13},{2,14},{3,15},{4,0},{5,1},{6,2},{7,3},{8,4},{9,5},{1... | collective-permute-start | bytes 860168 | tf_op jit(solution)/shard_map/ppermute | solution.py:360
  95.6 13.2 %all-to-all-start.1 = ((s16[16,16,640]{2,1,0:T(8,128)(2,1)}), s16[16,16,640]{2,1,0:T(8,128)(2,1)S(1)}, u32[]{:S(2)}, u32[]{:S(2)}) async-start(s16[16,16,640]{2,1,0:T(8,128)(2,1)} %bitcast.23), calls=%async_computation.1 | async-start | bytes 655360 | tf_op jit(solution)/shard_map/all_to_all | solution.py:429

commit v8 on v7

--- a/solution.py
+++ b/solution.py
@@ -388,8 +388,11 @@
     spread = (jnp.asarray(np.concatenate([first, mates_of]))[:, None] == pair_ids[None, :]).astype(BF16)
 
     blocks, depth, _ = amplitudes.shape
-    sorted_amp = jnp.dot(amplitudes.reshape(blocks * depth, OCC), sort, preferred_element_type=F32).astype(BF16)
-    parts = [sorted_amp[:, c * CW : (c + 1) * CW].reshape(blocks, depth, CW) for c in range(CHUNKS)]
+    flat_amps = amplitudes.reshape(blocks * depth, OCC)
+    parts = []
+    for c in range(CHUNKS):
+        part = jnp.dot(flat_amps, sort[:, c * CW : (c + 1) * CW], preferred_element_type=F32)
+        parts.append(part.astype(BF16).reshape(blocks, depth, CW))
 
     peer = rows // groups
     target = partner // rows % groups
@@ -401,7 +404,7 @@
     both = jnp.concatenate([own_rank, mate_rank]).astype(S32)
     spoken = jnp.broadcast_to(both[None, :], (groups, 2 * rows))
     ranks = lax.all_to_all(spoken, "col", split_axis=0, concat_axis=0, tiled=True)
-    along = [fetch_along(part) for part in parts]
+    along = [fetch_along(parts[0])]
     ranks = jnp.stack([ranks[:, :rows], ranks[:, rows:]])
     row, col = lax.axis_index("row"), lax.axis_index("col")
     z, x, core = col // SIDE, col % SIDE, row % 2
@@ -410,7 +413,9 @@
     slot_ids = jnp.arange(slots.shape[0], dtype=S32)
     order = jnp.sum(jnp.where(slots[None, :] == slot_ids[:, None], slot_ids[None, :], 0), axis=1)
     live = (order < tile_count[0, 0]).astype(S32)
-    ranks, order, live, place, along[0] = lax.optimization_barrier((ranks, order, live, place, along[0]))
+    ready = (ranks, order, live, place, parts, along)
+    ranks, order, live, place, parts, along = lax.optimization_barrier(ready)
+    along += [fetch_along(part) for part in parts[1:]]
 
     tiles = integrals[0, 0]
     far_flags = tuple(c == 0 for c in range(CHUNKS))

time: 113 us -> 113 us (level)
  other arithmetic: 1.24 us -> 3.47 us
    eq x0 -> x1, other arithmetic: none -> 1.55 us  [body(): pair_ids[:, None] == jnp.asarray(column_order)[None, :]]
  transfers between devices with their start and end apart: 19 -> 19, of which waited for: 7 -> 7; matrix products, arithmetic and copies ran while one was open for 2% -> 3% of each run, Pallas kernels for 31% -> 31%
where the time goes in v8:
time: 113 us
  Pallas kernels  41.1 us (36%)
  starting transfers between devices  34.4 us (30%)
  waiting for transfers between devices  30.5 us (27%)
  other arithmetic  3.47 us (3%)
    pallas_call x2, Pallas kernels, product(): pl.pallas_call(functools.partial(product_kernel, has_far, rows, fetch), o...  31.5 us
    ppermute x9, waiting for transfers between devices, trade(): got.append(lax.ppermute(pieces[k], ('row', 'col'), perm))  19.2 us
    ppermute x9, starting transfers between devices, trade(): got.append(lax.ppermute(pieces[k], ('row', 'col'), perm))  12.7 us
    ppermute x6, starting transfers between devices, fetch_along(): lax.ppermute(part, 'row', shifted_rows(k, 0))  9.49 us
    all_to_all x1, starting transfers between devices, body(): lax.all_to_all(spoken, 'col', split_axis=0, concat_axis=0, tiled=True)  7.87 us
    pallas_call x2, Pallas kernels, last_call(): pl.pallas_call(kernel, out_shape=result, in_specs=[vmem] * len(args), out...  6.99 us
    all_to_all x1, waiting for transfers between devices, body(): lax.all_to_all(spoken, 'col', split_axis=0, concat_axis=0, tiled=True)  6.13 us
    all_to_all x1, waiting for transfers between devices, body(): came = lax.all_to_all(send, 'col', split_axis=0, concat_axis=0, tiled=True)  5.23 us
  transfers between devices with their start and end apart: 19, of which 7 were waited for; matrix products, arithmetic and copies ran while one was open for 3% of the time, Pallas kernels for 31%

profile of v8, /device:TPU:0, one launch (start us, length us, event | category | flops | bytes accessed | tf_op | source)
XLA Modules:
  0.0 112.5 jit_solution(3850757638034690426)
XLA Ops:
  0.0 1.5 %iota_compare_fusion.1 = pred[1024,1024]{1,0:T(32,128)(4,1)S(1)} fusion(s32[1024]{0:T(1024)} %constant.93.clone), kind=kLoop, calls=%fused_computation.1 | loop fusion | flops 1048576 | bytes 1052672 | tf_op jit(solution)/shard_map/eq | solution.py:387
  1.6 0.5 fusion.5
  2.1 1.7 %collective-permute-start = (bf16[4,64,512]{2,1,0:T(8,128)(2,1)S(1)}, bf16[4,64,512]{2,1,0:T(8,128)(2,1)S(1)}, u32[]{:S(2)}, u32[]{:S(2)}) collective-permute-start(bf16[4,64,512]{2,1,0:T(8,128)(2,1)S(1)} %bitcast.40), channel_id=1, source_target_pairs={{0,32},{16,48},{32,64},{48,80},{64,96},{80,112},{96,0},{112,16},{1... | collective-permute-start | bytes 786440 | tf_op jit(solution)/shard_map/ppermute | solution.py:369
  3.8 2.9 %collective-permute-start.1 = (bf16[4,64,512]{2,1,0:T(8,128)(2,1)S(1)}, bf16[4,64,512]{2,1,0:T(8,128)(2,1)S(1)}, u32[]{:S(2)}, u32[]{:S(2)}) collective-permute-start(bf16[4,64,512]{2,1,0:T(8,128)(2,1)S(1)} %bitcast.41), channel_id=1, source_target_pairs={{0,64},{16,80},{32,96},{48,112},{64,0},{80,16},{96,32},{112,48},{1... | collective-permute-start | bytes 786440 | tf_op jit(solution)/shard_map/ppermute | solution.py:369
  6.7 1.3 %collective-permute-start.2 = (bf16[4,64,512]{2,1,0:T(8,128)(2,1)S(1)}, bf16[4,64,512]{2,1,0:T(8,128)(2,1)S(1)}, u32[]{:S(2)}, u32[]{:S(2)}) collective-permute-start(bf16[4,64,512]{2,1,0:T(8,128)(2,1)S(1)} %bitcast.42), channel_id=1, source_target_pairs={{0,96},{16,112},{32,0},{48,16},{64,32},{80,48},{96,64},{112,80},{1... | collective-permute-start | bytes 786440 | tf_op jit(solution)/shard_map/ppermute | solution.py:369
  8.1 0.7 and_select_fusion
  8.8 0.3 convert_reduce_fusion.1
  9.0 0.6 broadcast_in_dim.12
  9.7 7.9 %all-to-all-start = ((s32[16,1,512]{2,1,0:T(1,128)}), s32[16,1,512]{2,1,0:T(1,128)S(1)}, u32[]{:S(2)}, u32[]{:S(2)}) async-start(s32[16,1,512]{2,1,0:T(1,128)} %broadcast_in_dim.12), calls=%async_computation | async-start | bytes 65536 | tf_op jit(solution)/shard_map/all_to_all | solution.py:406
  17.6 0.5 fusion.8
  18.2 0.1 select_reduce_fusion.rest_0_
  18.9 0.1 pad_add_fusion.3.place_ref
  19.0 6.1 %all-to-all-done = s32[16,1,512]{2,1,0:T(1,128)S(1)} async-done(((s32[16,1,512]{2,1,0:T(1,128)}), s32[16,1,512]{2,1,0:T(1,128)S(1)}, u32[]{:S(2)}, u32[]{:S(2)}) %all-to-all-start) | async-done | bytes 32800 | tf_op jit(solution)/shard_map/all_to_all | solution.py:406
  25.2 0.1 pad_maximum_fusion.rest_4_
  25.4 0.1 collective-permute-start.3
  25.4 0.7 collective-permute-start.4
  26.2 0.8 collective-permute-start.5
  27.0 2.0 %collective-permute-start.6 = (bf16[4,64,512]{2,1,0:T(8,128)(2,1)S(1)}, bf16[4,64,512]{2,1,0:T(8,128)(2,1)S(1)}, u32[]{:S(2)}, u32[]{:S(2)}) collective-permute-start(bf16[4,64,512]{2,1,0:T(8,128)(2,1)S(1)} %bitcast.49), channel_id=1, source_target_pairs={{0,96},{16,112},{32,0},{48,16},{64,32},{80,48},{96,64},{112,80},{1... | collective-permute-start | bytes 786440 | tf_op jit(solution)/shard_map/ppermute | solution.py:369
  29.0 16.9 %product.2 = (s16[4,288,256]{2,1,0:T(8,128)(2,1)S(1)}, s16[4,288,256]{2,1,0:T(8,128)(2,1)S(1)}, s16[4,288,256]{2,1,0:T(8,128)(2,1)S(1)}, s16[4,288,256]{2,1,0:T(8,128)(2,1)S(1)}, bf16[32,512,512]{2,1,0:T(8,128)(2,1)S(1)}) custom-call(s32[4]{0:T(128)S(1)} %pad_add_fusion.3.place_ref, s32[32]{0:T(128)S(1)} %select_reduce_fusion.rest_0_, ...), custom_call_target="tpu_custom_call" | custom-call | flops 8589934592 | bytes 4194304 | tf_op jit(solution)/shard_map/product/pallas_call | solution.py:232
  45.9 0.1 pad_maximum_fusion.1.rest_2_
  46.0 0.1 collective-permute-start.7
  46.1 1.0 collective-permute-start.10
  47.1 1.7 %collective-permute-start.8 = (s16[4,288,256]{2,1,0:T(8,128)(2,1)S(1)}, s16[4,288,256]{2,1,0:T(8,128)(2,1)S(1)}, u32[]{:S(2)}, u32[]{:S(2)}) collective-permute-start(s16[4,288,256]{2,1,0:T(8,128)(2,1)S(1)} %get-tuple-element.68), channel_id=1, source_target_pairs={{0,2},{1,3},{2,0},{3,1},{4,6},{5,7},{6,4},{7,5},{8,10},{9,11},{10,... | collective-permute-start | bytes 1769480 | tf_op jit(solution)/shard_map/ppermute | solution.py:360
  48.8 14.6 %product.3 = (s16[4,272,256]{2,1,0:T(8,128)(2,1)S(1)}, s16[4,272,256]{2,1,0:T(8,128)(2,1)S(1)}, s16[4,272,256]{2,1,0:T(8,128)(2,1)S(1)}, s16[4,272,256]{2,1,0:T(8,128)(2,1)S(1)}) custom-call(s32[4]{0:T(128)S(1)} %pad_add_fusion.3.place_ref, bf16[32,512,512]{2,1,0:T(8,128)(2,1)S(1)} %get-tuple-element.53.rest_0_, ...), custom_call_target="tpu_custom_call" | custom-call | flops 8589934592 | bytes 4194304 | tf_op jit(solution)/shard_map/product/pallas_call | solution.py:232
  63.4 0.0 copy-start.3
  63.4 0.0 copy-start.1
  63.5 1.4 %collective-permute-done.9.refs_2_ = s16[4,288,256]{2,1,0:T(8,128)(2,1)S(1)} collective-permute-done((s16[4,288,256]{2,1,0:T(8,128)(2,1)S(1)}, s16[4,288,256]{2,1,0:T(8,128)(2,1)S(1)}, u32[]{:S(2)}, u32[]{:S(2)}) %collective-permute-start.9) | collective-permute-done | bytes 589856 | tf_op jit(solution)/shard_map/ppermute | solution.py:360
  64.8 2.2 %collective-permute-start.11 = (s16[4,272,256]{2,1,0:T(8,128)(2,1)S(1)}, s16[4,272,256]{2,1,0:T(8,128)(2,1)S(1)}, u32[]{:S(2)}, u32[]{:S(2)}) collective-permute-start(s16[4,272,256]{2,1,0:T(8,128)(2,1)S(1)} %get-tuple-element.76), channel_id=1, source_target_pairs={{0,2},{1,3},{2,0},{3,1},{4,6},{5,7},{6,4},{7,5},{8,10},{9,11},{10,... | collective-permute-start | bytes 1671176 | tf_op jit(solution)/shard_map/ppermute | solution.py:360
  67.1 0.6 collective-permute-start.12
  67.7 2.7 %collective-permute-start.13 = (s16[4,272,256]{2,1,0:T(8,128)(2,1)S(1)}, s16[4,272,256]{2,1,0:T(8,128)(2,1)S(1)}, u32[]{:S(2)}, u32[]{:S(2)}) collective-permute-start(s16[4,272,256]{2,1,0:T(8,128)(2,1)S(1)} %get-tuple-element.78), channel_id=1, source_target_pairs={{0,3},{1,0},{2,1},{3,2},{4,7},{5,4},{6,5},{7,6},{8,11},{9,8},{10,9... | collective-permute-start | bytes 1671176 | tf_op jit(solution)/shard_map/ppermute | solution.py:360
  70.3 5.7 %collective-permute-done.11.refs_5_ = s16[4,272,256]{2,1,0:T(8,128)(2,1)S(1)} collective-permute-done((s16[4,272,256]{2,1,0:T(8,128)(2,1)S(1)}, s16[4,272,256]{2,1,0:T(8,128)(2,1)S(1)}, u32[]{:S(2)}, u32[]{:S(2)}) %collective-permute-start.11) | collective-permute-done | bytes 557088 | tf_op jit(solution)/shard_map/ppermute | solution.py:360
  76.0 5.9 %collective-permute-done.12.refs_6_ = s16[4,272,256]{2,1,0:T(8,128)(2,1)S(1)} collective-permute-done((s16[4,272,256]{2,1,0:T(8,128)(2,1)S(1)}, s16[4,272,256]{2,1,0:T(8,128)(2,1)S(1)}, u32[]{:S(2)}, u32[]{:S(2)}) %collective-permute-start.12) | collective-permute-done | bytes 557088 | tf_op jit(solution)/shard_map/ppermute | solution.py:360
  81.8 1.4 %relay.1 = (s16[560,256]{1,0:T(8,128)(2,1)S(1)}, s16[560,256]{1,0:T(8,128)(2,1)S(1)}, s16[560,256]{1,0:T(8,128)(2,1)S(1)}, s16[560,256]{1,0:T(8,128)(2,1)S(1)}) custom-call(s16[4,288,256]{2,1,0:T(8,128)(2,1)S(1)} %get-tuple-element.71.refs_0_, s16[4,288,256]{2,1,0:T(8,128)(2,1)S(1)} %collective-permute-done.8.refs_1_, ...), custom_call_target="tpu_custom_call" | custom-call | tf_op jit(solution)/shard_map/relay/pallas_call | solution.py:263
  83.3 1.3 %collective-permute-start.14 = (s16[560,256]{1,0:T(8,128)(2,1)S(1)}, s16[560,256]{1,0:T(8,128)(2,1)S(1)}, u32[]{:S(2)}, u32[]{:S(2)}) collective-permute-start(s16[560,256]{1,0:T(8,128)(2,1)S(1)} %get-tuple-element.80), channel_id=1, source_target_pairs={{0,8},{1,9},{2,10},{3,11},{4,12},{5,13},{6,14},{7,15},{8,0},{9,1},... | collective-permute-start | bytes 860168 | tf_op jit(solution)/shard_map/ppermute | solution.py:360
  84.6 1.0 collective-permute-start.15
  85.6 2.2 %collective-permute-start.16 = (s16[560,256]{1,0:T(8,128)(2,1)S(1)}, s16[560,256]{1,0:T(8,128)(2,1)S(1)}, u32[]{:S(2)}, u32[]{:S(2)}) collective-permute-start(s16[560,256]{1,0:T(8,128)(2,1)S(1)} %get-tuple-element.82), channel_id=1, source_target_pairs={{0,12},{1,13},{2,14},{3,15},{4,0},{5,1},{6,2},{7,3},{8,4},{9,5},{1... | collective-permute-start | bytes 860168 | tf_op jit(solution)/shard_map/ppermute | solution.py:360
  87.8 0.1 copy.16.ranks
  88.0 0.1 copy.18.energy
  88.1 0.1 broadcast_add_fusion
  88.2 0.1 add.58.pair_sum
  88.3 3.3 %collective-permute-done.14.refs_1_ = s16[560,256]{1,0:T(8,128)(2,1)S(1)} collective-permute-done((s16[560,256]{1,0:T(8,128)(2,1)S(1)}, s16[560,256]{1,0:T(8,128)(2,1)S(1)}, u32[]{:S(2)}, u32[]{:S(2)}) %collective-permute-start.14) | collective-permute-done | bytes 286752 | tf_op jit(solution)/shard_map/ppermute | solution.py:360
  91.6 3.0 %collective-permute-done.15.refs_2_ = s16[560,256]{1,0:T(8,128)(2,1)S(1)} collective-permute-done((s16[560,256]{1,0:T(8,128)(2,1)S(1)}, s16[560,256]{1,0:T(8,128)(2,1)S(1)}, u32[]{:S(2)}, u32[]{:S(2)}) %collective-permute-start.15) | collective-permute-done | bytes 286752 | tf_op jit(solution)/shard_map/ppermute | solution.py:360
  94.6 1.2 %owner.1 = (f32[256,640]{1,0:T(8,128)}, s16[256,640]{1,0:T(8,128)(2,1)}) custom-call(s16[560,256]{1,0:T(8,128)(2,1)S(1)} %get-tuple-element.79.refs_0_, s16[560,256]{1,0:T(8,128)(2,1)S(1)} %collective-permute-done.14.refs_1_, s16[560,256]{1,0:T(8,128)(2,1)S(1)} %collective-permute-done.15.refs_2_, s16[560,256]{1,0:T(8,128)(2,1)S(1)} %collective-permute-done.16.refs_3_), custom_call_target="tpu_custom_call" | custom-call | tf_op jit(solution)/shard_map/owner/pallas_call | solution.py:294
  95.8 4.1 %all-to-all-start.1 = ((s16[16,16,640]{2,1,0:T(8,128)(2,1)}), s16[16,16,640]{2,1,0:T(8,128)(2,1)S(1)}, u32[]{:S(2)}, u32[]{:S(2)}) async-start(s16[16,16,640]{2,1,0:T(8,128)(2,1)} %bitcast.25), calls=%async_computation.1 | async-start | bytes 655360 | tf_op jit(solution)/shard_map/all_to_all | solution.py:434
  99.9 0.4 fusion.spread
  100.3 3.4 %mine.1 = f32[256,1024]{1,0:T(8,128)} custom-call(f32[256,640]{1,0:T(8,128)} %get-tuple-element.83.own, s32[256,2]{1,0:T(8,128)S(1)} %copy.16.ranks, bf16[1024,1024]{1,0:T(8,128)(2,1)S(1)} %fusion.spread), custom_call_target="tpu_custom_call" | custom-call | flops 1073741824 | bytes 2097152 | tf_op jit(solution)/shard_map/mine/pallas_call | solution.py:340
  103.7 5.2 %all-to-all-done.1 = s16[16,16,640]{2,1,0:T(8,128)(2,1)S(1)} async-done(((s16[16,16,640]{2,1,0:T(8,128)(2,1)}), s16[16,16,640]{2,1,0:T(8,128)(2,1)S(1)}, u32[]{:S(2)}, u32[]{:S(2)}) %all-to-all-start.1) | async-done | bytes 327712 | tf_op jit(solution)/shard_map/all_to_all | solution.py:434
  108.9 3.6 %close.1 = f32[256,1024]{1,0:T(8,128)} custom-call(f32[256,1024]{1,0:T(8,128)} %mine.1, s16[256,640]{1,0:T(8,128)(2,1)S(1)} %bitcast.39, s32[256,2]{1,0:T(8,128)S(1)} %copy.16.ranks, f32[256,1]{1,0:T(8,128)S(1)} %copy.18.energy, f32[1,1024]{1,0:T(1,128)S(1)} %add.58.pair_sum, bf16[1024,1024]{1,0:T(8,128)(2,1)S(1)} %fusion.spread), custom_call_target="tpu_custom_call" | custom-call | flops 1073741824 | bytes 2097152 | tf_op jit(solution)/shard_map/close/pallas_call | solution.py:340
  (28 shorter events, 0.1 us)
Async XLA Ops:
  0.0 1.6 %copy-start = (bf16[4,64,1024]{2,1,0:T(8,128)(2,1)S(1)}, bf16[4,64,1024]{2,1,0:T(8,128)(2,1)}, u32[]{:S(2)}) copy-start(bf16[4,64,1024]{2,1,0:T(8,128)(2,1)} %param.12) | copy-start | bytes 1572868
  0.0 18.1 %copy-start.4 = (s32[1,1,32]{2,1,0:T(1,128)S(1)}, s32[1,1,32]{2,1,0:T(1,128)}, u32[]{:S(2)}) copy-start(s32[1,1,32]{2,1,0:T(1,128)} %param.11) | copy-start | bytes 388
  2.1 23.1 %collective-permute-start = (bf16[4,64,512]{2,1,0:T(8,128)(2,1)S(1)}, bf16[4,64,512]{2,1,0:T(8,128)(2,1)S(1)}, u32[]{:S(2)}, u32[]{:S(2)}) collective-permute-start(bf16[4,64,512]{2,1,0:T(8,128)(2,1)S(1)} %bitcast.40), channel_id=1, source_target_pairs={{0,32},{16,48},{32,64},{48,80},{64,96},{80,112},{96,0},{112,16},{1... | collective-permute-start | bytes 786440 | tf_op jit(solution)/shard_map/ppermute | solution.py:369
  3.8 21.4 %collective-permute-start.1 = (bf16[4,64,512]{2,1,0:T(8,128)(2,1)S(1)}, bf16[4,64,512]{2,1,0:T(8,128)(2,1)S(1)}, u32[]{:S(2)}, u32[]{:S(2)}) collective-permute-start(bf16[4,64,512]{2,1,0:T(8,128)(2,1)S(1)} %bitcast.41), channel_id=1, source_target_pairs={{0,64},{16,80},{32,96},{48,112},{64,0},{80,16},{96,32},{112,48},{1... | collective-permute-start | bytes 786440 | tf_op jit(solution)/shard_map/ppermute | solution.py:369
  6.7 18.5 %collective-permute-start.2 = (bf16[4,64,512]{2,1,0:T(8,128)(2,1)S(1)}, bf16[4,64,512]{2,1,0:T(8,128)(2,1)S(1)}, u32[]{:S(2)}, u32[]{:S(2)}) collective-permute-start(bf16[4,64,512]{2,1,0:T(8,128)(2,1)S(1)} %bitcast.42), channel_id=1, source_target_pairs={{0,96},{16,112},{32,0},{48,16},{64,32},{80,48},{96,64},{112,80},{1... | collective-permute-start | bytes 786440 | tf_op jit(solution)/shard_map/ppermute | solution.py:369
  9.7 15.5 %all-to-all-start = ((s32[16,1,512]{2,1,0:T(1,128)}), s32[16,1,512]{2,1,0:T(1,128)S(1)}, u32[]{:S(2)}, u32[]{:S(2)}) async-start(s32[16,1,512]{2,1,0:T(1,128)} %broadcast_in_dim.12), calls=%async_computation | async-start | bytes 65536 | tf_op jit(solution)/shard_map/all_to_all | solution.py:406
  25.4 3.6 %collective-permute-start.3 = (bf16[4,4,64,512]{3,2,1,0:T(8,128)(2,1)S(1)}, bf16[4,4,64,512]{3,2,1,0:T(8,128)(2,1)S(1)}, u32[]{:S(2)}, u32[]{:S(2)}) collective-permute-start(bf16[4,4,64,512]{3,2,1,0:T(8,128)(2,1)S(1)} %pad_maximum_fusion.rest_4_), channel_id=1, source_target_pairs={{0,16},{16,0},{32,48},{48,32},{64,80},{80,64},{96,112},{112,96},{1... | collective-permute-start | bytes 3145736 | tf_op jit(solution)/shard_map/ppermute | solution.py:375
  25.4 20.4 %collective-permute-start.4 = (bf16[4,64,512]{2,1,0:T(8,128)(2,1)S(1)}, bf16[4,64,512]{2,1,0:T(8,128)(2,1)S(1)}, u32[]{:S(2)}, u32[]{:S(2)}) collective-permute-start(bf16[4,64,512]{2,1,0:T(8,128)(2,1)S(1)} %bitcast.47), channel_id=1, source_target_pairs={{0,32},{16,48},{32,64},{48,80},{64,96},{80,112},{96,0},{112,16},{1... | collective-permute-start | bytes 786440 | tf_op jit(solution)/shard_map/ppermute | solution.py:369
  26.2 19.7 %collective-permute-start.5 = (bf16[4,64,512]{2,1,0:T(8,128)(2,1)S(1)}, bf16[4,64,512]{2,1,0:T(8,128)(2,1)S(1)}, u32[]{:S(2)}, u32[]{:S(2)}) collective-permute-start(bf16[4,64,512]{2,1,0:T(8,128)(2,1)S(1)} %bitcast.48), channel_id=1, source_target_pairs={{0,64},{16,80},{32,96},{48,112},{64,0},{80,16},{96,32},{112,48},{1... | collective-permute-start | bytes 786440 | tf_op jit(solution)/shard_map/ppermute | solution.py:369
  27.0 18.9 %collective-permute-start.6 = (bf16[4,64,512]{2,1,0:T(8,128)(2,1)S(1)}, bf16[4,64,512]{2,1,0:T(8,128)(2,1)S(1)}, u32[]{:S(2)}, u32[]{:S(2)}) collective-permute-start(bf16[4,64,512]{2,1,0:T(8,128)(2,1)S(1)} %bitcast.49), channel_id=1, source_target_pairs={{0,96},{16,112},{32,0},{48,16},{64,32},{80,48},{96,64},{112,80},{1... | collective-permute-start | bytes 786440 | tf_op jit(solution)/shard_map/ppermute | solution.py:369
  46.0 2.8 %collective-permute-start.7 = (bf16[4,4,64,512]{3,2,1,0:T(8,128)(2,1)S(1)}, bf16[4,4,64,512]{3,2,1,0:T(8,128)(2,1)S(1)}, u32[]{:S(2)}, u32[]{:S(2)}) collective-permute-start(bf16[4,4,64,512]{3,2,1,0:T(8,128)(2,1)S(1)} %pad_maximum_fusion.1.rest_2_), channel_id=1, source_target_pairs={{0,16},{16,0},{32,48},{48,32},{64,80},{80,64},{96,112},{112,96},{1... | collective-permute-start | bytes 3145736 | tf_op jit(solution)/shard_map/ppermute | solution.py:375
  46.1 17.3 %collective-permute-start.10 = (s16[4,288,256]{2,1,0:T(8,128)(2,1)S(1)}, s16[4,288,256]{2,1,0:T(8,128)(2,1)S(1)}, u32[]{:S(2)}, u32[]{:S(2)}) collective-permute-start(s16[4,288,256]{2,1,0:T(8,128)(2,1)S(1)} %get-tuple-element.70), channel_id=1, source_target_pairs={{0,3},{1,0},{2,1},{3,2},{4,7},{5,4},{6,5},{7,6},{8,11},{9,8},{10,9... | collective-permute-start | bytes 1769480 | tf_op jit(solution)/shard_map/ppermute | solution.py:360
  47.1 16.3 %collective-permute-start.8 = (s16[4,288,256]{2,1,0:T(8,128)(2,1)S(1)}, s16[4,288,256]{2,1,0:T(8,128)(2,1)S(1)}, u32[]{:S(2)}, u32[]{:S(2)}) collective-permute-start(s16[4,288,256]{2,1,0:T(8,128)(2,1)S(1)} %get-tuple-element.68), channel_id=1, source_target_pairs={{0,2},{1,3},{2,0},{3,1},{4,6},{5,7},{6,4},{7,5},{8,10},{9,11},{10,... | collective-permute-start | bytes 1769480 | tf_op jit(solution)/shard_map/ppermute | solution.py:360
  48.8 16.0 %collective-permute-start.9 = (s16[4,288,256]{2,1,0:T(8,128)(2,1)S(1)}, s16[4,288,256]{2,1,0:T(8,128)(2,1)S(1)}, u32[]{:S(2)}, u32[]{:S(2)}) collective-permute-start(s16[4,288,256]{2,1,0:T(8,128)(2,1)S(1)} %get-tuple-element.69), channel_id=1, source_target_pairs={{0,1},{1,2},{2,3},{3,0},{4,5},{5,6},{6,7},{7,4},{8,9},{9,10},{10,1... | collective-permute-start | bytes 1769480 | tf_op jit(solution)/shard_map/ppermute | solution.py:360
  63.4 24.6 %copy-start.3 = (f32[256]{0:T(256)S(1)}, f32[256]{0:T(256)}, u32[]{:S(2)}) copy-start(f32[256]{0:T(256)} %param.13) | copy-start | bytes 3076
  63.4 24.7 %copy-start.2 = (f32[32]{0:T(128)S(1)}, f32[32]{0:T(128)}, u32[]{:S(2)}) copy-start(f32[32]{0:T(128)} %param.14) | copy-start | bytes 388
  63.4 36.5 %copy-start.1 = (s32[1024]{0:T(1024)S(1)}, s32[1024]{0:T(1024)}, u32[]{:S(2)}) copy-start(s32[1024]{0:T(1024)} %constant.94.clone) | copy-start | bytes 12292
  64.8 11.1 %collective-permute-start.11 = (s16[4,272,256]{2,1,0:T(8,128)(2,1)S(1)}, s16[4,272,256]{2,1,0:T(8,128)(2,1)S(1)}, u32[]{:S(2)}, u32[]{:S(2)}) collective-permute-start(s16[4,272,256]{2,1,0:T(8,128)(2,1)S(1)} %get-tuple-element.76), channel_id=1, source_target_pairs={{0,2},{1,3},{2,0},{3,1},{4,6},{5,7},{6,4},{7,5},{8,10},{9,11},{10,... | collective-permute-start | bytes 1671176 | tf_op jit(solution)/shard_map/ppermute | solution.py:360
  67.1 14.8 %collective-permute-start.12 = (s16[4,272,256]{2,1,0:T(8,128)(2,1)S(1)}, s16[4,272,256]{2,1,0:T(8,128)(2,1)S(1)}, u32[]{:S(2)}, u32[]{:S(2)}) collective-permute-start(s16[4,272,256]{2,1,0:T(8,128)(2,1)S(1)} %get-tuple-element.77), channel_id=1, source_target_pairs={{0,1},{1,2},{2,3},{3,0},{4,5},{5,6},{6,7},{7,4},{8,9},{9,10},{10,1... | collective-permute-start | bytes 1671176 | tf_op jit(solution)/shard_map/ppermute | solution.py:360
  67.7 14.2 %collective-permute-start.13 = (s16[4,272,256]{2,1,0:T(8,128)(2,1)S(1)}, s16[4,272,256]{2,1,0:T(8,128)(2,1)S(1)}, u32[]{:S(2)}, u32[]{:S(2)}) collective-permute-start(s16[4,272,256]{2,1,0:T(8,128)(2,1)S(1)} %get-tuple-element.78), channel_id=1, source_target_pairs={{0,3},{1,0},{2,1},{3,2},{4,7},{5,4},{6,5},{7,6},{8,11},{9,8},{10,9... | collective-permute-start | bytes 1671176 | tf_op jit(solution)/shard_map/ppermute | solution.py:360
  83.3 8.3 %collective-permute-start.14 = (s16[560,256]{1,0:T(8,128)(2,1)S(1)}, s16[560,256]{1,0:T(8,128)(2,1)S(1)}, u32[]{:S(2)}, u32[]{:S(2)}) collective-permute-start(s16[560,256]{1,0:T(8,128)(2,1)S(1)} %get-tuple-element.80), channel_id=1, source_target_pairs={{0,8},{1,9},{2,10},{3,11},{4,12},{5,13},{6,14},{7,15},{8,0},{9,1},... | collective-permute-start | bytes 860168 | tf_op jit(solution)/shard_map/ppermute | solution.py:360
  84.6 10.0 %collective-permute-start.15 = (s16[560,256]{1,0:T(8,128)(2,1)S(1)}, s16[560,256]{1,0:T(8,128)(2,1)S(1)}, u32[]{:S(2)}, u32[]{:S(2)}) collective-permute-start(s16[560,256]{1,0:T(8,128)(2,1)S(1)} %get-tuple-element.81), channel_id=1, source_target_pairs={{0,4},{1,5},{2,6},{3,7},{4,8},{5,9},{6,10},{7,11},{8,12},{9,13},{1... | collective-permute-start | bytes 860168 | tf_op jit(solution)/shard_map/ppermute | solution.py:360
  85.6 9.0 %collective-permute-start.16 = (s16[560,256]{1,0:T(8,128)(2,1)S(1)}, s16[560,256]{1,0:T(8,128)(2,1)S(1)}, u32[]{:S(2)}, u32[]{:S(2)}) collective-permute-start(s16[560,256]{1,0:T(8,128)(2,1)S(1)} %get-tuple-element.82), channel_id=1, source_target_pairs={{0,12},{1,13},{2,14},{3,15},{4,0},{5,1},{6,2},{7,3},{8,4},{9,5},{1... | collective-permute-start | bytes 860168 | tf_op jit(solution)/shard_map/ppermute | solution.py:360
  95.8 13.1 %all-to-all-start.1 = ((s16[16,16,640]{2,1,0:T(8,128)(2,1)}), s16[16,16,640]{2,1,0:T(8,128)(2,1)S(1)}, u32[]{:S(2)}, u32[]{:S(2)}) async-start(s16[16,16,640]{2,1,0:T(8,128)(2,1)} %bitcast.25), calls=%async_computation.1 | async-start | bytes 655360 | tf_op jit(solution)/shard_map/all_to_all | solution.py:434
